TPU v7x, 256 devices: a whole 4x4x8 slice. The times are simulated.
256 devices in a mesh: zg: 4 (over x), gy: 64 (over y, z, core).
Axes of the slice: x: 4, y: 4, z: 8, core: 2. Of those that a mesh axis runs over, the one named last changes fastest.
Arguments:
- initial_heat_state: float32 [256, 256, 128], P('gy', 'zg'), may hold values from -3 to 3
- thermal_conductance_grid: float32 [256, 256, 128], P('gy', 'zg'), may hold values from 1 to 30
Outputs:
- advanced: float32 [256, 256, 128], P('gy', 'zg')
All inputs are finite; a program needn't handle non-finite values.
Results may differ from a plain program's by a relative error of at most 0.004.
Values sent between devices are 32-bit elements; how exact they have to be, the bound alone decides.
No kernel may reach another device: no remote copies, remote signals or barrier semaphores. Data moves between devices by JAX's collectives and lax.ppermute only.
A program may use at most 64 MiB of HBM per device.

v0:
```python
import jax
import jax.numpy as jnp
from jax import lax
from jax.sharding import PartitionSpec as P

mesh_courant_number = 300.0


def with_halo(cells, sides, width):
    for axis, dim in sides:
        count = lax.axis_size(axis)
        ends = count - 1
        head = lax.slice_in_dim(cells, 0, width, axis=dim)
        tail = lax.slice_in_dim(cells, cells.shape[dim] - width, cells.shape[dim], axis=dim)
        cells = jnp.concatenate(
            [
                lax.ppermute(tail, axis, [(i, (i + 1) % count) for i in range(ends)]),
                cells,
                lax.ppermute(head, axis, [((i + 1) % count, i) for i in range(ends)]),
            ],
            axis=dim,
        )
    return cells


def from_behind(x, axis, by):
    count = lax.axis_size(axis)
    pairs = [(i, i + by) for i in range(count) if 0 <= i + by < count]
    return lax.ppermute(x, axis, pairs)


def harmonic(left_side, right_side):
    return 2.0 * left_side * right_side / (left_side + right_side)


def moved(values, stride, line_axis, filler):
    length = values.shape[line_axis]
    padded_shape = list(values.shape)
    padded_shape[line_axis] = abs(stride)
    padding = jnp.full(padded_shape, filler, values.dtype)
    if stride > 0:
        remain = lax.slice_in_dim(values, 0, length - stride, axis=line_axis)
        return jnp.concatenate([padding, remain], line_axis)
    remain = lax.slice_in_dim(values, -stride, length, axis=line_axis)
    return jnp.concatenate([remain, padding], line_axis)


def cyclic_solve(below_band, middle, above_band, source, line_axis):
    length = source.shape[line_axis]
    stride = 1
    while stride < length:
        low_lower = moved(below_band, stride, line_axis, 0.0)
        low_middle = moved(middle, stride, line_axis, 1.0)
        low_upper = moved(above_band, stride, line_axis, 0.0)
        low_source = moved(source, stride, line_axis, 0.0)
        high_lower = moved(below_band, -stride, line_axis, 0.0)
        high_middle = moved(middle, -stride, line_axis, 1.0)
        high_upper = moved(above_band, -stride, line_axis, 0.0)
        high_source = moved(source, -stride, line_axis, 0.0)
        factor_low = -below_band / low_middle
        factor_high = -above_band / high_middle
        middle = middle + factor_low * low_upper + factor_high * high_lower
        source = source + factor_low * low_source + factor_high * high_source
        below_band = factor_low * low_lower
        above_band = factor_high * high_upper
        stride = stride * 2
    return source / middle


def implicit_bands(low_face, high_face):
    return (
        -mesh_courant_number * low_face,
        1.0 + mesh_courant_number * (low_face + high_face),
        -mesh_courant_number * high_face,
    )


def matrix_product(left_side, right_side):
    return (
        left_side[0] * right_side[0] + left_side[1] * right_side[2],
        left_side[0] * right_side[1] + left_side[1] * right_side[3],
        left_side[2] * right_side[0] + left_side[3] * right_side[2],
        left_side[2] * right_side[1] + left_side[3] * right_side[3],
    )


def matrix_inverse(matrix):
    determinant = matrix[0] * matrix[3] - matrix[1] * matrix[2]
    return (
        matrix[3] / determinant,
        -matrix[1] / determinant,
        -matrix[2] / determinant,
        matrix[0] / determinant,
    )


def matrix_apply(matrix, target):
    return (
        matrix[0] * target[0] + matrix[1] * target[1],
        matrix[2] * target[0] + matrix[3] * target[1],
    )


def matrix_sum(left_side, right_side):
    return tuple(
        (left_entry + right_entry for left_entry, right_entry in zip(left_side, right_side))
    )


def matrix_negated(matrix):
    return tuple((-entry_value for entry_value in matrix))


def pack_bundle(couple_low, pivot_matrix, couple_high, target):
    shifted_pivot = (pivot_matrix[0] - 1.0, pivot_matrix[1], pivot_matrix[2], pivot_matrix[3] - 1.0)
    return jnp.stack(couple_low + shifted_pivot + couple_high + target)


def unpack_bundle(bundle):
    couple_low = (bundle[0], bundle[1], bundle[2], bundle[3])
    pivot_matrix = (bundle[4] + 1.0, bundle[5], bundle[6], bundle[7] + 1.0)
    couple_high = (bundle[8], bundle[9], bundle[10], bundle[11])
    target = (bundle[12], bundle[13])
    return (couple_low, pivot_matrix, couple_high, target)


def block_rounds(below_rows, above_rows, device_count, fetch_pair):
    nothing = jnp.zeros_like(below_rows[0])
    couple_low = (-below_rows[1], -below_rows[3], nothing, nothing)
    couple_high = (nothing, nothing, -above_rows[0], -above_rows[2])
    pivot_matrix = (nothing + 1.0, nothing, nothing, nothing + 1.0)
    target = (below_rows[5], above_rows[4])
    stride = 1
    while stride < device_count:
        from_below, from_above = fetch_pair(
            pack_bundle(couple_low, pivot_matrix, couple_high, target), stride
        )
        low_couple, low_pivot, low_high, low_target = unpack_bundle(from_below)
        high_low, high_pivot, high_couple, high_target = unpack_bundle(from_above)
        factor_low = matrix_negated(matrix_product(couple_low, matrix_inverse(low_pivot)))
        factor_high = matrix_negated(matrix_product(couple_high, matrix_inverse(high_pivot)))
        pivot_matrix = matrix_sum(
            pivot_matrix,
            matrix_sum(matrix_product(factor_low, low_high), matrix_product(factor_high, high_low)),
        )
        target = matrix_sum(
            target,
            matrix_sum(
                matrix_apply(factor_low, low_target), matrix_apply(factor_high, high_target)
            ),
        )
        couple_low = matrix_product(factor_low, low_couple)
        couple_high = matrix_product(factor_high, high_couple)
        stride = stride * 2
    return matrix_apply(matrix_inverse(pivot_matrix), target)


def doubling_solver(reduced, device_count, fetch_pair):
    from_below, from_above = fetch_pair(jnp.stack(reduced), 1)
    return block_rounds(from_below, from_above, device_count, fetch_pair)


def split_lines(below_band, middle, above_band, source, line_axis, solver):
    length = source.shape[line_axis]
    places = lax.broadcasted_iota(jnp.int32, source.shape, line_axis)
    spike_low = jnp.where(places == 0, -below_band, 0.0)
    spike_high = jnp.where(places == length - 1, -above_band, 0.0)
    solved = cyclic_solve(
        below_band[None],
        middle[None],
        above_band[None],
        jnp.stack([source, spike_low, spike_high]),
        line_axis + 1,
    )
    first_row = lax.slice_in_dim(solved, 0, 1, axis=line_axis + 1)
    final_row = lax.slice_in_dim(solved, length - 1, length, axis=line_axis + 1)
    reduced = (first_row[1], final_row[1], first_row[2], final_row[2], first_row[0], final_row[0])
    left_value, right_value = solver(reduced)
    return solved[0] + left_value * solved[1] + right_value * solved[2]


def shards(initial_heat_state, thermal_conductance_grid):
    joined_arrays = jnp.stack([initial_heat_state, thermal_conductance_grid])
    padded = with_halo(joined_arrays, (("zg", 2), ("gy", 1)), 1)
    along_y = padded[:, :, 1:-1, :]
    faces_y = harmonic(along_y[1, 1:], along_y[1, :-1])
    south_interface = faces_y[:-1]
    north_interface = faces_y[1:]
    field_y = along_y[0]
    second_difference_north = north_interface * (field_y[2:] - field_y[1:-1]) - south_interface * (
        field_y[1:-1] - field_y[:-2]
    )
    along_z = padded[:, 1:-1, :, :]
    faces_z = harmonic(along_z[1, :, 1:], along_z[1, :, :-1])
    bottom_interface = faces_z[:, :-1]
    top_interface = faces_z[:, 1:]
    field_z = along_z[0]
    second_difference_vertical = top_interface * (
        field_z[:, 2:] - field_z[:, 1:-1]
    ) - bottom_interface * (field_z[:, 1:-1] - field_z[:, :-2])
    low_x = harmonic(thermal_conductance_grid, moved(thermal_conductance_grid, 1, 2, 0.0))
    high_x = moved(low_x, -1, 2, 0.0)
    first_axis_forcing = (
        initial_heat_state
        + mesh_courant_number * second_difference_north
        + mesh_courant_number * second_difference_vertical
    )
    band_low, band_mid, band_high = implicit_bands(low_x, high_x)
    first_pass = cyclic_solve(band_low, band_mid, band_high, first_axis_forcing, 2)
    source_y = first_pass - mesh_courant_number * second_difference_north
    bundle = jnp.stack([source_y, thermal_conductance_grid])
    columns = lax.all_to_all(bundle, "gy", split_axis=2, concat_axis=1, tiled=True)
    col_faces = harmonic(columns[1, 1:], columns[1, :-1])
    border = jnp.zeros_like(col_faces[:1])
    low_col = jnp.concatenate([border, col_faces], 0)
    high_col = jnp.concatenate([col_faces, border], 0)
    col_lower, col_middle, col_upper = implicit_bands(low_col, high_col)
    columns_done = cyclic_solve(col_lower, col_middle, col_upper, columns[0], 0)
    second_pass = lax.all_to_all(columns_done, "gy", split_axis=0, concat_axis=1, tiled=True)
    source_z = second_pass - mesh_courant_number * second_difference_vertical

    def fetch_z(bundle, stride):
        return (from_behind(bundle, "zg", stride), from_behind(bundle, "zg", -stride))

    def solver_z(reduced):
        return doubling_solver(reduced, lax.axis_size("zg"), fetch_z)

    z_lower, z_middle, z_upper = implicit_bands(bottom_interface, top_interface)
    return split_lines(z_lower, z_middle, z_upper, source_z, 1, solver_z)


def solution(mesh):
    return jax.shard_map(
        shards,
        mesh=mesh,
        in_specs=(P("gy", "zg", None), P("gy", "zg", None)),
        out_specs=P("gy", "zg", None),
        check_vma=False,
    )
```

profile of v0, /device:TPU:4, one launch (start us, length us, event | category | flops | bytes accessed | tf_op | source)
XLA Modules:
  0.0 102.1 jit_solution(1383798884474840152)
XLA Ops:
  0.0 1.1 %copy.38 = f32[4,64,127]{2,0,1:T(4,128)S(1)} copy(f32[4,64,127]{2,1,0:T(8,128)} %bitcast.716) | data formatting | bytes 260096
  1.1 0.2 broadcast_multiply_fusion
  1.3 0.7 copy-done
  2.1 3.1 %collective-permute-start = (f32[2,4,1,128]{3,1,2,0:T(4,128)S(1)}, f32[2,4,1,128]{3,1,2,0:T(4,128)S(1)}, u32[]{:S(2)}, u32[]{:S(2)}) collective-permute-start(f32[2,4,1,128]{3,1,2,0:T(4,128)S(1)} %get-tuple-element.127), channel_id=1, source_target_pairs={{0,64},{64,128},{128,192},{1,65},{65,129},{129,193},{2,66},{66,130... | collective-permute-start | bytes 12296 | tf_op jit(solution)/shard_map/ppermute | solution.py:17
  5.2 2.7 %collective-permute-start.1 = (f32[2,4,1,128]{3,1,2,0:T(4,128)S(1)}, f32[2,4,1,128]{3,1,2,0:T(4,128)S(1)}, u32[]{:S(2)}, u32[]{:S(2)}) collective-permute-start(f32[2,4,1,128]{3,1,2,0:T(4,128)S(1)} %get-tuple-element.126), channel_id=1, source_target_pairs={{64,0},{128,64},{192,128},{65,1},{129,65},{193,129},{66,2},{130,66... | collective-permute-start | bytes 12296 | tf_op jit(solution)/shard_map/ppermute | solution.py:19
  8.1 0.1 slice.1039
  8.4 0.1 fusion.167
  8.6 2.1 %collective-permute-done.1 = f32[2,4,1,128]{3,1,2,0:T(4,128)S(1)} collective-permute-done((f32[2,4,1,128]{3,1,2,0:T(4,128)S(1)}, f32[2,4,1,128]{3,1,2,0:T(4,128)S(1)}, u32[]{:S(2)}, u32[]{:S(2)}) %collective-permute-start.1) | collective-permute-done | bytes 4128 | tf_op jit(solution)/shard_map/ppermute | solution.py:19
  10.8 1.3 %collective-permute-start.3 = (f32[2,1,66,128]{3,1,2,0:T(1,128)S(1)}, f32[2,1,66,128]{3,1,2,0:T(1,128)S(1)}, u32[]{:S(2)}, u32[]{:S(2)}) collective-permute-start(f32[2,1,66,128]{3,1,2,0:T(1,128)S(1)} %get-tuple-element.122), channel_id=1, source_target_pairs={{0,1},{1,2},{2,3},{3,4},{4,5},{5,6},{6,7},{7,8},{8,9},{9,10},{10,1... | collective-permute-start | bytes 202760 | tf_op jit(solution)/shard_map/ppermute | solution.py:17
  12.1 1.3 %collective-permute-start.2 = (f32[2,1,66,128]{3,1,2,0:T(1,128)S(1)}, f32[2,1,66,128]{3,1,2,0:T(1,128)S(1)}, u32[]{:S(2)}, u32[]{:S(2)}) collective-permute-start(f32[2,1,66,128]{3,1,2,0:T(1,128)S(1)} %get-tuple-element.121), channel_id=1, source_target_pairs={{1,0},{2,1},{3,2},{4,3},{5,4},{6,5},{7,6},{8,7},{9,8},{10,9},{11,1... | collective-permute-start | bytes 202760 | tf_op jit(solution)/shard_map/ppermute | solution.py:19
  13.5 0.2 fusion.20
  15.3 2.1 %collective-permute-done.2 = f32[2,1,66,128]{3,1,2,0:T(1,128)S(1)} collective-permute-done((f32[2,1,66,128]{3,1,2,0:T(1,128)S(1)}, f32[2,1,66,128]{3,1,2,0:T(1,128)S(1)}, u32[]{:S(2)}, u32[]{:S(2)}) %collective-permute-start.2) | collective-permute-done | bytes 67616 | tf_op jit(solution)/shard_map/ppermute | solution.py:19
  17.4 0.1 add_divide_fusion.1
  17.6 0.3 add_add_fusion
  18.0 0.3 multiply_add_fusion.35
  18.3 0.2 fusion.165
  18.5 0.4 multiply_add_fusion.34
  19.0 0.1 fusion.159
  19.1 0.1 fusion.160
  19.3 0.2 multiply_add_fusion.33
  19.6 0.4 multiply_add_fusion.32
  20.2 0.1 fusion.155
  20.3 0.1 fusion.156
  20.4 0.2 multiply_add_fusion.31
  20.8 0.4 multiply_add_fusion.30
  21.3 0.1 fusion.151
  21.4 0.1 fusion.152
  21.6 0.2 multiply_add_fusion.29
  22.0 0.4 multiply_add_fusion.28
  22.5 0.1 fusion.147
  22.6 0.1 fusion.148
  22.7 0.2 multiply_add_fusion.27
  23.1 0.4 multiply_add_fusion.26
  23.6 0.1 fusion.146
  23.8 0.3 pad_multiply_fusion.24
  24.2 0.1 fusion.144
  24.3 0.1 fusion.143
  24.5 0.3 subtract_bitcast_fusion.1
  24.8 0.8 copy.27
  25.6 14.7 %all-to-all-start = ((f32[2,4,64,128]{3,1,0,2:T(4,128)}), f32[2,4,64,128]{3,1,0,2:T(4,128)S(1)}, u32[]{:S(2)}, u32[]{:S(2)}) async-start(f32[2,4,64,128]{3,1,0,2:T(4,128)} %copy.27), calls=%async_computation | async-start | bytes 524288 | tf_op jit(solution)/shard_map/all_to_all | solution.py:212
  40.3 0.1 multiply_add_fusion.5
  40.5 11.6 %all-to-all-done = f32[2,4,64,128]{3,1,0,2:T(4,128)S(1)} async-done(((f32[2,4,64,128]{3,1,0,2:T(4,128)}), f32[2,4,64,128]{3,1,0,2:T(4,128)S(1)}, u32[]{:S(2)}, u32[]{:S(2)}) %all-to-all-start) | async-done | bytes 262176 | tf_op jit(solution)/shard_map/all_to_all | solution.py:212
  52.6 0.1 multiply_add_fusion.21
  53.5 0.1 multiply_add_fusion.15
  54.4 0.7 add_divide_fusion.3
  55.1 6.0 %all-to-all-start.1 = ((f32[256,1,128]{2,1,0:T(1,128)}), f32[256,1,128]{2,1,0:T(1,128)S(1)}, u32[]{:S(2)}, u32[]{:S(2)}) async-start(f32[256,1,128]{2,1,0:T(1,128)} %bitcast.19), calls=%async_computation.1 | async-start | bytes 262144 | tf_op jit(solution)/shard_map/all_to_all | solution.py:219
  61.4 10.1 %all-to-all-done.1 = f32[256,1,128]{2,1,0:T(1,128)S(1)} async-done(((f32[256,1,128]{2,1,0:T(1,128)}), f32[256,1,128]{2,1,0:T(1,128)S(1)}, u32[]{:S(2)}, u32[]{:S(2)}) %all-to-all-start.1) | async-done | bytes 131104 | tf_op jit(solution)/shard_map/all_to_all | solution.py:219
  71.7 0.2 multiply_add_fusion.4
  72.0 0.2 multiply_add_fusion.3
  72.3 0.2 multiply_add_fusion.2
  72.6 0.2 multiply_add_fusion.1
  72.8 0.2 multiply_add_fusion
  73.0 0.2 add_divide_fusion
  73.2 1.9 %collective-permute-start.4 = (f32[6,4,1,128]{3,1,2,0:T(4,128)S(1)}, f32[6,4,1,128]{3,1,2,0:T(4,128)S(1)}, u32[]{:S(2)}, u32[]{:S(2)}) collective-permute-start(f32[6,4,1,128]{3,1,2,0:T(4,128)S(1)} %constant_dynamic-update-slice_fusion), channel_id=1, source_target_pairs={{0,64},{64,128},{128,192},{1,65},{65,129},{129,193},{2,66},{66,130... | collective-permute-start | bytes 36872 | tf_op jit(solution)/shard_map/ppermute | solution.py:29
  75.2 3.9 %collective-permute-start.5 = (f32[6,4,1,128]{3,1,2,0:T(4,128)S(1)}, f32[6,4,1,128]{3,1,2,0:T(4,128)S(1)}, u32[]{:S(2)}, u32[]{:S(2)}) collective-permute-start(f32[6,4,1,128]{3,1,2,0:T(4,128)S(1)} %constant_dynamic-update-slice_fusion), channel_id=1, source_target_pairs={{64,0},{128,64},{192,128},{65,1},{129,65},{193,129},{66,2},{130,66... | collective-permute-start | bytes 36872 | tf_op jit(solution)/shard_map/ppermute | solution.py:29
  79.2 1.6 %collective-permute-done.5 = f32[6,4,1,128]{3,1,2,0:T(4,128)S(1)} collective-permute-done((f32[6,4,1,128]{3,1,2,0:T(4,128)S(1)}, f32[6,4,1,128]{3,1,2,0:T(4,128)S(1)}, u32[]{:S(2)}, u32[]{:S(2)}) %collective-permute-start.5) | collective-permute-done | bytes 12320 | tf_op jit(solution)/shard_map/ppermute | solution.py:29
  80.8 1.9 %collective-permute-start.6 = (f32[14,4,1,128]{3,1,2,0:T(4,128)S(1)}, f32[14,4,1,128]{3,1,2,0:T(4,128)S(1)}, u32[]{:S(2)}, u32[]{:S(2)}) collective-permute-start(f32[14,4,1,128]{3,1,2,0:T(4,128)S(1)} %constant_dynamic-update-slice_fusion.6), channel_id=1, source_target_pairs={{0,64},{64,128},{128,192},{1,65},{65,129},{129,193},{2,66},{66,130... | collective-permute-start | bytes 86024 | tf_op jit(solution)/shard_map/ppermute | solution.py:29
  82.7 3.9 %collective-permute-start.7 = (f32[14,4,1,128]{3,1,2,0:T(4,128)S(1)}, f32[14,4,1,128]{3,1,2,0:T(4,128)S(1)}, u32[]{:S(2)}, u32[]{:S(2)}) collective-permute-start(f32[14,4,1,128]{3,1,2,0:T(4,128)S(1)} %constant_dynamic-update-slice_fusion.6), channel_id=1, source_target_pairs={{64,0},{128,64},{192,128},{65,1},{129,65},{193,129},{66,2},{130,66... | collective-permute-start | bytes 86024 | tf_op jit(solution)/shard_map/ppermute | solution.py:29
  86.7 1.8 %collective-permute-done.7 = f32[14,4,1,128]{3,1,2,0:T(4,128)S(1)} collective-permute-done((f32[14,4,1,128]{3,1,2,0:T(4,128)S(1)}, f32[14,4,1,128]{3,1,2,0:T(4,128)S(1)}, u32[]{:S(2)}, u32[]{:S(2)}) %collective-permute-start.7) | collective-permute-done | bytes 28704 | tf_op jit(solution)/shard_map/ppermute | solution.py:29
  88.6 5.4 %collective-permute-start.9 = (f32[14,4,1,128]{3,1,2,0:T(4,128)S(1)}, f32[14,4,1,128]{3,1,2,0:T(4,128)S(1)}, u32[]{:S(2)}, u32[]{:S(2)}) collective-permute-start(f32[14,4,1,128]{3,1,2,0:T(4,128)S(1)} %constant_dynamic-update-slice_fusion.17), channel_id=1, source_target_pairs={{128,0},{192,64},{129,1},{193,65},{130,2},{194,66},{131,3},{195,67... | collective-permute-start | bytes 86024 | tf_op jit(solution)/shard_map/ppermute | solution.py:29
  94.0 1.3 %collective-permute-start.8 = (f32[14,4,1,128]{3,1,2,0:T(4,128)S(1)}, f32[14,4,1,128]{3,1,2,0:T(4,128)S(1)}, u32[]{:S(2)}, u32[]{:S(2)}) collective-permute-start(f32[14,4,1,128]{3,1,2,0:T(4,128)S(1)} %constant_dynamic-update-slice_fusion.17), channel_id=1, source_target_pairs={{0,128},{64,192},{1,129},{65,193},{2,130},{66,194},{3,131},{67,195... | collective-permute-start | bytes 86024 | tf_op jit(solution)/shard_map/ppermute | solution.py:29
  95.4 0.2 collective-permute-done.9
  95.6 5.7 %collective-permute-done.8 = f32[14,4,1,128]{3,1,2,0:T(4,128)S(1)} collective-permute-done((f32[14,4,1,128]{3,1,2,0:T(4,128)S(1)}, f32[14,4,1,128]{3,1,2,0:T(4,128)S(1)}, u32[]{:S(2)}, u32[]{:S(2)}) %collective-permute-start.8) | collective-permute-done | bytes 28704 | tf_op jit(solution)/shard_map/ppermute | solution.py:29
  101.4 0.7 copy.32
  (157 shorter events, 6.5 us)
Async XLA Ops:
  0.0 1.1 %copy-start.1 = (f32[4,64,128]{2,1,0:T(8,128)S(1)}, f32[4,64,128]{2,1,0:T(8,128)}, u32[]{:S(2)}) copy-start(f32[4,64,128]{2,1,0:T(8,128)} %param.3) | copy-start | bytes 393220
  1.1 0.9 copy-start
  2.1 6.5 %collective-permute-start = (f32[2,4,1,128]{3,1,2,0:T(4,128)S(1)}, f32[2,4,1,128]{3,1,2,0:T(4,128)S(1)}, u32[]{:S(2)}, u32[]{:S(2)}) collective-permute-start(f32[2,4,1,128]{3,1,2,0:T(4,128)S(1)} %get-tuple-element.127), channel_id=1, source_target_pairs={{0,64},{64,128},{128,192},{1,65},{65,129},{129,193},{2,66},{66,130... | collective-permute-start | bytes 12296 | tf_op jit(solution)/shard_map/ppermute | solution.py:17
  5.2 5.5 %collective-permute-start.1 = (f32[2,4,1,128]{3,1,2,0:T(4,128)S(1)}, f32[2,4,1,128]{3,1,2,0:T(4,128)S(1)}, u32[]{:S(2)}, u32[]{:S(2)}) collective-permute-start(f32[2,4,1,128]{3,1,2,0:T(4,128)S(1)} %get-tuple-element.126), channel_id=1, source_target_pairs={{64,0},{128,64},{192,128},{65,1},{129,65},{193,129},{66,2},{130,66... | collective-permute-start | bytes 12296 | tf_op jit(solution)/shard_map/ppermute | solution.py:19
  10.8 4.4 %collective-permute-start.3 = (f32[2,1,66,128]{3,1,2,0:T(1,128)S(1)}, f32[2,1,66,128]{3,1,2,0:T(1,128)S(1)}, u32[]{:S(2)}, u32[]{:S(2)}) collective-permute-start(f32[2,1,66,128]{3,1,2,0:T(1,128)S(1)} %get-tuple-element.122), channel_id=1, source_target_pairs={{0,1},{1,2},{2,3},{3,4},{4,5},{5,6},{6,7},{7,8},{8,9},{9,10},{10,1... | collective-permute-start | bytes 202760 | tf_op jit(solution)/shard_map/ppermute | solution.py:17
  12.1 5.3 %collective-permute-start.2 = (f32[2,1,66,128]{3,1,2,0:T(1,128)S(1)}, f32[2,1,66,128]{3,1,2,0:T(1,128)S(1)}, u32[]{:S(2)}, u32[]{:S(2)}) collective-permute-start(f32[2,1,66,128]{3,1,2,0:T(1,128)S(1)} %get-tuple-element.121), channel_id=1, source_target_pairs={{1,0},{2,1},{3,2},{4,3},{5,4},{6,5},{7,6},{8,7},{9,8},{10,9},{11,1... | collective-permute-start | bytes 202760 | tf_op jit(solution)/shard_map/ppermute | solution.py:19
  25.6 26.5 %all-to-all-start = ((f32[2,4,64,128]{3,1,0,2:T(4,128)}), f32[2,4,64,128]{3,1,0,2:T(4,128)S(1)}, u32[]{:S(2)}, u32[]{:S(2)}) async-start(f32[2,4,64,128]{3,1,0,2:T(4,128)} %copy.27), calls=%async_computation | async-start | bytes 524288 | tf_op jit(solution)/shard_map/all_to_all | solution.py:212
  55.1 16.3 %all-to-all-start.1 = ((f32[256,1,128]{2,1,0:T(1,128)}), f32[256,1,128]{2,1,0:T(1,128)S(1)}, u32[]{:S(2)}, u32[]{:S(2)}) async-start(f32[256,1,128]{2,1,0:T(1,128)} %bitcast.19), calls=%async_computation.1 | async-start | bytes 262144 | tf_op jit(solution)/shard_map/all_to_all | solution.py:219
  73.2 5.9 %collective-permute-start.4 = (f32[6,4,1,128]{3,1,2,0:T(4,128)S(1)}, f32[6,4,1,128]{3,1,2,0:T(4,128)S(1)}, u32[]{:S(2)}, u32[]{:S(2)}) collective-permute-start(f32[6,4,1,128]{3,1,2,0:T(4,128)S(1)} %constant_dynamic-update-slice_fusion), channel_id=1, source_target_pairs={{0,64},{64,128},{128,192},{1,65},{65,129},{129,193},{2,66},{66,130... | collective-permute-start | bytes 36872 | tf_op jit(solution)/shard_map/ppermute | solution.py:29
  75.2 5.6 %collective-permute-start.5 = (f32[6,4,1,128]{3,1,2,0:T(4,128)S(1)}, f32[6,4,1,128]{3,1,2,0:T(4,128)S(1)}, u32[]{:S(2)}, u32[]{:S(2)}) collective-permute-start(f32[6,4,1,128]{3,1,2,0:T(4,128)S(1)} %constant_dynamic-update-slice_fusion), channel_id=1, source_target_pairs={{64,0},{128,64},{192,128},{65,1},{129,65},{193,129},{66,2},{130,66... | collective-permute-start | bytes 36872 | tf_op jit(solution)/shard_map/ppermute | solution.py:29
  80.8 5.9 %collective-permute-start.6 = (f32[14,4,1,128]{3,1,2,0:T(4,128)S(1)}, f32[14,4,1,128]{3,1,2,0:T(4,128)S(1)}, u32[]{:S(2)}, u32[]{:S(2)}) collective-permute-start(f32[14,4,1,128]{3,1,2,0:T(4,128)S(1)} %constant_dynamic-update-slice_fusion.6), channel_id=1, source_target_pairs={{0,64},{64,128},{128,192},{1,65},{65,129},{129,193},{2,66},{66,130... | collective-permute-start | bytes 86024 | tf_op jit(solution)/shard_map/ppermute | solution.py:29
  82.7 5.8 %collective-permute-start.7 = (f32[14,4,1,128]{3,1,2,0:T(4,128)S(1)}, f32[14,4,1,128]{3,1,2,0:T(4,128)S(1)}, u32[]{:S(2)}, u32[]{:S(2)}) collective-permute-start(f32[14,4,1,128]{3,1,2,0:T(4,128)S(1)} %constant_dynamic-update-slice_fusion.6), channel_id=1, source_target_pairs={{64,0},{128,64},{192,128},{65,1},{129,65},{193,129},{66,2},{130,66... | collective-permute-start | bytes 86024 | tf_op jit(solution)/shard_map/ppermute | solution.py:29
  88.6 6.9 %collective-permute-start.9 = (f32[14,4,1,128]{3,1,2,0:T(4,128)S(1)}, f32[14,4,1,128]{3,1,2,0:T(4,128)S(1)}, u32[]{:S(2)}, u32[]{:S(2)}) collective-permute-start(f32[14,4,1,128]{3,1,2,0:T(4,128)S(1)} %constant_dynamic-update-slice_fusion.17), channel_id=1, source_target_pairs={{128,0},{192,64},{129,1},{193,65},{130,2},{194,66},{131,3},{195,67... | collective-permute-start | bytes 86024 | tf_op jit(solution)/shard_map/ppermute | solution.py:29
  94.0 7.3 %collective-permute-start.8 = (f32[14,4,1,128]{3,1,2,0:T(4,128)S(1)}, f32[14,4,1,128]{3,1,2,0:T(4,128)S(1)}, u32[]{:S(2)}, u32[]{:S(2)}) collective-permute-start(f32[14,4,1,128]{3,1,2,0:T(4,128)S(1)} %constant_dynamic-update-slice_fusion.17), channel_id=1, source_target_pairs={{0,128},{64,192},{1,129},{65,193},{2,130},{66,194},{3,131},{67,195... | collective-permute-start | bytes 86024 | tf_op jit(solution)/shard_map/ppermute | solution.py:29
where the time goes:
time: 103 us; the launch traced here: 102 us
  starting transfers between devices  47.5 us (46%)
  waiting for transfers between devices  35.1 us (34%)
  other arithmetic  9.61 us (9%)
  local copies, waits for them, and re-layouts  8.6 us (8%)
  between operations  1.26 us (1%)
    ppermute x6, starting transfers between devices, from_behind(): return lax.ppermute(x, axis, pairs)  18.3 us
    all_to_all x1, starting transfers between devices, shards(): lax.all_to_all(bundle, 'gy', split_axis=2, concat_axis=1, tiled=True)  14.7 us
    all_to_all x1, waiting for transfers between devices, shards(): lax.all_to_all(bundle, 'gy', split_axis=2, concat_axis=1, tiled=True)  11.6 us
    all_to_all x1, waiting for transfers between devices, shards(): lax.all_to_all(columns_done, 'gy', split_axis=0, concat_axis=1, tiled=True)  10.1 us
    ppermute x6, waiting for transfers between devices, from_behind(): return lax.ppermute(x, axis, pairs)  9.22 us
    all_to_all x1, starting transfers between devices, shards(): lax.all_to_all(columns_done, 'gy', split_axis=0, concat_axis=1, tiled=True)  6.03 us
    ppermute x2, starting transfers between devices, with_halo(): lax.ppermute(tail, axis, [(i, (i + 1) % count) for i in range(ends)])  4.4 us
    ppermute x2, waiting for transfers between devices, with_halo(): lax.ppermute(head, axis, [((i + 1) % count, i) for i in range(ends)])  4.24 us
  transfers between devices with their start and end apart: 12, of which 8 were waited for; matrix products, arithmetic and copies ran while one was open for 3% of the time, Pallas kernels for 0%

commit v1 on v0

v1 whole, which is shorter than its diff:
```python
import jax
import jax.numpy as jnp
from jax import lax
from jax.experimental import pallas as pl
from jax.experimental.pallas import tpu as pltpu
from jax.sharding import PartitionSpec as P

mesh_courant_number = 300.0

NB, NZB, NX = 4, 64, 128
NGY, NZG = 64, 4
X_STRIDES = (1, 2, 4, 8, 16, 32, 64)
Z_STRIDES = (1, 2, 4, 8, 16, 32)
VALUES = 5


def face(k, q):
    return (2.0 * mesh_courant_number) * k * q / (k + q)


def shift(v, by, axis):
    return pltpu.roll(v, by % v.shape[axis], axis)


def rows_of(shape, axis):
    return lax.broadcasted_iota(jnp.int32, shape, axis)


def reduction_factors(leak, low, high, strides, axis, put):
    for j, s in enumerate(strides):
        inverse = 1.0 / (leak + low + high)
        from_low = low * shift(inverse, s, axis)
        from_high = high * shift(inverse, -s, axis)
        put(2 * j, from_low)
        put(2 * j + 1, from_high)
        leak = leak + from_low * shift(leak, s, axis) + from_high * shift(leak, -s, axis)
        low = from_low * shift(low, s, axis)
        high = from_high * shift(high, -s, axis)
    put(2 * len(strides), 1.0 / (leak + low + high))


def reduced_source(b, strides, axis, get):
    for j, s in enumerate(strides):
        b = b + get(2 * j) * shift(b, s, axis) + get(2 * j + 1) * shift(b, -s, axis)
    return b * get(2 * len(strides))


def inner_kernel(t_ref, k_ref, factors_ref, inner_ref, faces_ref):
    lane = rows_of((NZB, NX), 1)
    row = rows_of((NZB, NX), 0)
    flux_y = None
    for y in range(NB):
        k = k_ref[y]
        t = t_ref[y]
        low = jnp.where(lane > 0, face(k, shift(k, 1, 1)), 0.0)
        high = shift(low, -1, 1)
        flux = low * (t - shift(t, 1, 1))
        total = shift(flux, -1, 1) - flux
        face_z = jnp.where(row > 0, face(k, shift(k, 1, 0)), 0.0)
        flux = face_z * (t - shift(t, 1, 0))
        total = total + (shift(flux, -1, 0) - flux)
        if y > 0:
            total = total - flux_y
        if y < NB - 1:
            next_face = face(k_ref[y + 1], k)
            faces_ref[y] = next_face
            flux_y = next_face * (t_ref[y + 1] - t)
            total = total + flux_y
        inner_ref[y] = total
    half = NZB // 2
    for y in range(NB):
        for part in range(2):
            at = pl.ds(part * half, half)
            k = k_ref[y, at, :]
            low = jnp.where(rows_of((half, NX), 1) > 0, face(k, shift(k, 1, 1)), 0.0)
            high = shift(low, -1, 1)

            def put(j, v):
                factors_ref[j, y, at, :] = v

            reduction_factors(jnp.ones_like(k), low, high, X_STRIDES, 1, put)


def first_kernel(t_ref, k_ref, factors_ref, inner_ref, faces_ref, yp_ref, yn_ref, zp_ref, zn_ref,
                 bundle_ref, back_ref):
    gy = lax.axis_index("gy")
    zg = lax.axis_index("zg")
    has_south = jnp.where(gy > 0, 1.0, 0.0)
    has_north = jnp.where(gy < NGY - 1, 1.0, 0.0)
    has_below = jnp.where(zg > 0, 1.0, 0.0)
    has_above = jnp.where(zg < NZG - 1, 1.0, 0.0)
    row = rows_of((NZB, NX), 0)
    solved = []
    g4 = None
    for y in range(NB):
        b = inner_ref[y]
        t = t_ref[y]
        k = k_ref[y]
        if y == 0:
            b = b + face(k, yp_ref[1] * has_south) * (yp_ref[0] - t)
        if y == NB - 1:
            g4 = face(k, yn_ref[1] * has_north)
            b = b + g4 * (yn_ref[0] - t)
        below = face(k[:1], zp_ref[1, y:y + 1] * has_below) * (zp_ref[0, y:y + 1] - t[:1])
        above = face(k[NZB - 1:], zn_ref[1, y:y + 1] * has_above) * (zn_ref[0, y:y + 1] - t[NZB - 1:])
        b = b + jnp.where(row == 0, below, 0.0) + jnp.where(row == NZB - 1, above, 0.0)
        solved.append(reduced_source(b, X_STRIDES, 1, lambda j: factors_ref[j, y]))
    b0, b1, b2, b3 = solved
    g1, g2, g3 = faces_ref[0], faces_ref[1], faces_ref[2]
    i1 = 1.0 / (1.0 + g1 + g2)
    left, right = g1 * i1, g2 * i1
    source = b0 + left * b1
    b2 = b2 + right * b1
    leak = 1.0 + left
    m2 = 1.0 + right
    a2 = g1 * right
    i2 = 1.0 / (m2 + a2 + g3)
    left, right = a2 * i2, g3 * i2
    source = source + left * b2
    b3 = b3 + right * b2
    leak = leak + left * m2
    m3 = 1.0 + right * m2
    a3 = a2 * right
    i3 = 1.0 / (m3 + a3 + g4)
    left, right = a3 * i3, g4 * i3
    put = lambda v, x: pltpu.store(bundle_ref.at[pl.ds(v, NZB, stride=VALUES), :], x)
    put(0, leak + left * m3)
    put(1, right * m3)
    put(2, a3 * right)
    put(3, source + left * b3)
    put(4, right * b3)
    beta, lam, rho = b3 * i3, left, right
    back_ref[0, 2], back_ref[1, 2], back_ref[2, 2] = beta, lam, rho
    beta, lam, rho = (b2 + g3 * beta) * i2, (a2 + g3 * lam) * i2, g3 * rho * i2
    back_ref[0, 1], back_ref[1, 1], back_ref[2, 1] = beta, lam, rho
    beta, lam, rho = (b1 + g2 * beta) * i1, (g1 + g2 * lam) * i1, g2 * rho * i1
    back_ref[0, 0], back_ref[1, 0], back_ref[2, 0] = beta, lam, rho


def column_kernel(bundle_ref, out_ref):
    get = lambda v: bundle_ref[pl.ds(v, NGY, stride=VALUES), :]
    leak = get(0) + shift(get(1), 1, 0)
    high = get(2)
    low = shift(high, 1, 0)
    b = get(3) + shift(get(4), 1, 0)
    for s in (1, 2, 4, 8, 16, 32):
        inverse = 1.0 / (leak + low + high)
        from_low = low * shift(inverse, s, 0)
        from_high = high * shift(inverse, -s, 0)
        leak = leak + from_low * shift(leak, s, 0) + from_high * shift(leak, -s, 0)
        b = b + from_low * shift(b, s, 0) + from_high * shift(b, -s, 0)
        low = from_low * shift(low, s, 0)
        high = from_high * shift(high, -s, 0)
    own = b / (leak + low + high)
    out_ref[pl.ds(0, NGY, stride=2), :] = own
    out_ref[pl.ds(1, NGY, stride=2), :] = shift(own, -1, 0)


def z_kernel(k_ref, zn_ref, factors_ref, spikes_ref, coeffs_ref):
    zg = lax.axis_index("zg")
    has_above = jnp.where(zg < NZG - 1, 1.0, 0.0)
    row = rows_of((NZB, NX), 0)
    for y in range(NB):
        k = k_ref[y]
        g = face(k, shift(k, 1, 0))
        top = face(k[NZB - 1:], zn_ref[1, y:y + 1] * has_above)
        low = jnp.where(row > 1, g, 0.0)
        high = shift(low, -1, 0)
        at_first = jnp.where(row == 1, g, 0.0)
        at_last = jnp.where(row == NZB - 1, top, 0.0)

        def put(j, v):
            factors_ref[j, y] = v

        reduction_factors(1.0 + at_first + at_last, low, high, Z_STRIDES, 0, put)
        get = lambda j: factors_ref[j, y]
        lam = reduced_source(at_first, Z_STRIDES, 0, get)
        lam = jnp.where(row == 0, 1.0, lam)
        rho = reduced_source(at_last, Z_STRIDES, 0, get)
        spikes_ref[0, y] = lam
        spikes_ref[1, y] = rho
        coeffs_ref[0, y:y + 1] = jnp.sum(lam, axis=0, keepdims=True)
        coeffs_ref[1, y:y + 1] = jnp.sum(rho, axis=0, keepdims=True)
        coeffs_ref[2, y:y + 1] = lam[NZB - 1:] * top


def second_kernel(ends_ref, back_ref, spikes_ref, second_ref, sums_ref):
    own = ends_ref[pl.ds(0, NZB, stride=2), :]
    following = ends_ref[pl.ds(1, NZB, stride=2), :]
    for y in range(NB):
        if y == 0:
            u = own
        else:
            u = back_ref[0, y - 1] + back_ref[1, y - 1] * own + back_ref[2, y - 1] * following
        second_ref[y] = u
        sums_ref[0, y:y + 1] = jnp.sum(spikes_ref[0, y] * u, axis=0, keepdims=True)
        sums_ref[1, y:y + 1] = jnp.sum(spikes_ref[1, y] * u, axis=0, keepdims=True)


def local_z_kernel(second_ref, factors_ref, t_ref, out_ref):
    row = rows_of((NZB, NX), 0)
    for y in range(NB):
        b = jnp.where(row == 0, 0.0, second_ref[y])
        out_ref[y] = t_ref[y] + reduced_source(b, Z_STRIDES, 0, lambda j: factors_ref[j, y])


def last_kernel(local_ref, spikes_ref, c0_ref, c1_ref, c2_ref, c3_ref, s0_ref, s1_ref, s2_ref, s3_ref,
                out_ref, coeffs, sums, ends):
    zg = lax.axis_index("zg")
    for j, (c_ref, s_ref) in enumerate(((c0_ref, s0_ref), (c1_ref, s1_ref), (c2_ref, s2_ref), (c3_ref, s3_ref))):
        at = lax.rem(zg + (NZG - j), NZG)
        coeffs[at] = c_ref[...]
        sums[at] = s_ref[...]
    inverses, sources = [], []
    leak, source = coeffs[0, 0], sums[0, 0]
    for d in range(NZG):
        couple = coeffs[d, 2]
        inverse = 1.0 / (leak + couple)
        inverses.append(inverse)
        sources.append(source)
        if d + 1 < NZG:
            passed = couple * inverse
            leak = coeffs[d + 1, 0] + coeffs[d, 1] + passed * leak
            source = sums[d + 1, 0] + sums[d, 1] + passed * source
    value = jnp.zeros_like(source)
    ends[NZG] = value
    for d in reversed(range(NZG)):
        value = (sources[d] + coeffs[d, 2] * value) * inverses[d]
        ends[d] = value
    own = ends[zg]
    following = ends[zg + 1]
    for y in range(NB):
        out_ref[y] = (local_ref[y] + spikes_ref[0, y] * own[y:y + 1] + spikes_ref[1, y] * following[y:y + 1])


def call(kernel, name, outs, args, scratch=(), cost=2000000):
    shapes = [jax.ShapeDtypeStruct(o, jnp.float32) for o in outs]
    vmem = pl.BlockSpec(memory_space=pltpu.VMEM)
    return pl.pallas_call(
        kernel,
        name=name,
        out_shape=shapes,
        in_specs=[vmem] * len(args),
        out_specs=[vmem] * len(outs),
        scratch_shapes=[pltpu.VMEM(s, jnp.float32) for s in scratch],
        cost_estimate=pl.CostEstimate(flops=cost, bytes_accessed=cost, transcendentals=0),
        compiler_params=pltpu.CompilerParams(vmem_limit_bytes=24 * 1024 * 1024),
    )(*args)


def around(x, axis, by):
    count = lax.axis_size(axis)
    return lax.ppermute(x, axis, [(i, (i + by) % count) for i in range(count)])


def shards(t, k):
    joined = jnp.stack([t, k])
    yp = around(joined[:, NB - 1], "gy", 1)
    yn = around(joined[:, 0], "gy", -1)
    zp = around(joined[:, :, NZB - 1], "zg", 1)
    zn = around(joined[:, :, 0], "zg", -1)
    block = (NB, NZB, NX)
    factors, inner, faces = call(
        inner_kernel, "inner", [(2 * len(X_STRIDES) + 1,) + block, block, (NB - 1, NZB, NX)], [t, k])
    bundle, back = call(
        first_kernel, "first", [(NZB * VALUES, NX), (3, NB - 1, NZB, NX)],
        [t, k, factors, inner, faces, yp, yn, zp, zn])
    columns = lax.all_to_all(bundle, "gy", split_axis=0, concat_axis=0, tiled=True)
    z_factors, spikes, coeffs = call(
        z_kernel, "z", [(2 * len(Z_STRIDES) + 1,) + block, (2,) + block, (3, NB, NX)], [k, zn])
    coeffs = [coeffs] + [around(coeffs, "zg", j) for j in range(1, NZG)]
    (ends,) = call(column_kernel, "column", [(2 * NGY, NX)], [columns])
    ends = lax.all_to_all(ends, "gy", split_axis=0, concat_axis=0, tiled=True)
    second, sums = call(second_kernel, "second", [block, (2, NB, NX)], [ends, back, spikes])
    sums = [sums] + [around(sums, "zg", j) for j in range(1, NZG)]
    (local,) = call(local_z_kernel, "local_z", [block], [second, z_factors, t])
    (out,) = call(last_kernel, "last", [block], [local, spikes] + coeffs + sums,
                  scratch=((NZG, 3, NB, NX), (NZG, 2, NB, NX), (NZG + 1, NB, NX)))
    return out


def solution(mesh):
    return jax.shard_map(
        shards,
        mesh=mesh,
        in_specs=(P("gy", "zg", None), P("gy", "zg", None)),
        out_specs=P("gy", "zg", None),
        check_vma=False,
    )
```

time: 103 us -> 63.6 us (0.62)
  the two profiles are of different devices: /device:TPU:4 before, /device:TPU:1 now
where the time goes in v1:
time: 63.6 us; the launch traced here: 63.4 us
  blocking collectives  24.8 us (39%)
  starting transfers between devices  19.6 us (31%)
  Pallas kernels  7.49 us (12%)
  waiting for transfers between devices  7.32 us (12%)
  local copies, waits for them, and re-layouts  3.92 us (6%)
    all_to_all x1, blocking collectives, shards(): lax.all_to_all(bundle, 'gy', split_axis=0, concat_axis=0, tiled=True)  24.8 us
    ppermute x10, starting transfers between devices, around(): return lax.ppermute(x, axis, [(i, (i + by) % count) for i in range(count)])  13.5 us
    pallas_call x7, Pallas kernels, call(): pl.pallas_call(kernel, name=name, out_shape=shapes, in_specs=[vmem] * len...  7.49 us
    all_to_all x1, starting transfers between devices, shards(): ends = lax.all_to_all(ends, 'gy', split_axis=0, concat_axis=0, tiled=True)  6.03 us
    all_to_all x1, waiting for transfers between devices, shards(): ends = lax.all_to_all(ends, 'gy', split_axis=0, concat_axis=0, tiled=True)  5.04 us
    unnamed x10, local copies, waits for them, and re-layouts  2.71 us
    ppermute x10, waiting for transfers between devices, around(): return lax.ppermute(x, axis, [(i, (i + by) % count) for i in range(count)])  2.27 us
  transfers between devices with their start and end apart: 11, of which 3 were waited for; matrix products, arithmetic and copies ran while one was open for 0% of the time, Pallas kernels for 8%

profile of v1, /device:TPU:1, one launch (start us, length us, event | category | flops | bytes accessed | tf_op | source)
XLA Modules:
  0.0 63.4 jit_solution(17480205689449972716)
XLA Ops:
  0.0 1.1 %copy_bitcast_fusion = (f32[1,4,64,128]{3,1,0,2:T(4,128)S(1)}, f32[1,4,64,128]{3,1,0,2:T(4,128)S(1)}) fusion(f32[4,64,128]{2,1,0:T(8,128)} %k_ref.5, f32[4,64,128]{2,1,0:T(8,128)} %t_ref.5), kind=kLoop, calls=%fused_computation.6 | loop fusion | bytes 524288 | tf_op jit(solution)/shard_map/stack | solution.py:257
  1.1 0.1 fusion.1
  1.3 3.3 %collective-permute-start.1 = (f32[2,64,128]{2,0,1:T(2,128)S(1)}, f32[2,64,128]{2,0,1:T(2,128)S(1)}, u32[]{:S(2)}, u32[]{:S(2)}) collective-permute-start(f32[2,64,128]{2,0,1:T(2,128)S(1)} %bitcast.14), channel_id=1, source_target_pairs={{0,63},{1,0},{2,1},{3,2},{4,3},{5,4},{6,5},{7,6},{8,7},{9,8},{10,9... | collective-permute-start | bytes 196616 | tf_op jit(solution)/shard_map/ppermute | solution.py:253
  4.6 0.0 collective-permute-start
  4.6 2.4 %collective-permute-start.3 = (f32[2,4,128]{2,1,0:T(4,128)S(1)}, f32[2,4,128]{2,1,0:T(4,128)S(1)}, u32[]{:S(2)}, u32[]{:S(2)}) collective-permute-start(f32[2,4,128]{2,1,0:T(4,128)S(1)} %get-tuple-element.25), channel_id=1, source_target_pairs={{0,192},{64,0},{128,64},{192,128},{1,193},{65,1},{129,65},{193,129... | collective-permute-start | bytes 12296 | tf_op jit(solution)/shard_map/ppermute | solution.py:253
  6.9 0.0 collective-permute-start.2
  6.9 0.0 copy-start
  6.9 0.9 %copy-done = f32[4,64,128]{2,1,0:T(8,128)S(1)} copy-done((f32[4,64,128]{2,1,0:T(8,128)S(1)}, f32[4,64,128]{2,1,0:T(8,128)}, u32[]{:S(2)}) %copy-start) | copy-done | bytes 131096
  7.8 0.0 copy-start.2
  7.8 0.9 %copy-done.2 = f32[4,64,128]{2,1,0:T(8,128)S(1)} copy-done((f32[4,64,128]{2,1,0:T(8,128)S(1)}, f32[4,64,128]{2,1,0:T(8,128)}, u32[]{:S(2)}) %copy-start.2) | copy-done | bytes 131096
  8.7 4.2 %inner.1 = (f32[15,4,64,128]{3,2,1,0:T(8,128)S(1)}, f32[4,64,128]{2,1,0:T(8,128)S(1)}, f32[3,64,128]{2,1,0:T(8,128)S(1)}) custom-call(f32[4,64,128]{2,1,0:T(8,128)S(1)} %copy-done, f32[4,64,128]{2,1,0:T(8,128)S(1)} %copy-done.2), custom_call_target="tpu_custom_call" | custom-call | flops 2000000 | bytes 2000000 | tf_op jit(solution)/shard_map/inner/pallas_call | solution.py:239
  13.0 0.0 collective-permute-done.1
  13.0 0.0 collective-permute-done
  13.0 0.0 collective-permute-done.3.zn_ref
  13.0 0.0 collective-permute-done.2.zp_ref
  13.0 0.0 copy-start.3
  13.0 0.9 %copy-done.3 = f32[4,64,128]{2,1,0:T(8,128)S(1)} copy-done((f32[4,64,128]{2,1,0:T(8,128)S(1)}, f32[4,64,128]{2,1,0:T(8,128)}, u32[]{:S(2)}) %copy-start.3) | copy-done | bytes 131096
  13.9 0.0 copy-start.4
  13.9 0.0 copy-start.1
  13.9 0.7 %first.1 = (f32[320,128]{1,0:T(8,128)S(1)}, f32[3,3,64,128]{3,2,1,0:T(8,128)S(1)}) custom-call(f32[4,64,128]{2,1,0:T(8,128)S(1)} %copy-done, f32[4,64,128]{2,1,0:T(8,128)S(1)} %copy-done.3, f32[15,4,64,128]{3,2,1,0:T(8,128)S(1)} %get-tuple-element.15.factors_ref, f32[4,64,128]{2,1,0:T(8,128)S(1)} %get-tuple-element.16.inner_ref, ...), custom_call_target="tpu_custom_call" | custom-call | flops 2000000 | bytes 2000000 | tf_op jit(solution)/shard_map/first/pallas_call | solution.py:239
  14.7 24.8 %all_to_all.22 = f32[64,5,128]{2,1,0:T(8,128)S(1)} all-to-all(f32[64,5,128]{2,1,0:T(8,128)S(1)} %all_to_all.14), channel_id=1, replica_groups=mesh['zg'=4,'gy'=64] {'gy'}, dimensions={0} | all-to-all | bytes 327680 | tf_op jit(solution)/shard_map/all_to_all | solution.py:268
  39.6 0.8 %column.1 = f32[128,128]{1,0:T(8,128)} custom-call(f32[320,128]{1,0:T(8,128)S(1)} %all_to_all.16.bundle_ref), custom_call_target="tpu_custom_call" | custom-call | flops 2000000 | bytes 2000000 | tf_op jit(solution)/shard_map/column/pallas_call | solution.py:239
  40.4 6.0 %all-to-all-start.1 = ((f32[64,2,128]{2,1,0:T(2,128)}), f32[64,2,128]{2,1,0:T(2,128)S(1)}, u32[]{:S(2)}, u32[]{:S(2)}) async-start(f32[64,2,128]{2,1,0:T(2,128)} %bitcast.6), calls=%async_computation.1 | async-start | bytes 131072 | tf_op jit(solution)/shard_map/all_to_all | solution.py:273
  46.4 0.0 copy-done.4
  46.4 0.8 %z.1 = (f32[13,4,64,128]{3,2,1,0:T(8,128)S(1)}, f32[2,4,64,128]{3,2,1,0:T(8,128)S(1)}, f32[3,4,128]{2,1,0:T(4,128)S(1)}) custom-call(f32[4,64,128]{2,1,0:T(8,128)S(1)} %copy-done.4, f32[2,4,128]{2,1,0:T(4,128)S(1)} %collective-permute-done.3.zn_ref), custom_call_target="tpu_custom_call" | custom-call | flops 2000000 | bytes 2000000 | tf_op jit(solution)/shard_map/z/pallas_call | solution.py:239
  47.2 0.3 collective-permute-start.4
  47.5 3.7 %collective-permute-start.5 = (f32[3,4,128]{2,1,0:T(4,128)S(1)}, f32[3,4,128]{2,1,0:T(4,128)S(1)}, u32[]{:S(2)}, u32[]{:S(2)}) collective-permute-start(f32[3,4,128]{2,1,0:T(4,128)S(1)} %get-tuple-element.23.c0_ref), channel_id=1, source_target_pairs={{0,128},{64,192},{128,0},{192,64},{1,129},{65,193},{129,1},{193,65... | collective-permute-start | bytes 18440 | tf_op jit(solution)/shard_map/ppermute | solution.py:253
  51.2 0.0 collective-permute-start.6
  51.2 5.0 %all-to-all-done.1 = f32[64,2,128]{2,1,0:T(2,128)S(1)} async-done(((f32[64,2,128]{2,1,0:T(2,128)}), f32[64,2,128]{2,1,0:T(2,128)S(1)}, u32[]{:S(2)}, u32[]{:S(2)}) %all-to-all-start.1) | async-done | bytes 65568 | tf_op jit(solution)/shard_map/all_to_all | solution.py:273
  56.3 0.3 collective-permute-start.7
  56.5 3.7 %collective-permute-start.8 = (f32[2,4,128]{2,1,0:T(4,128)S(1)}, f32[2,4,128]{2,1,0:T(4,128)S(1)}, u32[]{:S(2)}, u32[]{:S(2)}) collective-permute-start(f32[2,4,128]{2,1,0:T(4,128)S(1)} %get-tuple-element.24.s0_ref), channel_id=1, source_target_pairs={{0,128},{64,192},{128,0},{192,64},{1,129},{65,193},{129,1},{193,65... | collective-permute-start | bytes 12296 | tf_op jit(solution)/shard_map/ppermute | solution.py:253
  60.2 0.0 collective-permute-done.4.c1_ref
  60.2 0.0 collective-permute-start.9
  60.2 0.0 copy-done.1
  60.2 0.2 local_z.1.local_ref
  60.4 0.0 collective-permute-done.5.c2_ref
  60.4 0.0 collective-permute-done.6.c3_ref
  60.4 0.0 collective-permute-done.7.s1_ref
  60.4 0.8 %collective-permute-done.8.s2_ref = f32[2,4,128]{2,1,0:T(4,128)S(1)} collective-permute-done((f32[2,4,128]{2,1,0:T(4,128)S(1)}, f32[2,4,128]{2,1,0:T(4,128)S(1)}, u32[]{:S(2)}, u32[]{:S(2)}) %collective-permute-start.8) | collective-permute-done | bytes 4128 | tf_op jit(solution)/shard_map/ppermute | solution.py:253
  61.2 1.4 %collective-permute-done.9.s3_ref = f32[2,4,128]{2,1,0:T(4,128)S(1)} collective-permute-done((f32[2,4,128]{2,1,0:T(4,128)S(1)}, f32[2,4,128]{2,1,0:T(4,128)S(1)}, u32[]{:S(2)}, u32[]{:S(2)}) %collective-permute-start.9) | collective-permute-done | bytes 4128 | tf_op jit(solution)/shard_map/ppermute | solution.py:253
  62.7 0.7 %last.1 = f32[4,64,128]{2,1,0:T(8,128)} custom-call(f32[4,64,128]{2,1,0:T(8,128)S(1)} %local_z.1.local_ref, f32[2,4,64,128]{3,2,1,0:T(8,128)S(1)} %get-tuple-element.20.spikes_ref, f32[3,4,128]{2,1,0:T(4,128)S(1)} %get-tuple-element.23.c0_ref, f32[3,4,128]{2,1,0:T(4,128)S(1)} %collective-permute-done.4.c1_ref, ...), custom_call_target="tpu_custom_call" | custom-call | flops 2000000 | bytes 2000000 | tf_op jit(solution)/shard_map/last/pallas_call | solution.py:239
  (6 shorter events, 0.1 us)
Async XLA Ops:
  1.3 11.7 %collective-permute-start.1 = (f32[2,64,128]{2,0,1:T(2,128)S(1)}, f32[2,64,128]{2,0,1:T(2,128)S(1)}, u32[]{:S(2)}, u32[]{:S(2)}) collective-permute-start(f32[2,64,128]{2,0,1:T(2,128)S(1)} %bitcast.14), channel_id=1, source_target_pairs={{0,63},{1,0},{2,1},{3,2},{4,3},{5,4},{6,5},{7,6},{8,7},{9,8},{10,9... | collective-permute-start | bytes 196616 | tf_op jit(solution)/shard_map/ppermute | solution.py:253
  4.6 8.4 %collective-permute-start = (f32[2,64,128]{2,0,1:T(2,128)S(1)}, f32[2,64,128]{2,0,1:T(2,128)S(1)}, u32[]{:S(2)}, u32[]{:S(2)}) collective-permute-start(f32[2,64,128]{2,0,1:T(2,128)S(1)} %bitcast.13), channel_id=1, source_target_pairs={{0,1},{1,2},{2,3},{3,4},{4,5},{5,6},{6,7},{7,8},{8,9},{9,10},{10,1... | collective-permute-start | bytes 196616 | tf_op jit(solution)/shard_map/ppermute | solution.py:253
  4.6 8.4 %collective-permute-start.3 = (f32[2,4,128]{2,1,0:T(4,128)S(1)}, f32[2,4,128]{2,1,0:T(4,128)S(1)}, u32[]{:S(2)}, u32[]{:S(2)}) collective-permute-start(f32[2,4,128]{2,1,0:T(4,128)S(1)} %get-tuple-element.25), channel_id=1, source_target_pairs={{0,192},{64,0},{128,64},{192,128},{1,193},{65,1},{129,65},{193,129... | collective-permute-start | bytes 12296 | tf_op jit(solution)/shard_map/ppermute | solution.py:253
  6.9 6.1 %collective-permute-start.2 = (f32[2,4,128]{2,1,0:T(4,128)S(1)}, f32[2,4,128]{2,1,0:T(4,128)S(1)}, u32[]{:S(2)}, u32[]{:S(2)}) collective-permute-start(f32[2,4,128]{2,1,0:T(4,128)S(1)} %get-tuple-element.26), channel_id=1, source_target_pairs={{0,64},{64,128},{128,192},{192,0},{1,65},{65,129},{129,193},{193,1... | collective-permute-start | bytes 12296 | tf_op jit(solution)/shard_map/ppermute | solution.py:253
  6.9 0.9 %copy-start = (f32[4,64,128]{2,1,0:T(8,128)S(1)}, f32[4,64,128]{2,1,0:T(8,128)}, u32[]{:S(2)}) copy-start(f32[4,64,128]{2,1,0:T(8,128)} %t_ref.5) | copy-start | bytes 393220
  7.8 0.9 %copy-start.2 = (f32[4,64,128]{2,1,0:T(8,128)S(1)}, f32[4,64,128]{2,1,0:T(8,128)}, u32[]{:S(2)}) copy-start(f32[4,64,128]{2,1,0:T(8,128)} %k_ref.5) | copy-start | bytes 393220
  13.0 0.9 %copy-start.3 = (f32[4,64,128]{2,1,0:T(8,128)S(1)}, f32[4,64,128]{2,1,0:T(8,128)}, u32[]{:S(2)}) copy-start(f32[4,64,128]{2,1,0:T(8,128)} %k_ref.5) | copy-start | bytes 393220
  13.9 32.5 %copy-start.4 = (f32[4,64,128]{2,1,0:T(8,128)S(1)}, f32[4,64,128]{2,1,0:T(8,128)}, u32[]{:S(2)}) copy-start(f32[4,64,128]{2,1,0:T(8,128)} %k_ref.5) | copy-start | bytes 393220
  13.9 46.3 %copy-start.1 = (f32[4,64,128]{2,1,0:T(8,128)S(1)}, f32[4,64,128]{2,1,0:T(8,128)}, u32[]{:S(2)}) copy-start(f32[4,64,128]{2,1,0:T(8,128)} %t_ref.5) | copy-start | bytes 393220
  40.4 15.8 %all-to-all-start.1 = ((f32[64,2,128]{2,1,0:T(2,128)}), f32[64,2,128]{2,1,0:T(2,128)S(1)}, u32[]{:S(2)}, u32[]{:S(2)}) async-start(f32[64,2,128]{2,1,0:T(2,128)} %bitcast.6), calls=%async_computation.1 | async-start | bytes 131072 | tf_op jit(solution)/shard_map/all_to_all | solution.py:273
  47.2 13.0 %collective-permute-start.4 = (f32[3,4,128]{2,1,0:T(4,128)S(1)}, f32[3,4,128]{2,1,0:T(4,128)S(1)}, u32[]{:S(2)}, u32[]{:S(2)}) collective-permute-start(f32[3,4,128]{2,1,0:T(4,128)S(1)} %get-tuple-element.23.c0_ref), channel_id=1, source_target_pairs={{0,64},{64,128},{128,192},{192,0},{1,65},{65,129},{129,193},{193,1... | collective-permute-start | bytes 18440 | tf_op jit(solution)/shard_map/ppermute | solution.py:253
  47.5 12.9 %collective-permute-start.5 = (f32[3,4,128]{2,1,0:T(4,128)S(1)}, f32[3,4,128]{2,1,0:T(4,128)S(1)}, u32[]{:S(2)}, u32[]{:S(2)}) collective-permute-start(f32[3,4,128]{2,1,0:T(4,128)S(1)} %get-tuple-element.23.c0_ref), channel_id=1, source_target_pairs={{0,128},{64,192},{128,0},{192,64},{1,129},{65,193},{129,1},{193,65... | collective-permute-start | bytes 18440 | tf_op jit(solution)/shard_map/ppermute | solution.py:253
  51.2 9.2 %collective-permute-start.6 = (f32[3,4,128]{2,1,0:T(4,128)S(1)}, f32[3,4,128]{2,1,0:T(4,128)S(1)}, u32[]{:S(2)}, u32[]{:S(2)}) collective-permute-start(f32[3,4,128]{2,1,0:T(4,128)S(1)} %get-tuple-element.23.c0_ref), channel_id=1, source_target_pairs={{0,192},{64,0},{128,64},{192,128},{1,193},{65,1},{129,65},{193,129... | collective-permute-start | bytes 18440 | tf_op jit(solution)/shard_map/ppermute | solution.py:253
  56.3 4.1 %collective-permute-start.7 = (f32[2,4,128]{2,1,0:T(4,128)S(1)}, f32[2,4,128]{2,1,0:T(4,128)S(1)}, u32[]{:S(2)}, u32[]{:S(2)}) collective-permute-start(f32[2,4,128]{2,1,0:T(4,128)S(1)} %get-tuple-element.24.s0_ref), channel_id=1, source_target_pairs={{0,64},{64,128},{128,192},{192,0},{1,65},{65,129},{129,193},{193,1... | collective-permute-start | bytes 12296 | tf_op jit(solution)/shard_map/ppermute | solution.py:253
  56.5 4.7 %collective-permute-start.8 = (f32[2,4,128]{2,1,0:T(4,128)S(1)}, f32[2,4,128]{2,1,0:T(4,128)S(1)}, u32[]{:S(2)}, u32[]{:S(2)}) collective-permute-start(f32[2,4,128]{2,1,0:T(4,128)S(1)} %get-tuple-element.24.s0_ref), channel_id=1, source_target_pairs={{0,128},{64,192},{128,0},{192,64},{1,129},{65,193},{129,1},{193,65... | collective-permute-start | bytes 12296 | tf_op jit(solution)/shard_map/ppermute | solution.py:253
  60.2 2.5 %collective-permute-start.9 = (f32[2,4,128]{2,1,0:T(4,128)S(1)}, f32[2,4,128]{2,1,0:T(4,128)S(1)}, u32[]{:S(2)}, u32[]{:S(2)}) collective-permute-start(f32[2,4,128]{2,1,0:T(4,128)S(1)} %get-tuple-element.24.s0_ref), channel_id=1, source_target_pairs={{0,192},{64,0},{128,64},{192,128},{1,193},{65,1},{129,65},{193,129... | collective-permute-start | bytes 12296 | tf_op jit(solution)/shard_map/ppermute | solution.py:253

commit v2 on v1

--- a/solution.py
+++ b/solution.py
@@ -45,6 +45,23 @@
     return b * get(2 * len(strides))
 
 
+def load_kernel(t_hbm, k_hbm, t_ref, k_ref, yp_ref, yn_ref, zp_ref, zn_ref, sems):
+    copies = [pltpu.make_async_copy(t_hbm, t_ref, sems.at[0]), pltpu.make_async_copy(k_hbm, k_ref, sems.at[1])]
+    for copy in copies:
+        copy.start()
+    for j, (copy, ref) in enumerate(zip(copies, (t_ref, k_ref))):
+        copy.wait()
+        yp_ref[j] = ref[NB - 1]
+        yn_ref[j] = ref[0]
+        for y in range(NB):
+            zp_ref[j, y:y + 1] = ref[y, NZB - 1:]
+            zn_ref[j, y:y + 1] = ref[y, :1]
+
+
+def pair(ref, h):
+    return ref[2 * h:2 * h + 2].reshape(2 * NZB, NX).T
+
+
 def inner_kernel(t_ref, k_ref, factors_ref, inner_ref, faces_ref):
     lane = rows_of((NZB, NX), 1)
     row = rows_of((NZB, NX), 0)
@@ -53,7 +70,6 @@
         k = k_ref[y]
         t = t_ref[y]
         low = jnp.where(lane > 0, face(k, shift(k, 1, 1)), 0.0)
-        high = shift(low, -1, 1)
         flux = low * (t - shift(t, 1, 1))
         total = shift(flux, -1, 1) - flux
         face_z = jnp.where(row > 0, face(k, shift(k, 1, 0)), 0.0)
@@ -67,18 +83,14 @@
             flux_y = next_face * (t_ref[y + 1] - t)
             total = total + flux_y
         inner_ref[y] = total
-    half = NZB // 2
-    for y in range(NB):
-        for part in range(2):
-            at = pl.ds(part * half, half)
-            k = k_ref[y, at, :]
-            low = jnp.where(rows_of((half, NX), 1) > 0, face(k, shift(k, 1, 1)), 0.0)
-            high = shift(low, -1, 1)
-
-            def put(j, v):
-                factors_ref[j, y, at, :] = v
-
-            reduction_factors(jnp.ones_like(k), low, high, X_STRIDES, 1, put)
+    for h in range(NB // 2):
+        k = pair(k_ref, h)
+        low = jnp.where(rows_of(k.shape, 0) > 0, face(k, shift(k, 1, 0)), 0.0)
+
+        def put(j, v):
+            factors_ref[j, h] = v
+
+        reduction_factors(jnp.ones_like(k), low, shift(low, -1, 0), X_STRIDES, 0, put)
 
 
 def first_kernel(t_ref, k_ref, factors_ref, inner_ref, faces_ref, yp_ref, yn_ref, zp_ref, zn_ref,
@@ -90,7 +102,7 @@
     has_below = jnp.where(zg > 0, 1.0, 0.0)
     has_above = jnp.where(zg < NZG - 1, 1.0, 0.0)
     row = rows_of((NZB, NX), 0)
-    solved = []
+    sources = []
     g4 = None
     for y in range(NB):
         b = inner_ref[y]
@@ -104,7 +116,12 @@
         below = face(k[:1], zp_ref[1, y:y + 1] * has_below) * (zp_ref[0, y:y + 1] - t[:1])
         above = face(k[NZB - 1:], zn_ref[1, y:y + 1] * has_above) * (zn_ref[0, y:y + 1] - t[NZB - 1:])
         b = b + jnp.where(row == 0, below, 0.0) + jnp.where(row == NZB - 1, above, 0.0)
-        solved.append(reduced_source(b, X_STRIDES, 1, lambda j: factors_ref[j, y]))
+        sources.append(b)
+    solved = []
+    for h in range(NB // 2):
+        b = jnp.concatenate(sources[2 * h:2 * h + 2], axis=0).T
+        b = reduced_source(b, X_STRIDES, 0, lambda j: factors_ref[j, h]).T
+        solved += [b[:NZB], b[NZB:]]
     b0, b1, b2, b3 = solved
     g1, g2, g3 = faces_ref[0], faces_ref[1], faces_ref[2]
     i1 = 1.0 / (1.0 + g1 + g2)
@@ -184,17 +201,18 @@
         coeffs_ref[2, y:y + 1] = lam[NZB - 1:] * top
 
 
-def second_kernel(ends_ref, back_ref, spikes_ref, second_ref, sums_ref):
+def second_kernel(ends_ref, back_ref, spikes_ref, coeffs_ref, second_ref, sums_ref):
     own = ends_ref[pl.ds(0, NZB, stride=2), :]
     following = ends_ref[pl.ds(1, NZB, stride=2), :]
+    sums_ref[:3] = coeffs_ref[...]
     for y in range(NB):
         if y == 0:
             u = own
         else:
             u = back_ref[0, y - 1] + back_ref[1, y - 1] * own + back_ref[2, y - 1] * following
         second_ref[y] = u
-        sums_ref[0, y:y + 1] = jnp.sum(spikes_ref[0, y] * u, axis=0, keepdims=True)
-        sums_ref[1, y:y + 1] = jnp.sum(spikes_ref[1, y] * u, axis=0, keepdims=True)
+        sums_ref[3, y:y + 1] = jnp.sum(spikes_ref[0, y] * u, axis=0, keepdims=True)
+        sums_ref[4, y:y + 1] = jnp.sum(spikes_ref[1, y] * u, axis=0, keepdims=True)
 
 
 def local_z_kernel(second_ref, factors_ref, t_ref, out_ref):
@@ -204,47 +222,44 @@
         out_ref[y] = t_ref[y] + reduced_source(b, Z_STRIDES, 0, lambda j: factors_ref[j, y])
 
 
-def last_kernel(local_ref, spikes_ref, c0_ref, c1_ref, c2_ref, c3_ref, s0_ref, s1_ref, s2_ref, s3_ref,
-                out_ref, coeffs, sums, ends):
+def last_kernel(local_ref, spikes_ref, e0_ref, e1_ref, e2_ref, e3_ref, out_ref, line, ends):
     zg = lax.axis_index("zg")
-    for j, (c_ref, s_ref) in enumerate(((c0_ref, s0_ref), (c1_ref, s1_ref), (c2_ref, s2_ref), (c3_ref, s3_ref))):
-        at = lax.rem(zg + (NZG - j), NZG)
-        coeffs[at] = c_ref[...]
-        sums[at] = s_ref[...]
+    for j, e_ref in enumerate((e0_ref, e1_ref, e2_ref, e3_ref)):
+        line[lax.rem(zg + (NZG - j), NZG)] = e_ref[...]
     inverses, sources = [], []
-    leak, source = coeffs[0, 0], sums[0, 0]
+    leak, source = line[0, 0], line[0, 3]
     for d in range(NZG):
-        couple = coeffs[d, 2]
+        couple = line[d, 2]
         inverse = 1.0 / (leak + couple)
         inverses.append(inverse)
         sources.append(source)
         if d + 1 < NZG:
             passed = couple * inverse
-            leak = coeffs[d + 1, 0] + coeffs[d, 1] + passed * leak
-            source = sums[d + 1, 0] + sums[d, 1] + passed * source
+            leak = line[d + 1, 0] + line[d, 1] + passed * leak
+            source = line[d + 1, 3] + line[d, 4] + passed * source
     value = jnp.zeros_like(source)
     ends[NZG] = value
     for d in reversed(range(NZG)):
-        value = (sources[d] + coeffs[d, 2] * value) * inverses[d]
+        value = (sources[d] + line[d, 2] * value) * inverses[d]
         ends[d] = value
     own = ends[zg]
     following = ends[zg + 1]
     for y in range(NB):
-        out_ref[y] = (local_ref[y] + spikes_ref[0, y] * own[y:y + 1] + spikes_ref[1, y] * following[y:y + 1])
-
-
-def call(kernel, name, outs, args, scratch=(), cost=2000000):
+        out_ref[y] = local_ref[y] + spikes_ref[0, y] * own[y:y + 1] + spikes_ref[1, y] * following[y:y + 1]
+
+
+def call(kernel, name, outs, args, scratch=(), cost=2000000, whole=False):
     shapes = [jax.ShapeDtypeStruct(o, jnp.float32) for o in outs]
     vmem = pl.BlockSpec(memory_space=pltpu.VMEM)
     return pl.pallas_call(
         kernel,
         name=name,
         out_shape=shapes,
-        in_specs=[vmem] * len(args),
+        in_specs=[pl.BlockSpec(memory_space=pltpu.HBM)] * len(args) if whole else [vmem] * len(args),
         out_specs=[vmem] * len(outs),
-        scratch_shapes=[pltpu.VMEM(s, jnp.float32) for s in scratch],
+        scratch_shapes=scratch,
         cost_estimate=pl.CostEstimate(flops=cost, bytes_accessed=cost, transcendentals=0),
-        compiler_params=pltpu.CompilerParams(vmem_limit_bytes=24 * 1024 * 1024),
+        compiler_params=pltpu.CompilerParams(vmem_limit_bytes=(54816 if whole else 24576) * 1024),
     )(*args)
 
 
@@ -254,28 +269,30 @@
 
 
 def shards(t, k):
-    joined = jnp.stack([t, k])
-    yp = around(joined[:, NB - 1], "gy", 1)
-    yn = around(joined[:, 0], "gy", -1)
-    zp = around(joined[:, :, NZB - 1], "zg", 1)
-    zn = around(joined[:, :, 0], "zg", -1)
     block = (NB, NZB, NX)
+    t, k, yp, yn, zp, zn = call(
+        load_kernel, "load", [block, block, (2, NZB, NX), (2, NZB, NX), (2, NB, NX), (2, NB, NX)], [t, k],
+        scratch=[pltpu.SemaphoreType.DMA((2,))], whole=True)
+    yp = around(yp, "gy", 1)
+    yn = around(yn, "gy", -1)
+    zp = around(zp, "zg", 1)
+    zn = around(zn, "zg", -1)
     factors, inner, faces = call(
-        inner_kernel, "inner", [(2 * len(X_STRIDES) + 1,) + block, block, (NB - 1, NZB, NX)], [t, k])
+        inner_kernel, "inner",
+        [(2 * len(X_STRIDES) + 1, NB // 2, NX, 2 * NZB), block, (NB - 1, NZB, NX)], [t, k])
     bundle, back = call(
         first_kernel, "first", [(NZB * VALUES, NX), (3, NB - 1, NZB, NX)],
         [t, k, factors, inner, faces, yp, yn, zp, zn])
-    columns = lax.all_to_all(bundle, "gy", split_axis=0, concat_axis=0, tiled=True)
+    columns = lax.all_to_all(bundle.reshape(NZB * VALUES, 1, NX), "gy", split_axis=0, concat_axis=0, tiled=True)
     z_factors, spikes, coeffs = call(
         z_kernel, "z", [(2 * len(Z_STRIDES) + 1,) + block, (2,) + block, (3, NB, NX)], [k, zn])
-    coeffs = [coeffs] + [around(coeffs, "zg", j) for j in range(1, NZG)]
-    (ends,) = call(column_kernel, "column", [(2 * NGY, NX)], [columns])
+    (ends,) = call(column_kernel, "column", [(2 * NGY, NX)], [columns.reshape(NGY * VALUES, NX)])
     ends = lax.all_to_all(ends, "gy", split_axis=0, concat_axis=0, tiled=True)
-    second, sums = call(second_kernel, "second", [block, (2, NB, NX)], [ends, back, spikes])
+    second, sums = call(second_kernel, "second", [block, (5, NB, NX)], [ends, back, spikes, coeffs])
     sums = [sums] + [around(sums, "zg", j) for j in range(1, NZG)]
     (local,) = call(local_z_kernel, "local_z", [block], [second, z_factors, t])
-    (out,) = call(last_kernel, "last", [block], [local, spikes] + coeffs + sums,
-                  scratch=((NZG, 3, NB, NX), (NZG, 2, NB, NX), (NZG + 1, NB, NX)))
+    (out,) = call(last_kernel, "last", [block], [local, spikes] + sums,
+                  scratch=[pltpu.VMEM((NZG, 5, NB, NX), jnp.float32), pltpu.VMEM((NZG + 1, NB, NX), jnp.float32)])
     return out
 
 

time: 63.6 us -> 57.7 us (0.907)
  waiting for transfers between devices: 7.32 us -> 13.7 us
  starting transfers between devices: 19.6 us -> 13.7 us
  local copies, waits for them, and re-layouts: 3.92 us -> 0 us
  Pallas kernels: 7.49 us -> 4.74 us
    ppermute x10 -> x7, starting transfers between devices: 13.5 us -> 8.34 us  [around(): return lax.ppermute(x, axis, [(i, (i + by) % count) for i in range(count)])]
    all_to_all x1, waiting for transfers between devices: 5.04 us -> 8.99 us  [shards(): ends = lax.all_to_all(ends, 'gy', split_axis=0, concat_axis=0, tiled=True)]
    pallas_call x7 -> x8, Pallas kernels: 7.49 us -> 4.74 us  [call(): pl.pallas_call(kernel, name=name, out_shape=shapes, in_specs=[pl.BlockSpe...]
    unnamed x10 -> x0, local copies, waits for them, and re-layouts: 2.71 us -> none
    ppermute x10 -> x7, waiting for transfers between devices: 2.27 us -> 4.7 us  [around(): return lax.ppermute(x, axis, [(i, (i + by) % count) for i in range(count)])]
    another operation x1 -> x0, local copies, waits for them, and re-layouts: 1.14 us -> none  [shards(): joined = jnp.stack([t, k])]
    all_to_all x1, starting transfers between devices: 6.03 us -> 5.35 us  [shards(): ends = lax.all_to_all(ends, 'gy', split_axis=0, concat_axis=0, tiled=True)]
  transfers between devices with their start and end apart: 11 -> 8, of which waited for: 3 -> 5; matrix products, arithmetic and copies ran while one was open for 0% -> 0% of each run, Pallas kernels for 8% -> 3%
where the time goes in v2:
time: 57.7 us; the launch traced here: 57.1 us
  blocking collectives  24.9 us (43%)
  starting transfers between devices  13.7 us (24%)
  waiting for transfers between devices  13.7 us (24%)
  Pallas kernels  4.74 us (8%)
    all_to_all x1, blocking collectives, shards(): lax.all_to_all(bundle.reshape(NZB * VALUES, 1, NX), 'gy', split_axis=0, c...  24.9 us
    all_to_all x1, waiting for transfers between devices, shards(): ends = lax.all_to_all(ends, 'gy', split_axis=0, concat_axis=0, tiled=True)  8.99 us
    ppermute x7, starting transfers between devices, around(): return lax.ppermute(x, axis, [(i, (i + by) % count) for i in range(count)])  8.34 us
    all_to_all x1, starting transfers between devices, shards(): ends = lax.all_to_all(ends, 'gy', split_axis=0, concat_axis=0, tiled=True)  5.35 us
    pallas_call x8, Pallas kernels, call(): pl.pallas_call(kernel, name=name, out_shape=shapes, in_specs=[pl.BlockSpe...  4.74 us
    ppermute x7, waiting for transfers between devices, around(): return lax.ppermute(x, axis, [(i, (i + by) % count) for i in range(count)])  4.7 us
  transfers between devices with their start and end apart: 8, of which 5 were waited for; matrix products, arithmetic and copies ran while one was open for 0% of the time, Pallas kernels for 3%

profile of v2, /device:TPU:1, one launch (start us, length us, event | category | flops | bytes accessed | tf_op | source)
XLA Modules:
  0.0 57.1 jit_solution(2011192254583115652)
XLA Ops:
  0.0 1.0 %load.1 = (f32[4,64,128]{2,1,0:T(8,128)S(1)}, f32[4,64,128]{2,1,0:T(8,128)S(1)}, f32[2,64,128]{2,1,0:T(8,128)S(1)}, f32[2,64,128]{2,1,0:T(8,128)S(1)}, f32[2,4,1...) custom-call(f32[4,64,128]{2,1,0:T(8,128)} %t_hbm.1, f32[4,64,128]{2,1,0:T(8,128)} %k_hbm.1), custom_call_target="tpu_custom_call" | custom-call | flops 2000000 | bytes 2000000 | tf_op jit(solution)/shard_map/load/pallas_call | solution.py:254
  1.0 3.1 %collective-permute-start = (f32[2,64,128]{2,1,0:T(8,128)S(1)}, f32[2,64,128]{2,1,0:T(8,128)S(1)}, u32[]{:S(2)}, u32[]{:S(2)}) collective-permute-start(f32[2,64,128]{2,1,0:T(8,128)S(1)} %get-tuple-element.26), channel_id=1, source_target_pairs={{0,1},{1,2},{2,3},{3,4},{4,5},{5,6},{6,7},{7,8},{8,9},{9,10},{10,1... | collective-permute-start | bytes 196616 | tf_op jit(solution)/shard_map/ppermute | solution.py:268
  4.1 0.3 collective-permute-start.1
  4.4 2.2 %collective-permute-start.3 = (f32[2,4,128]{2,1,0:T(4,128)S(1)}, f32[2,4,128]{2,1,0:T(4,128)S(1)}, u32[]{:S(2)}, u32[]{:S(2)}) collective-permute-start(f32[2,4,128]{2,1,0:T(4,128)S(1)} %get-tuple-element.29), channel_id=1, source_target_pairs={{0,192},{64,0},{128,64},{192,128},{1,193},{65,1},{129,65},{193,129... | collective-permute-start | bytes 12296 | tf_op jit(solution)/shard_map/ppermute | solution.py:268
  6.6 0.0 collective-permute-start.2
  6.6 0.8 %inner.1 = (f32[15,2,128,128]{3,2,1,0:T(8,128)S(1)}, f32[4,64,128]{2,1,0:T(8,128)S(1)}, f32[3,64,128]{2,1,0:T(8,128)S(1)}) custom-call(f32[4,64,128]{2,1,0:T(8,128)S(1)} %get-tuple-element.21.t_ref, f32[4,64,128]{2,1,0:T(8,128)S(1)} %get-tuple-element.22.k_ref), custom_call_target="tpu_custom_call" | custom-call | flops 2000000 | bytes 2000000 | tf_op jit(solution)/shard_map/inner/pallas_call | solution.py:254
  7.4 0.0 collective-permute-done.3.zn_ref
  7.4 2.8 %collective-permute-done.2.zp_ref = f32[2,4,128]{2,1,0:T(4,128)S(1)} collective-permute-done((f32[2,4,128]{2,1,0:T(4,128)S(1)}, f32[2,4,128]{2,1,0:T(4,128)S(1)}, u32[]{:S(2)}, u32[]{:S(2)}) %collective-permute-start.2) | collective-permute-done | bytes 4128 | tf_op jit(solution)/shard_map/ppermute | solution.py:268
  10.3 0.0 collective-permute-done.yp_ref
  10.3 0.0 collective-permute-done.1.yn_ref
  10.3 0.4 first.1
  10.6 24.9 %all_to_all.16 = f32[320,1,128]{2,1,0:T(1,128)S(1)} all-to-all(f32[320,1,128]{2,1,0:T(1,128)S(1)} %bitcast.8), channel_id=1, replica_groups=mesh['zg'=4,'gy'=64] {'gy'}, dimensions={0} | all-to-all | bytes 327680 | tf_op jit(solution)/shard_map/all_to_all | solution.py:286
  35.5 0.8 %column.1 = f32[128,128]{1,0:T(8,128)} custom-call(f32[320,128]{1,0:T(8,128)S(1)} %bitcast.6), custom_call_target="tpu_custom_call" | custom-call | flops 2000000 | bytes 2000000 | tf_op jit(solution)/shard_map/column/pallas_call | solution.py:254
  36.3 5.3 %all-to-all-start.1 = ((f32[64,2,128]{2,1,0:T(2,128)}), f32[64,2,128]{2,1,0:T(2,128)S(1)}, u32[]{:S(2)}, u32[]{:S(2)}) async-start(f32[64,2,128]{2,1,0:T(2,128)} %bitcast.3), calls=%async_computation.1 | async-start | bytes 131072 | tf_op jit(solution)/shard_map/all_to_all | solution.py:290
  41.7 0.8 %z.1 = (f32[13,4,64,128]{3,2,1,0:T(8,128)S(1)}, f32[2,4,64,128]{3,2,1,0:T(8,128)S(1)}, f32[3,4,128]{2,1,0:T(4,128)S(1)}) custom-call(f32[4,64,128]{2,1,0:T(8,128)S(1)} %get-tuple-element.22.k_ref, f32[2,4,128]{2,1,0:T(4,128)S(1)} %collective-permute-done.3.zn_ref), custom_call_target="tpu_custom_call" | custom-call | flops 2000000 | bytes 2000000 | tf_op jit(solution)/shard_map/z/pallas_call | solution.py:254
  42.5 9.0 %all-to-all-done.1 = f32[64,2,128]{2,1,0:T(2,128)S(1)} async-done(((f32[64,2,128]{2,1,0:T(2,128)}), f32[64,2,128]{2,1,0:T(2,128)S(1)}, u32[]{:S(2)}, u32[]{:S(2)}) %all-to-all-start.1) | async-done | bytes 65568 | tf_op jit(solution)/shard_map/all_to_all | solution.py:290
  51.5 0.1 collective-permute-start.4
  51.6 0.9 %collective-permute-start.5 = (f32[5,4,128]{2,1,0:T(4,128)S(1)}, f32[5,4,128]{2,1,0:T(4,128)S(1)}, u32[]{:S(2)}, u32[]{:S(2)}) collective-permute-start(f32[5,4,128]{2,1,0:T(4,128)S(1)} %get-tuple-element.36.e0_ref), channel_id=1, source_target_pairs={{0,128},{64,192},{128,0},{192,64},{1,129},{65,193},{129,1},{193,65... | collective-permute-start | bytes 30728 | tf_op jit(solution)/shard_map/ppermute | solution.py:268
  52.5 1.8 %collective-permute-start.6 = (f32[5,4,128]{2,1,0:T(4,128)S(1)}, f32[5,4,128]{2,1,0:T(4,128)S(1)}, u32[]{:S(2)}, u32[]{:S(2)}) collective-permute-start(f32[5,4,128]{2,1,0:T(4,128)S(1)} %get-tuple-element.36.e0_ref), channel_id=1, source_target_pairs={{0,192},{64,0},{128,64},{192,128},{1,193},{65,1},{129,65},{193,129... | collective-permute-start | bytes 30728 | tf_op jit(solution)/shard_map/ppermute | solution.py:268
  54.3 0.2 local_z.1.local_ref
  54.5 0.9 %collective-permute-done.4.e1_ref = f32[5,4,128]{2,1,0:T(4,128)S(1)} collective-permute-done((f32[5,4,128]{2,1,0:T(4,128)S(1)}, f32[5,4,128]{2,1,0:T(4,128)S(1)}, u32[]{:S(2)}, u32[]{:S(2)}) %collective-permute-start.4) | collective-permute-done | bytes 10272 | tf_op jit(solution)/shard_map/ppermute | solution.py:268
  55.3 0.4 collective-permute-done.5.e2_ref
  55.7 0.6 %collective-permute-done.6.e3_ref = f32[5,4,128]{2,1,0:T(4,128)S(1)} collective-permute-done((f32[5,4,128]{2,1,0:T(4,128)S(1)}, f32[5,4,128]{2,1,0:T(4,128)S(1)}, u32[]{:S(2)}, u32[]{:S(2)}) %collective-permute-start.6) | collective-permute-done | bytes 10272 | tf_op jit(solution)/shard_map/ppermute | solution.py:268
  56.3 0.7 %last.1 = f32[4,64,128]{2,1,0:T(8,128)} custom-call(f32[4,64,128]{2,1,0:T(8,128)S(1)} %local_z.1.local_ref, f32[2,4,64,128]{3,2,1,0:T(8,128)S(1)} %get-tuple-element.32.spikes_ref, f32[5,4,128]{2,1,0:T(4,128)S(1)} %get-tuple-element.36.e0_ref, f32[5,4,128]{2,1,0:T(4,128)S(1)} %collective-permute-done.4.e1_ref, ...), custom_call_target="tpu_custom_call" | custom-call | flops 2000000 | bytes 2000000 | tf_op jit(solution)/shard_map/last/pallas_call | solution.py:254
  (1 shorter events, 0.0 us)
Async XLA Ops:
  1.0 9.3 %collective-permute-start = (f32[2,64,128]{2,1,0:T(8,128)S(1)}, f32[2,64,128]{2,1,0:T(8,128)S(1)}, u32[]{:S(2)}, u32[]{:S(2)}) collective-permute-start(f32[2,64,128]{2,1,0:T(8,128)S(1)} %get-tuple-element.26), channel_id=1, source_target_pairs={{0,1},{1,2},{2,3},{3,4},{4,5},{5,6},{6,7},{7,8},{8,9},{9,10},{10,1... | collective-permute-start | bytes 196616 | tf_op jit(solution)/shard_map/ppermute | solution.py:268
  4.1 6.2 %collective-permute-start.1 = (f32[2,64,128]{2,1,0:T(8,128)S(1)}, f32[2,64,128]{2,1,0:T(8,128)S(1)}, u32[]{:S(2)}, u32[]{:S(2)}) collective-permute-start(f32[2,64,128]{2,1,0:T(8,128)S(1)} %get-tuple-element.27), channel_id=1, source_target_pairs={{0,63},{1,0},{2,1},{3,2},{4,3},{5,4},{6,5},{7,6},{8,7},{9,8},{10,9... | collective-permute-start | bytes 196616 | tf_op jit(solution)/shard_map/ppermute | solution.py:268
  4.4 3.0 %collective-permute-start.3 = (f32[2,4,128]{2,1,0:T(4,128)S(1)}, f32[2,4,128]{2,1,0:T(4,128)S(1)}, u32[]{:S(2)}, u32[]{:S(2)}) collective-permute-start(f32[2,4,128]{2,1,0:T(4,128)S(1)} %get-tuple-element.29), channel_id=1, source_target_pairs={{0,192},{64,0},{128,64},{192,128},{1,193},{65,1},{129,65},{193,129... | collective-permute-start | bytes 12296 | tf_op jit(solution)/shard_map/ppermute | solution.py:268
  6.6 3.7 %collective-permute-start.2 = (f32[2,4,128]{2,1,0:T(4,128)S(1)}, f32[2,4,128]{2,1,0:T(4,128)S(1)}, u32[]{:S(2)}, u32[]{:S(2)}) collective-permute-start(f32[2,4,128]{2,1,0:T(4,128)S(1)} %get-tuple-element.28), channel_id=1, source_target_pairs={{0,64},{64,128},{128,192},{192,0},{1,65},{65,129},{129,193},{193,1... | collective-permute-start | bytes 12296 | tf_op jit(solution)/shard_map/ppermute | solution.py:268
  36.3 15.1 %all-to-all-start.1 = ((f32[64,2,128]{2,1,0:T(2,128)}), f32[64,2,128]{2,1,0:T(2,128)S(1)}, u32[]{:S(2)}, u32[]{:S(2)}) async-start(f32[64,2,128]{2,1,0:T(2,128)} %bitcast.3), calls=%async_computation.1 | async-start | bytes 131072 | tf_op jit(solution)/shard_map/all_to_all | solution.py:290
  51.5 3.8 %collective-permute-start.4 = (f32[5,4,128]{2,1,0:T(4,128)S(1)}, f32[5,4,128]{2,1,0:T(4,128)S(1)}, u32[]{:S(2)}, u32[]{:S(2)}) collective-permute-start(f32[5,4,128]{2,1,0:T(4,128)S(1)} %get-tuple-element.36.e0_ref), channel_id=1, source_target_pairs={{0,64},{64,128},{128,192},{192,0},{1,65},{65,129},{129,193},{193,1... | collective-permute-start | bytes 30728 | tf_op jit(solution)/shard_map/ppermute | solution.py:268
  51.6 4.1 %collective-permute-start.5 = (f32[5,4,128]{2,1,0:T(4,128)S(1)}, f32[5,4,128]{2,1,0:T(4,128)S(1)}, u32[]{:S(2)}, u32[]{:S(2)}) collective-permute-start(f32[5,4,128]{2,1,0:T(4,128)S(1)} %get-tuple-element.36.e0_ref), channel_id=1, source_target_pairs={{0,128},{64,192},{128,0},{192,64},{1,129},{65,193},{129,1},{193,65... | collective-permute-start | bytes 30728 | tf_op jit(solution)/shard_map/ppermute | solution.py:268
  52.5 3.8 %collective-permute-start.6 = (f32[5,4,128]{2,1,0:T(4,128)S(1)}, f32[5,4,128]{2,1,0:T(4,128)S(1)}, u32[]{:S(2)}, u32[]{:S(2)}) collective-permute-start(f32[5,4,128]{2,1,0:T(4,128)S(1)} %get-tuple-element.36.e0_ref), channel_id=1, source_target_pairs={{0,192},{64,0},{128,64},{192,128},{1,193},{65,1},{129,65},{193,129... | collective-permute-start | bytes 30728 | tf_op jit(solution)/shard_map/ppermute | solution.py:268

commit v3 on v2

--- a/solution.py
+++ b/solution.py
@@ -62,7 +62,32 @@
     return ref[2 * h:2 * h + 2].reshape(2 * NZB, NX).T
 
 
-def inner_kernel(t_ref, k_ref, factors_ref, inner_ref, faces_ref):
+def z_part(k_ref, factors_ref, spikes_ref, coeffs_ref):
+    row = rows_of((NZB, NX), 0)
+    for y in range(NB):
+        k = k_ref[y]
+        g = face(k, shift(k, 1, 0))
+        low = jnp.where((row > 1) & (row < NZB - 1), g, 0.0)
+        at_first = jnp.where(row == 1, g, 0.0)
+        at_last = jnp.where(row == NZB - 2, shift(g, -1, 0), 0.0)
+
+        def put(j, v):
+            factors_ref[j, y] = v
+
+        reduction_factors(1.0 + at_first + at_last, low, shift(low, -1, 0), Z_STRIDES, 0, put)
+        get = lambda j: factors_ref[j, y]
+        lam = reduced_source(at_first, Z_STRIDES, 0, get)
+        rho = reduced_source(at_last, Z_STRIDES, 0, get)
+        coeffs_ref[2, y:y + 1] = g[NZB - 1:] * lam[NZB - 2:NZB - 1]
+        lam = jnp.where(row == 0, 1.0, lam)
+        rho = jnp.where(row == NZB - 1, 1.0, rho)
+        spikes_ref[0, y] = lam
+        spikes_ref[1, y] = rho
+        coeffs_ref[0, y:y + 1] = jnp.sum(lam, axis=0, keepdims=True)
+        coeffs_ref[1, y:y + 1] = jnp.sum(rho, axis=0, keepdims=True)
+
+
+def inner_kernel(t_ref, k_ref, factors_ref, inner_ref, faces_ref, z_factors_ref, spikes_ref, coeffs_ref):
     lane = rows_of((NZB, NX), 1)
     row = rows_of((NZB, NX), 0)
     flux_y = None
@@ -91,10 +116,11 @@
             factors_ref[j, h] = v
 
         reduction_factors(jnp.ones_like(k), low, shift(low, -1, 0), X_STRIDES, 0, put)
+    z_part(k_ref, z_factors_ref, spikes_ref, coeffs_ref)
 
 
 def first_kernel(t_ref, k_ref, factors_ref, inner_ref, faces_ref, yp_ref, yn_ref, zp_ref, zn_ref,
-                 bundle_ref, back_ref):
+                 bundle_ref, back_ref, top_ref):
     gy = lax.axis_index("gy")
     zg = lax.axis_index("zg")
     has_south = jnp.where(gy > 0, 1.0, 0.0)
@@ -114,7 +140,9 @@
             g4 = face(k, yn_ref[1] * has_north)
             b = b + g4 * (yn_ref[0] - t)
         below = face(k[:1], zp_ref[1, y:y + 1] * has_below) * (zp_ref[0, y:y + 1] - t[:1])
-        above = face(k[NZB - 1:], zn_ref[1, y:y + 1] * has_above) * (zn_ref[0, y:y + 1] - t[NZB - 1:])
+        top = face(k[NZB - 1:], zn_ref[1, y:y + 1] * has_above)
+        top_ref[y:y + 1] = top
+        above = top * (zn_ref[0, y:y + 1] - t[NZB - 1:])
         b = b + jnp.where(row == 0, below, 0.0) + jnp.where(row == NZB - 1, above, 0.0)
         sources.append(b)
     solved = []
@@ -173,56 +201,40 @@
     out_ref[pl.ds(1, NGY, stride=2), :] = shift(own, -1, 0)
 
 
-def z_kernel(k_ref, zn_ref, factors_ref, spikes_ref, coeffs_ref):
-    zg = lax.axis_index("zg")
-    has_above = jnp.where(zg < NZG - 1, 1.0, 0.0)
-    row = rows_of((NZB, NX), 0)
-    for y in range(NB):
-        k = k_ref[y]
-        g = face(k, shift(k, 1, 0))
-        top = face(k[NZB - 1:], zn_ref[1, y:y + 1] * has_above)
-        low = jnp.where(row > 1, g, 0.0)
-        high = shift(low, -1, 0)
-        at_first = jnp.where(row == 1, g, 0.0)
-        at_last = jnp.where(row == NZB - 1, top, 0.0)
-
-        def put(j, v):
-            factors_ref[j, y] = v
-
-        reduction_factors(1.0 + at_first + at_last, low, high, Z_STRIDES, 0, put)
-        get = lambda j: factors_ref[j, y]
-        lam = reduced_source(at_first, Z_STRIDES, 0, get)
-        lam = jnp.where(row == 0, 1.0, lam)
-        rho = reduced_source(at_last, Z_STRIDES, 0, get)
-        spikes_ref[0, y] = lam
-        spikes_ref[1, y] = rho
-        coeffs_ref[0, y:y + 1] = jnp.sum(lam, axis=0, keepdims=True)
-        coeffs_ref[1, y:y + 1] = jnp.sum(rho, axis=0, keepdims=True)
-        coeffs_ref[2, y:y + 1] = lam[NZB - 1:] * top
-
-
-def second_kernel(ends_ref, back_ref, spikes_ref, coeffs_ref, second_ref, sums_ref):
+def second_kernel(ends_ref, back_ref, spikes_ref, coeffs_ref, top_ref, second_ref, sums_ref, last_row_ref):
     own = ends_ref[pl.ds(0, NZB, stride=2), :]
     following = ends_ref[pl.ds(1, NZB, stride=2), :]
-    sums_ref[:3] = coeffs_ref[...]
+    firsts, lasts = [], []
     for y in range(NB):
         if y == 0:
             u = own
         else:
             u = back_ref[0, y - 1] + back_ref[1, y - 1] * own + back_ref[2, y - 1] * following
         second_ref[y] = u
-        sums_ref[3, y:y + 1] = jnp.sum(spikes_ref[0, y] * u, axis=0, keepdims=True)
-        sums_ref[4, y:y + 1] = jnp.sum(spikes_ref[1, y] * u, axis=0, keepdims=True)
+        firsts.append(jnp.sum(spikes_ref[0, y] * u, axis=0, keepdims=True))
+        lasts.append(jnp.sum(spikes_ref[1, y] * u, axis=0, keepdims=True))
+    first, last = jnp.concatenate(firsts, axis=0), jnp.concatenate(lasts, axis=0)
+    leak, couple, top = coeffs_ref[1], coeffs_ref[2], top_ref[...]
+    inverse = 1.0 / (leak + couple + top)
+    left, right = couple * inverse, top * inverse
+    sums_ref[0] = coeffs_ref[0] + left * leak
+    sums_ref[1] = right * leak
+    sums_ref[2] = left * top
+    sums_ref[3] = first + left * last
+    sums_ref[4] = right * last
+    last_row_ref[0] = last * inverse
+    last_row_ref[1] = left
+    last_row_ref[2] = right
 
 
 def local_z_kernel(second_ref, factors_ref, t_ref, out_ref):
     row = rows_of((NZB, NX), 0)
     for y in range(NB):
-        b = jnp.where(row == 0, 0.0, second_ref[y])
+        b = jnp.where((row == 0) | (row == NZB - 1), 0.0, second_ref[y])
         out_ref[y] = t_ref[y] + reduced_source(b, Z_STRIDES, 0, lambda j: factors_ref[j, y])
 
 
-def last_kernel(local_ref, spikes_ref, e0_ref, e1_ref, e2_ref, e3_ref, out_ref, line, ends):
+def last_kernel(local_ref, spikes_ref, last_row_ref, e0_ref, e1_ref, e2_ref, e3_ref, out_ref, line, ends):
     zg = lax.axis_index("zg")
     for j, e_ref in enumerate((e0_ref, e1_ref, e2_ref, e3_ref)):
         line[lax.rem(zg + (NZG - j), NZG)] = e_ref[...]
@@ -243,7 +255,7 @@
         value = (sources[d] + line[d, 2] * value) * inverses[d]
         ends[d] = value
     own = ends[zg]
-    following = ends[zg + 1]
+    following = last_row_ref[0] + last_row_ref[1] * own + last_row_ref[2] * ends[zg + 1]
     for y in range(NB):
         out_ref[y] = local_ref[y] + spikes_ref[0, y] * own[y:y + 1] + spikes_ref[1, y] * following[y:y + 1]
 
@@ -277,21 +289,21 @@
     yn = around(yn, "gy", -1)
     zp = around(zp, "zg", 1)
     zn = around(zn, "zg", -1)
-    factors, inner, faces = call(
+    factors, inner, faces, z_factors, spikes, coeffs = call(
         inner_kernel, "inner",
-        [(2 * len(X_STRIDES) + 1, NB // 2, NX, 2 * NZB), block, (NB - 1, NZB, NX)], [t, k])
-    bundle, back = call(
-        first_kernel, "first", [(NZB * VALUES, NX), (3, NB - 1, NZB, NX)],
+        [(2 * len(X_STRIDES) + 1, NB // 2, NX, 2 * NZB), block, (NB - 1, NZB, NX),
+         (2 * len(Z_STRIDES) + 1,) + block, (2,) + block, (3, NB, NX)], [t, k])
+    bundle, back, top = call(
+        first_kernel, "first", [(NZB * VALUES, NX), (3, NB - 1, NZB, NX), (NB, NX)],
         [t, k, factors, inner, faces, yp, yn, zp, zn])
     columns = lax.all_to_all(bundle.reshape(NZB * VALUES, 1, NX), "gy", split_axis=0, concat_axis=0, tiled=True)
-    z_factors, spikes, coeffs = call(
-        z_kernel, "z", [(2 * len(Z_STRIDES) + 1,) + block, (2,) + block, (3, NB, NX)], [k, zn])
     (ends,) = call(column_kernel, "column", [(2 * NGY, NX)], [columns.reshape(NGY * VALUES, NX)])
     ends = lax.all_to_all(ends, "gy", split_axis=0, concat_axis=0, tiled=True)
-    second, sums = call(second_kernel, "second", [block, (5, NB, NX)], [ends, back, spikes, coeffs])
+    second, sums, last_row = call(
+        second_kernel, "second", [block, (5, NB, NX), (3, NB, NX)], [ends, back, spikes, coeffs, top])
     sums = [sums] + [around(sums, "zg", j) for j in range(1, NZG)]
     (local,) = call(local_z_kernel, "local_z", [block], [second, z_factors, t])
-    (out,) = call(last_kernel, "last", [block], [local, spikes] + sums,
+    (out,) = call(last_kernel, "last", [block], [local, spikes, last_row] + sums,
                   scratch=[pltpu.VMEM((NZG, 5, NB, NX), jnp.float32), pltpu.VMEM((NZG + 1, NB, NX), jnp.float32)])
     return out
 

time: 57.7 us -> 56 us (0.971)
  blocking collectives: 24.9 us -> 38.9 us
  waiting for transfers between devices: 13.7 us -> 3.29 us
  starting transfers between devices: 13.7 us -> 9.52 us
  Pallas kernels: 4.74 us -> 4.14 us
    all_to_all x0 -> x1, blocking collectives: none -> 14.9 us  [shards(): ends = lax.all_to_all(ends, 'gy', split_axis=0, concat_axis=0, tiled=True)]
    all_to_all x1 -> x0, waiting for transfers between devices: 8.99 us -> none  [shards(): ends = lax.all_to_all(ends, 'gy', split_axis=0, concat_axis=0, tiled=True)]
    all_to_all x1 -> x0, starting transfers between devices: 5.35 us -> none  [shards(): ends = lax.all_to_all(ends, 'gy', split_axis=0, concat_axis=0, tiled=True)]
    ppermute x7, waiting for transfers between devices: 4.7 us -> 3.29 us  [around(): return lax.ppermute(x, axis, [(i, (i + by) % count) for i in range(count)])]
    ppermute x7, starting transfers between devices: 8.34 us -> 9.52 us  [around(): return lax.ppermute(x, axis, [(i, (i + by) % count) for i in range(count)])]
    all_to_all x1, blocking collectives: 24.9 us -> 23.9 us  [shards(): lax.all_to_all(bundle.reshape(NZB * VALUES, 1, NX), 'gy', split_axis=0, c...]
    pallas_call x8 -> x7, Pallas kernels: 4.74 us -> 4.14 us  [call(): pl.pallas_call(kernel, name=name, out_shape=shapes, in_specs=[pl.BlockSpe...]
  transfers between devices with their start and end apart: 8 -> 7, of which waited for: 5 -> 2; matrix products, arithmetic and copies ran while one was open for 0% -> 0% of each run, Pallas kernels for 3% -> 3%
where the time goes in v3:
time: 56 us; the launch traced here: 55.9 us
  blocking collectives  38.9 us (69%)
  starting transfers between devices  9.52 us (17%)
  Pallas kernels  4.14 us (7%)
  waiting for transfers between devices  3.29 us (6%)
    all_to_all x1, blocking collectives, shards(): lax.all_to_all(bundle.reshape(NZB * VALUES, 1, NX), 'gy', split_axis=0, c...  23.9 us
    all_to_all x1, blocking collectives, shards(): ends = lax.all_to_all(ends, 'gy', split_axis=0, concat_axis=0, tiled=True)  14.9 us
    ppermute x7, starting transfers between devices, around(): return lax.ppermute(x, axis, [(i, (i + by) % count) for i in range(count)])  9.52 us
    pallas_call x7, Pallas kernels, call(): pl.pallas_call(kernel, name=name, out_shape=shapes, in_specs=[pl.BlockSpe...  4.14 us
    ppermute x7, waiting for transfers between devices, around(): return lax.ppermute(x, axis, [(i, (i + by) % count) for i in range(count)])  3.29 us
  transfers between devices with their start and end apart: 7, of which 2 were waited for; matrix products, arithmetic and copies ran while one was open for 0% of the time, Pallas kernels for 3%

profile of v3, /device:TPU:1, one launch (start us, length us, event | category | flops | bytes accessed | tf_op | source)
XLA Modules:
  0.0 55.9 jit_solution(18431369649722385584)
XLA Ops:
  0.0 1.0 %load.1 = (f32[4,64,128]{2,1,0:T(8,128)S(1)}, f32[4,64,128]{2,1,0:T(8,128)S(1)}, f32[2,64,128]{2,1,0:T(8,128)S(1)}, f32[2,64,128]{2,1,0:T(8,128)S(1)}, f32[2,4,1...) custom-call(f32[4,64,128]{2,1,0:T(8,128)} %t_hbm.1, f32[4,64,128]{2,1,0:T(8,128)} %k_hbm.1), custom_call_target="tpu_custom_call" | custom-call | flops 2000000 | bytes 2000000 | tf_op jit(solution)/shard_map/load/pallas_call | solution.py:266
  1.0 3.1 %collective-permute-start = (f32[2,64,128]{2,1,0:T(8,128)S(1)}, f32[2,64,128]{2,1,0:T(8,128)S(1)}, u32[]{:S(2)}, u32[]{:S(2)}) collective-permute-start(f32[2,64,128]{2,1,0:T(8,128)S(1)} %get-tuple-element.28), channel_id=1, source_target_pairs={{0,1},{1,2},{2,3},{3,4},{4,5},{5,6},{6,7},{7,8},{8,9},{9,10},{10,1... | collective-permute-start | bytes 196616 | tf_op jit(solution)/shard_map/ppermute | solution.py:280
  4.1 0.3 collective-permute-start.1
  4.4 0.9 %collective-permute-start.2 = (f32[2,4,128]{2,1,0:T(4,128)S(1)}, f32[2,4,128]{2,1,0:T(4,128)S(1)}, u32[]{:S(2)}, u32[]{:S(2)}) collective-permute-start(f32[2,4,128]{2,1,0:T(4,128)S(1)} %get-tuple-element.30), channel_id=1, source_target_pairs={{0,64},{64,128},{128,192},{192,0},{1,65},{65,129},{129,193},{193,1... | collective-permute-start | bytes 12296 | tf_op jit(solution)/shard_map/ppermute | solution.py:280
  5.3 1.8 %collective-permute-start.3 = (f32[2,4,128]{2,1,0:T(4,128)S(1)}, f32[2,4,128]{2,1,0:T(4,128)S(1)}, u32[]{:S(2)}, u32[]{:S(2)}) collective-permute-start(f32[2,4,128]{2,1,0:T(4,128)S(1)} %get-tuple-element.31), channel_id=1, source_target_pairs={{0,192},{64,0},{128,64},{192,128},{1,193},{65,1},{129,65},{193,129... | collective-permute-start | bytes 12296 | tf_op jit(solution)/shard_map/ppermute | solution.py:280
  7.1 1.6 %inner.1 = (f32[15,2,128,128]{3,2,1,0:T(8,128)S(1)}, f32[4,64,128]{2,1,0:T(8,128)S(1)}, f32[3,64,128]{2,1,0:T(8,128)S(1)}, f32[13,4,64,128]{3,2,1,0:T(8,128)S(1)...) custom-call(f32[4,64,128]{2,1,0:T(8,128)S(1)} %get-tuple-element.23.t_ref, ...), custom_call_target="tpu_custom_call" | custom-call | flops 2000000 | bytes 2000000 | tf_op jit(solution)/shard_map/inner/pallas_call | solution.py:266
  8.7 0.0 collective-permute-done.2.zp_ref
  8.7 0.0 collective-permute-done.3.zn_ref
  8.7 0.0 collective-permute-done.yp_ref
  8.7 0.0 collective-permute-done.1.yn_ref
  8.8 0.4 first.1
  9.1 23.9 %all_to_all.16 = f32[320,1,128]{2,1,0:T(1,128)S(1)} all-to-all(f32[320,1,128]{2,1,0:T(1,128)S(1)} %bitcast.9), channel_id=1, replica_groups=mesh['zg'=4,'gy'=64] {'gy'}, dimensions={0} | all-to-all | bytes 327680 | tf_op jit(solution)/shard_map/all_to_all | solution.py:299
  33.1 0.2 column.1
  33.2 14.9 %all_to_all.17 = f32[64,2,128]{2,1,0:T(2,128)S(1)} all-to-all(f32[64,2,128]{2,1,0:T(2,128)S(1)} %bitcast.8), channel_id=1, replica_groups=mesh['zg'=4,'gy'=64] {'gy'}, dimensions={0} | all-to-all | bytes 131072 | tf_op jit(solution)/shard_map/all_to_all | solution.py:301
  48.2 0.1 second.1
  48.2 2.8 %collective-permute-start.6 = (f32[5,4,128]{2,1,0:T(4,128)S(1)}, f32[5,4,128]{2,1,0:T(4,128)S(1)}, u32[]{:S(2)}, u32[]{:S(2)}) collective-permute-start(f32[5,4,128]{2,1,0:T(4,128)S(1)} %get-tuple-element.40.e0_ref), channel_id=1, source_target_pairs={{0,192},{64,0},{128,64},{192,128},{1,193},{65,1},{129,65},{193,129... | collective-permute-start | bytes 30728 | tf_op jit(solution)/shard_map/ppermute | solution.py:280
  51.0 0.3 collective-permute-start.5
  51.3 0.4 collective-permute-start.4
  51.7 0.2 local_z.1.local_ref
  51.8 0.0 collective-permute-done.6.e3_ref
  51.9 3.2 %collective-permute-done.5.e2_ref = f32[5,4,128]{2,1,0:T(4,128)S(1)} collective-permute-done((f32[5,4,128]{2,1,0:T(4,128)S(1)}, f32[5,4,128]{2,1,0:T(4,128)S(1)}, u32[]{:S(2)}, u32[]{:S(2)}) %collective-permute-start.5) | collective-permute-done | bytes 10272 | tf_op jit(solution)/shard_map/ppermute | solution.py:280
  55.0 0.1 collective-permute-done.4.e1_ref
  55.1 0.7 %last.1 = f32[4,64,128]{2,1,0:T(8,128)} custom-call(f32[4,64,128]{2,1,0:T(8,128)S(1)} %local_z.1.local_ref, f32[2,4,64,128]{3,2,1,0:T(8,128)S(1)} %get-tuple-element.34.spikes_ref, f32[3,4,128]{2,1,0:T(4,128)S(1)} %get-tuple-element.39.last_row_ref, f32[5,4,128]{2,1,0:T(4,128)S(1)} %get-tuple-element.40.e0_ref, ...), custom_call_target="tpu_custom_call" | custom-call | flops 2000000 | bytes 2000000 | tf_op jit(solution)/shard_map/last/pallas_call | solution.py:266
Async XLA Ops:
  1.0 7.7 %collective-permute-start = (f32[2,64,128]{2,1,0:T(8,128)S(1)}, f32[2,64,128]{2,1,0:T(8,128)S(1)}, u32[]{:S(2)}, u32[]{:S(2)}) collective-permute-start(f32[2,64,128]{2,1,0:T(8,128)S(1)} %get-tuple-element.28), channel_id=1, source_target_pairs={{0,1},{1,2},{2,3},{3,4},{4,5},{5,6},{6,7},{7,8},{8,9},{9,10},{10,1... | collective-permute-start | bytes 196616 | tf_op jit(solution)/shard_map/ppermute | solution.py:280
  4.1 4.6 %collective-permute-start.1 = (f32[2,64,128]{2,1,0:T(8,128)S(1)}, f32[2,64,128]{2,1,0:T(8,128)S(1)}, u32[]{:S(2)}, u32[]{:S(2)}) collective-permute-start(f32[2,64,128]{2,1,0:T(8,128)S(1)} %get-tuple-element.29), channel_id=1, source_target_pairs={{0,63},{1,0},{2,1},{3,2},{4,3},{5,4},{6,5},{7,6},{8,7},{9,8},{10,9... | collective-permute-start | bytes 196616 | tf_op jit(solution)/shard_map/ppermute | solution.py:280
  4.4 4.3 %collective-permute-start.2 = (f32[2,4,128]{2,1,0:T(4,128)S(1)}, f32[2,4,128]{2,1,0:T(4,128)S(1)}, u32[]{:S(2)}, u32[]{:S(2)}) collective-permute-start(f32[2,4,128]{2,1,0:T(4,128)S(1)} %get-tuple-element.30), channel_id=1, source_target_pairs={{0,64},{64,128},{128,192},{192,0},{1,65},{65,129},{129,193},{193,1... | collective-permute-start | bytes 12296 | tf_op jit(solution)/shard_map/ppermute | solution.py:280
  5.3 3.4 %collective-permute-start.3 = (f32[2,4,128]{2,1,0:T(4,128)S(1)}, f32[2,4,128]{2,1,0:T(4,128)S(1)}, u32[]{:S(2)}, u32[]{:S(2)}) collective-permute-start(f32[2,4,128]{2,1,0:T(4,128)S(1)} %get-tuple-element.31), channel_id=1, source_target_pairs={{0,192},{64,0},{128,64},{192,128},{1,193},{65,1},{129,65},{193,129... | collective-permute-start | bytes 12296 | tf_op jit(solution)/shard_map/ppermute | solution.py:280
  48.2 3.6 %collective-permute-start.6 = (f32[5,4,128]{2,1,0:T(4,128)S(1)}, f32[5,4,128]{2,1,0:T(4,128)S(1)}, u32[]{:S(2)}, u32[]{:S(2)}) collective-permute-start(f32[5,4,128]{2,1,0:T(4,128)S(1)} %get-tuple-element.40.e0_ref), channel_id=1, source_target_pairs={{0,192},{64,0},{128,64},{192,128},{1,193},{65,1},{129,65},{193,129... | collective-permute-start | bytes 30728 | tf_op jit(solution)/shard_map/ppermute | solution.py:280
  51.0 4.0 %collective-permute-start.5 = (f32[5,4,128]{2,1,0:T(4,128)S(1)}, f32[5,4,128]{2,1,0:T(4,128)S(1)}, u32[]{:S(2)}, u32[]{:S(2)}) collective-permute-start(f32[5,4,128]{2,1,0:T(4,128)S(1)} %get-tuple-element.40.e0_ref), channel_id=1, source_target_pairs={{0,128},{64,192},{128,0},{192,64},{1,129},{65,193},{129,1},{193,65... | collective-permute-start | bytes 30728 | tf_op jit(solution)/shard_map/ppermute | solution.py:280
  51.3 3.8 %collective-permute-start.4 = (f32[5,4,128]{2,1,0:T(4,128)S(1)}, f32[5,4,128]{2,1,0:T(4,128)S(1)}, u32[]{:S(2)}, u32[]{:S(2)}) collective-permute-start(f32[5,4,128]{2,1,0:T(4,128)S(1)} %get-tuple-element.40.e0_ref), channel_id=1, source_target_pairs={{0,64},{64,128},{128,192},{192,0},{1,65},{65,129},{129,193},{193,1... | collective-permute-start | bytes 30728 | tf_op jit(solution)/shard_map/ppermute | solution.py:280

commit v4 on v3

--- a/solution.py
+++ b/solution.py
@@ -12,6 +12,8 @@
 X_STRIDES = (1, 2, 4, 8, 16, 32, 64)
 Z_STRIDES = (1, 2, 4, 8, 16, 32)
 VALUES = 5
+
+HALO_GRANT, STAGE_GRANT = 55000, 54940
 
 
 def face(k, q):
@@ -45,17 +47,25 @@
     return b * get(2 * len(strides))
 
 
-def load_kernel(t_hbm, k_hbm, t_ref, k_ref, yp_ref, yn_ref, zp_ref, zn_ref, sems):
-    copies = [pltpu.make_async_copy(t_hbm, t_ref, sems.at[0]), pltpu.make_async_copy(k_hbm, k_ref, sems.at[1])]
+def halo_kernel(t_hbm, k_hbm, across_ref, inside_ref, zp_ref, zn_ref, edges, sems):
+    odd = lax.rem(lax.axis_index("gy"), 2)
+    copies = []
+    for j, array in enumerate((t_hbm, k_hbm)):
+        moves = (
+            (array.at[odd * (NB - 1)], across_ref.at[j]),
+            (array.at[(1 - odd) * (NB - 1)], inside_ref.at[j]),
+            (array.at[:, pl.ds(NZB - 8, 8)], edges.at[j, 0]),
+            (array.at[:, pl.ds(0, 8)], edges.at[j, 1]),
+        )
+        for n, (source, target) in enumerate(moves):
+            copies.append(pltpu.make_async_copy(source, target, sems.at[j, n]))
+            copies[-1].start()
     for copy in copies:
-        copy.start()
-    for j, (copy, ref) in enumerate(zip(copies, (t_ref, k_ref))):
         copy.wait()
-        yp_ref[j] = ref[NB - 1]
-        yn_ref[j] = ref[0]
+    for j in range(2):
         for y in range(NB):
-            zp_ref[j, y:y + 1] = ref[y, NZB - 1:]
-            zn_ref[j, y:y + 1] = ref[y, :1]
+            zp_ref[j, y:y + 1] = edges[j, 0, y, 7:]
+            zn_ref[j, y:y + 1] = edges[j, 1, y, :1]
 
 
 def pair(ref, h):
@@ -85,6 +95,14 @@
         spikes_ref[1, y] = rho
         coeffs_ref[0, y:y + 1] = jnp.sum(lam, axis=0, keepdims=True)
         coeffs_ref[1, y:y + 1] = jnp.sum(rho, axis=0, keepdims=True)
+
+
+def stage_kernel(t_hbm, k_hbm, t_ref, k_ref, sems):
+    copies = [pltpu.make_async_copy(t_hbm, t_ref, sems.at[0]), pltpu.make_async_copy(k_hbm, k_ref, sems.at[1])]
+    for copy in copies:
+        copy.start()
+    for copy in copies:
+        copy.wait()
 
 
 def inner_kernel(t_ref, k_ref, factors_ref, inner_ref, faces_ref, z_factors_ref, spikes_ref, coeffs_ref):
@@ -119,10 +137,13 @@
     z_part(k_ref, z_factors_ref, spikes_ref, coeffs_ref)
 
 
-def first_kernel(t_ref, k_ref, factors_ref, inner_ref, faces_ref, yp_ref, yn_ref, zp_ref, zn_ref,
+def first_kernel(t_ref, k_ref, factors_ref, inner_ref, faces_ref, across_ref, inside_ref, zp_ref, zn_ref,
                  bundle_ref, back_ref, top_ref):
     gy = lax.axis_index("gy")
     zg = lax.axis_index("zg")
+    odd = lax.rem(gy, 2) == 1
+    yp = [jnp.where(odd, inside_ref[j], across_ref[j]) for j in range(2)]
+    yn = [jnp.where(odd, across_ref[j], inside_ref[j]) for j in range(2)]
     has_south = jnp.where(gy > 0, 1.0, 0.0)
     has_north = jnp.where(gy < NGY - 1, 1.0, 0.0)
     has_below = jnp.where(zg > 0, 1.0, 0.0)
@@ -135,10 +156,10 @@
         t = t_ref[y]
         k = k_ref[y]
         if y == 0:
-            b = b + face(k, yp_ref[1] * has_south) * (yp_ref[0] - t)
+            b = b + face(k, yp[1] * has_south) * (yp[0] - t)
         if y == NB - 1:
-            g4 = face(k, yn_ref[1] * has_north)
-            b = b + g4 * (yn_ref[0] - t)
+            g4 = face(k, yn[1] * has_north)
+            b = b + g4 * (yn[0] - t)
         below = face(k[:1], zp_ref[1, y:y + 1] * has_below) * (zp_ref[0, y:y + 1] - t[:1])
         top = face(k[NZB - 1:], zn_ref[1, y:y + 1] * has_above)
         top_ref[y:y + 1] = top
@@ -260,18 +281,18 @@
         out_ref[y] = local_ref[y] + spikes_ref[0, y] * own[y:y + 1] + spikes_ref[1, y] * following[y:y + 1]
 
 
-def call(kernel, name, outs, args, scratch=(), cost=2000000, whole=False):
+def call(kernel, name, outs, args, scratch=(), cost=2000000, granted=0):
     shapes = [jax.ShapeDtypeStruct(o, jnp.float32) for o in outs]
     vmem = pl.BlockSpec(memory_space=pltpu.VMEM)
     return pl.pallas_call(
         kernel,
         name=name,
         out_shape=shapes,
-        in_specs=[pl.BlockSpec(memory_space=pltpu.HBM)] * len(args) if whole else [vmem] * len(args),
+        in_specs=[pl.BlockSpec(memory_space=pltpu.HBM)] * len(args) if granted else [vmem] * len(args),
         out_specs=[vmem] * len(outs),
         scratch_shapes=scratch,
         cost_estimate=pl.CostEstimate(flops=cost, bytes_accessed=cost, transcendentals=0),
-        compiler_params=pltpu.CompilerParams(vmem_limit_bytes=(54816 if whole else 24576) * 1024),
+        compiler_params=pltpu.CompilerParams(vmem_limit_bytes=(granted or 24576) * 1024),
     )(*args)
 
 
@@ -280,22 +301,29 @@
     return lax.ppermute(x, axis, [(i, (i + by) % count) for i in range(count)])
 
 
+def swapped(x, axis, first):
+    count = lax.axis_size(axis)
+    return lax.ppermute(x, axis, [(i, (((i - first) ^ 1) + first) % count) for i in range(count)])
+
+
 def shards(t, k):
     block = (NB, NZB, NX)
-    t, k, yp, yn, zp, zn = call(
-        load_kernel, "load", [block, block, (2, NZB, NX), (2, NZB, NX), (2, NB, NX), (2, NB, NX)], [t, k],
-        scratch=[pltpu.SemaphoreType.DMA((2,))], whole=True)
-    yp = around(yp, "gy", 1)
-    yn = around(yn, "gy", -1)
+    across, inside, zp, zn = call(
+        halo_kernel, "halo", [(2, NZB, NX), (2, NZB, NX), (2, NB, NX), (2, NB, NX)], [t, k],
+        scratch=[pltpu.VMEM((2, 2, NB, 8, NX), jnp.float32), pltpu.SemaphoreType.DMA((2, 4))], granted=HALO_GRANT)
+    across = swapped(across, "gy", 1)
     zp = around(zp, "zg", 1)
     zn = around(zn, "zg", -1)
+    inside = swapped(inside, "gy", 0)
+    t, k = call(stage_kernel, "stage", [block, block], [t, k],
+                scratch=[pltpu.SemaphoreType.DMA((2,))], granted=STAGE_GRANT)
     factors, inner, faces, z_factors, spikes, coeffs = call(
         inner_kernel, "inner",
         [(2 * len(X_STRIDES) + 1, NB // 2, NX, 2 * NZB), block, (NB - 1, NZB, NX),
          (2 * len(Z_STRIDES) + 1,) + block, (2,) + block, (3, NB, NX)], [t, k])
     bundle, back, top = call(
         first_kernel, "first", [(NZB * VALUES, NX), (3, NB - 1, NZB, NX), (NB, NX)],
-        [t, k, factors, inner, faces, yp, yn, zp, zn])
+        [t, k, factors, inner, faces, across, inside, zp, zn])
     columns = lax.all_to_all(bundle.reshape(NZB * VALUES, 1, NX), "gy", split_axis=0, concat_axis=0, tiled=True)
     (ends,) = call(column_kernel, "column", [(2 * NGY, NX)], [columns.reshape(NGY * VALUES, NX)])
     ends = lax.all_to_all(ends, "gy", split_axis=0, concat_axis=0, tiled=True)

time: 56 us -> 54.2 us (0.968)
  blocking collectives: 38.9 us -> 30.9 us
  starting transfers between devices: 9.52 us -> 14.6 us
  Pallas kernels: 4.14 us -> 5.07 us
    ppermute x0 -> x2, starting transfers between devices: none -> 9.34 us  [swapped(): lax.ppermute(x, axis, [(i, ((i - first ^ 1) + first) % count) for i in ra...]
    all_to_all x1, blocking collectives: 23.9 us -> 16 us  [shards(): lax.all_to_all(bundle.reshape(NZB * VALUES, 1, NX), 'gy', split_axis=0, c...]
    ppermute x7 -> x5, starting transfers between devices: 9.52 us -> 5.29 us  [around(): return lax.ppermute(x, axis, [(i, (i + by) % count) for i in range(count)])]
    pallas_call x7 -> x8, Pallas kernels: 4.14 us -> 5.07 us  [call(): pl.pallas_call(kernel, name=name, out_shape=shapes, in_specs=[pl.BlockSpe...]
    ppermute x7 -> x5, waiting for transfers between devices: 3.29 us -> 3.29 us  [around(): return lax.ppermute(x, axis, [(i, (i + by) % count) for i in range(count)])]
  transfers between devices with their start and end apart: 7 -> 7, of which waited for: 2 -> 2; matrix products, arithmetic and copies ran while one was open for 0% -> 0% of each run, Pallas kernels for 3% -> 5%
where the time goes in v4:
time: 54.2 us; the launch traced here: 54 us
  blocking collectives  30.9 us (57%)
  starting transfers between devices  14.6 us (27%)
  Pallas kernels  5.07 us (9%)
  waiting for transfers between devices  3.29 us (6%)
    all_to_all x1, blocking collectives, shards(): lax.all_to_all(bundle.reshape(NZB * VALUES, 1, NX), 'gy', split_axis=0, c...  16 us
    all_to_all x1, blocking collectives, shards(): ends = lax.all_to_all(ends, 'gy', split_axis=0, concat_axis=0, tiled=True)  14.9 us
    ppermute x2, starting transfers between devices, swapped(): lax.ppermute(x, axis, [(i, ((i - first ^ 1) + first) % count) for i in ra...  9.34 us
    ppermute x5, starting transfers between devices, around(): return lax.ppermute(x, axis, [(i, (i + by) % count) for i in range(count)])  5.29 us
    pallas_call x8, Pallas kernels, call(): pl.pallas_call(kernel, name=name, out_shape=shapes, in_specs=[pl.BlockSpe...  5.07 us
    ppermute x5, waiting for transfers between devices, around(): return lax.ppermute(x, axis, [(i, (i + by) % count) for i in range(count)])  3.29 us
  transfers between devices with their start and end apart: 7, of which 2 were waited for; matrix products, arithmetic and copies ran while one was open for 0% of the time, Pallas kernels for 5%

profile of v4, /device:TPU:1, one launch (start us, length us, event | category | flops | bytes accessed | tf_op | source)
XLA Modules:
  0.0 54.0 jit_solution(16181843046589257236)
XLA Ops:
  0.0 0.9 %halo.1 = (f32[2,64,128]{2,1,0:T(8,128)S(1)}, f32[2,64,128]{2,1,0:T(8,128)S(1)}, f32[2,4,128]{2,1,0:T(4,128)S(1)}, f32[2,4,128]{2,1,0:T(4,128)S(1)}) custom-call(f32[4,64,128]{2,1,0:T(8,128)} %t_hbm.3, f32[4,64,128]{2,1,0:T(8,128)} %k_hbm.3), custom_call_target="tpu_custom_call" | custom-call | flops 2000000 | bytes 2000000 | tf_op jit(solution)/shard_map/halo/pallas_call | solution.py:287
  0.9 3.1 %collective-permute-start = (f32[2,64,128]{2,1,0:T(8,128)S(1)}, f32[2,64,128]{2,1,0:T(8,128)S(1)}, u32[]{:S(2)}, u32[]{:S(2)}) collective-permute-start(f32[2,64,128]{2,1,0:T(8,128)S(1)} %get-tuple-element.28), channel_id=1, source_target_pairs={{0,63},{1,2},{2,1},{3,4},{4,3},{5,6},{6,5},{7,8},{8,7},{9,10},{10,... | collective-permute-start | bytes 196616 | tf_op jit(solution)/shard_map/ppermute | solution.py:306
  4.0 6.2 %collective-permute-start.1 = (f32[2,64,128]{2,1,0:T(8,128)S(1)}, f32[2,64,128]{2,1,0:T(8,128)S(1)}, u32[]{:S(2)}, u32[]{:S(2)}) collective-permute-start(f32[2,64,128]{2,1,0:T(8,128)S(1)} %get-tuple-element.29), channel_id=1, source_target_pairs={{0,1},{1,0},{2,3},{3,2},{4,5},{5,4},{6,7},{7,6},{8,9},{9,8},{10,11... | collective-permute-start | bytes 196616 | tf_op jit(solution)/shard_map/ppermute | solution.py:306
  10.3 1.2 %collective-permute-start.2 = (f32[2,4,128]{2,1,0:T(4,128)S(1)}, f32[2,4,128]{2,1,0:T(4,128)S(1)}, u32[]{:S(2)}, u32[]{:S(2)}) collective-permute-start(f32[2,4,128]{2,1,0:T(4,128)S(1)} %get-tuple-element.30), channel_id=1, source_target_pairs={{0,64},{64,128},{128,192},{192,0},{1,65},{65,129},{129,193},{193,1... | collective-permute-start | bytes 12296 | tf_op jit(solution)/shard_map/ppermute | solution.py:301
  11.5 1.5 %collective-permute-start.3 = (f32[2,4,128]{2,1,0:T(4,128)S(1)}, f32[2,4,128]{2,1,0:T(4,128)S(1)}, u32[]{:S(2)}, u32[]{:S(2)}) collective-permute-start(f32[2,4,128]{2,1,0:T(4,128)S(1)} %get-tuple-element.31), channel_id=1, source_target_pairs={{0,192},{64,0},{128,64},{192,128},{1,193},{65,1},{129,65},{193,129... | collective-permute-start | bytes 12296 | tf_op jit(solution)/shard_map/ppermute | solution.py:301
  12.9 1.0 %stage.1 = (f32[4,64,128]{2,1,0:T(8,128)S(1)}, f32[4,64,128]{2,1,0:T(8,128)S(1)}) custom-call(f32[4,64,128]{2,1,0:T(8,128)} %t_hbm.3, f32[4,64,128]{2,1,0:T(8,128)} %k_hbm.3), custom_call_target="tpu_custom_call" | custom-call | flops 2000000 | bytes 2000000 | tf_op jit(solution)/shard_map/stage/pallas_call | solution.py:287
  13.9 1.6 %inner.1 = (f32[15,2,128,128]{3,2,1,0:T(8,128)S(1)}, f32[4,64,128]{2,1,0:T(8,128)S(1)}, f32[3,64,128]{2,1,0:T(8,128)S(1)}, f32[13,4,64,128]{3,2,1,0:T(8,128)S(1)...) custom-call(f32[4,64,128]{2,1,0:T(8,128)S(1)} %get-tuple-element.23.t_ref, ...), custom_call_target="tpu_custom_call" | custom-call | flops 2000000 | bytes 2000000 | tf_op jit(solution)/shard_map/inner/pallas_call | solution.py:287
  15.6 0.0 collective-permute-done.2.zp_ref
  15.6 0.0 collective-permute-done.3.zn_ref
  15.6 0.0 collective-permute-done.across_ref
  15.6 0.0 collective-permute-done.1.inside_ref
  15.6 0.4 first.1
  16.0 16.0 %all_to_all.16 = f32[320,1,128]{2,1,0:T(1,128)S(1)} all-to-all(f32[320,1,128]{2,1,0:T(1,128)S(1)} %bitcast.9), channel_id=1, replica_groups=mesh['zg'=4,'gy'=64] {'gy'}, dimensions={0} | all-to-all | bytes 327680 | tf_op jit(solution)/shard_map/all_to_all | solution.py:327
  32.0 0.2 column.1
  32.2 14.9 %all_to_all.17 = f32[64,2,128]{2,1,0:T(2,128)S(1)} all-to-all(f32[64,2,128]{2,1,0:T(2,128)S(1)} %bitcast.8), channel_id=1, replica_groups=mesh['zg'=4,'gy'=64] {'gy'}, dimensions={0} | all-to-all | bytes 131072 | tf_op jit(solution)/shard_map/all_to_all | solution.py:329
  47.1 0.1 second.1
  47.2 1.9 %collective-permute-start.6 = (f32[5,4,128]{2,1,0:T(4,128)S(1)}, f32[5,4,128]{2,1,0:T(4,128)S(1)}, u32[]{:S(2)}, u32[]{:S(2)}) collective-permute-start(f32[5,4,128]{2,1,0:T(4,128)S(1)} %get-tuple-element.40.e0_ref), channel_id=1, source_target_pairs={{0,192},{64,0},{128,64},{192,128},{1,193},{65,1},{129,65},{193,129... | collective-permute-start | bytes 30728 | tf_op jit(solution)/shard_map/ppermute | solution.py:301
  49.1 0.3 collective-permute-start.5
  49.4 0.4 collective-permute-start.4
  49.8 0.2 local_z.1.local_ref
  50.0 0.0 collective-permute-done.6.e3_ref
  50.0 3.2 %collective-permute-done.5.e2_ref = f32[5,4,128]{2,1,0:T(4,128)S(1)} collective-permute-done((f32[5,4,128]{2,1,0:T(4,128)S(1)}, f32[5,4,128]{2,1,0:T(4,128)S(1)}, u32[]{:S(2)}, u32[]{:S(2)}) %collective-permute-start.5) | collective-permute-done | bytes 10272 | tf_op jit(solution)/shard_map/ppermute | solution.py:301
  53.1 0.1 collective-permute-done.4.e1_ref
  53.3 0.7 %last.1 = f32[4,64,128]{2,1,0:T(8,128)} custom-call(f32[4,64,128]{2,1,0:T(8,128)S(1)} %local_z.1.local_ref, f32[2,4,64,128]{3,2,1,0:T(8,128)S(1)} %get-tuple-element.34.spikes_ref, f32[3,4,128]{2,1,0:T(4,128)S(1)} %get-tuple-element.39.last_row_ref, f32[5,4,128]{2,1,0:T(4,128)S(1)} %get-tuple-element.40.e0_ref, ...), custom_call_target="tpu_custom_call" | custom-call | flops 2000000 | bytes 2000000 | tf_op jit(solution)/shard_map/last/pallas_call | solution.py:287
Async XLA Ops:
  0.9 14.7 %collective-permute-start = (f32[2,64,128]{2,1,0:T(8,128)S(1)}, f32[2,64,128]{2,1,0:T(8,128)S(1)}, u32[]{:S(2)}, u32[]{:S(2)}) collective-permute-start(f32[2,64,128]{2,1,0:T(8,128)S(1)} %get-tuple-element.28), channel_id=1, source_target_pairs={{0,63},{1,2},{2,1},{3,4},{4,3},{5,6},{6,5},{7,8},{8,7},{9,10},{10,... | collective-permute-start | bytes 196616 | tf_op jit(solution)/shard_map/ppermute | solution.py:306
  4.0 11.6 %collective-permute-start.1 = (f32[2,64,128]{2,1,0:T(8,128)S(1)}, f32[2,64,128]{2,1,0:T(8,128)S(1)}, u32[]{:S(2)}, u32[]{:S(2)}) collective-permute-start(f32[2,64,128]{2,1,0:T(8,128)S(1)} %get-tuple-element.29), channel_id=1, source_target_pairs={{0,1},{1,0},{2,3},{3,2},{4,5},{5,4},{6,7},{7,6},{8,9},{9,8},{10,11... | collective-permute-start | bytes 196616 | tf_op jit(solution)/shard_map/ppermute | solution.py:306
  10.3 5.3 %collective-permute-start.2 = (f32[2,4,128]{2,1,0:T(4,128)S(1)}, f32[2,4,128]{2,1,0:T(4,128)S(1)}, u32[]{:S(2)}, u32[]{:S(2)}) collective-permute-start(f32[2,4,128]{2,1,0:T(4,128)S(1)} %get-tuple-element.30), channel_id=1, source_target_pairs={{0,64},{64,128},{128,192},{192,0},{1,65},{65,129},{129,193},{193,1... | collective-permute-start | bytes 12296 | tf_op jit(solution)/shard_map/ppermute | solution.py:301
  11.5 4.1 %collective-permute-start.3 = (f32[2,4,128]{2,1,0:T(4,128)S(1)}, f32[2,4,128]{2,1,0:T(4,128)S(1)}, u32[]{:S(2)}, u32[]{:S(2)}) collective-permute-start(f32[2,4,128]{2,1,0:T(4,128)S(1)} %get-tuple-element.31), channel_id=1, source_target_pairs={{0,192},{64,0},{128,64},{192,128},{1,193},{65,1},{129,65},{193,129... | collective-permute-start | bytes 12296 | tf_op jit(solution)/shard_map/ppermute | solution.py:301
  47.2 2.8 %collective-permute-start.6 = (f32[5,4,128]{2,1,0:T(4,128)S(1)}, f32[5,4,128]{2,1,0:T(4,128)S(1)}, u32[]{:S(2)}, u32[]{:S(2)}) collective-permute-start(f32[5,4,128]{2,1,0:T(4,128)S(1)} %get-tuple-element.40.e0_ref), channel_id=1, source_target_pairs={{0,192},{64,0},{128,64},{192,128},{1,193},{65,1},{129,65},{193,129... | collective-permute-start | bytes 30728 | tf_op jit(solution)/shard_map/ppermute | solution.py:301
  49.1 4.0 %collective-permute-start.5 = (f32[5,4,128]{2,1,0:T(4,128)S(1)}, f32[5,4,128]{2,1,0:T(4,128)S(1)}, u32[]{:S(2)}, u32[]{:S(2)}) collective-permute-start(f32[5,4,128]{2,1,0:T(4,128)S(1)} %get-tuple-element.40.e0_ref), channel_id=1, source_target_pairs={{0,128},{64,192},{128,0},{192,64},{1,129},{65,193},{129,1},{193,65... | collective-permute-start | bytes 30728 | tf_op jit(solution)/shard_map/ppermute | solution.py:301
  49.4 3.8 %collective-permute-start.4 = (f32[5,4,128]{2,1,0:T(4,128)S(1)}, f32[5,4,128]{2,1,0:T(4,128)S(1)}, u32[]{:S(2)}, u32[]{:S(2)}) collective-permute-start(f32[5,4,128]{2,1,0:T(4,128)S(1)} %get-tuple-element.40.e0_ref), channel_id=1, source_target_pairs={{0,64},{64,128},{128,192},{192,0},{1,65},{65,129},{129,193},{193,1... | collective-permute-start | bytes 30728 | tf_op jit(solution)/shard_map/ppermute | solution.py:301

commit v5 on v3

v5 whole, which is shorter than its diff:
```python
import jax
import jax.numpy as jnp
from jax import lax
from jax.experimental import pallas as pl
from jax.experimental.pallas import tpu as pltpu
from jax.sharding import PartitionSpec as P

mesh_courant_number = 300.0

NB, NZB, NX = 4, 64, 128
NGY, NZG = 64, 4
LANES = 8
XC, ZC, YC = NX // LANES, NZB // LANES, NGY // LANES
STRIDES = (1, 2, 4)
VALUES = 5

LOAD_GRANT = 54816


def face(k, q):
    return (2.0 * mesh_courant_number) * k * q / (k + q)


def shift(v, by, axis):
    return pltpu.roll(v, by % v.shape[axis], axis)


def rows_of(shape, axis):
    return lax.broadcasted_iota(jnp.int32, shape, axis)


def chunked(load, count):
    return jnp.concatenate([load(pl.ds(a, LANES, stride=count)) for a in range(count)], axis=0)


def split(v):
    return [v[LANES * a:LANES * (a + 1)] for a in range(v.shape[0] // LANES)]


def before(v):
    last = v.shape[0] - LANES
    return jnp.concatenate([shift(v[last:], 1, 0), v[:last]], axis=0)


def after(v):
    return jnp.concatenate([v[LANES:], shift(v[:LANES], -1, 0)], axis=0)


def order(count):
    step = 1
    while step < count:
        for a in range(step, count, 2 * step):
            yield a, step
        step *= 2


def fold(leaks, couples, closed=None):
    leaks, couples, plan, over = list(leaks), list(couples), [], 0.0
    count = len(leaks)
    for a, step in order(count):
        low, high = couples[a - step], couples[a]
        inverse = 1.0 / (leaks[a] + low + high)
        left, right = low * inverse, high * inverse
        if closed is not None and a == count - 1:
            inverse = jnp.where(closed, 0.0, inverse)
            left = jnp.where(closed, 0.0, left)
            right = jnp.where(closed, 1.0, right)
        plan.append((inverse, left, right))
        leaks[a - step] = leaks[a - step] + left * leaks[a]
        if a + step < count:
            leaks[a + step] = leaks[a + step] + right * leaks[a]
        else:
            over = over + right * leaks[a]
        couples[a - step] = low * right
    return plan, leaks[0], over, couples[0]


def fold_sources(plan, sources):
    sources, over = list(sources), 0.0
    count = len(sources)
    for (a, step), (_, left, right) in zip(order(count), plan):
        sources[a - step] = sources[a - step] + left * sources[a]
        if a + step < count:
            sources[a + step] = sources[a + step] + right * sources[a]
        else:
            over = over + right * sources[a]
    return sources, over


def unfold(plan, sources, head, following):
    count = len(plan) + 1
    x = [head] + [None] * (count - 1) + [following]
    for (a, step), (inverse, left, right) in reversed(list(zip(order(count), plan))):
        x[a] = left * x[a - step] + right * x[min(a + step, count)]
        if sources is not None:
            x[a] = x[a] + inverse * sources[a]
    return x[:count]


def put_plan(ref, at, plan):
    for i, entries in enumerate(plan):
        for j, entry in enumerate(entries):
            ref[at + (i, j)] = entry


def get_plan(ref, at, count):
    return [tuple(ref[at + (i, j)] for j in range(3)) for i in range(count - 1)]


def separator_factors(leak, low, high):
    factors = []
    for s in STRIDES:
        inverse = 1.0 / (leak + low + high)
        from_low = low * shift(inverse, s, 0)
        from_high = high * shift(inverse, -s, 0)
        factors += [from_low, from_high]
        leak = leak + from_low * shift(leak, s, 0) + from_high * shift(leak, -s, 0)
        low = from_low * shift(low, s, 0)
        high = from_high * shift(high, -s, 0)
    return factors + [1.0 / (leak + low + high)]


def separator_solve(factors, b):
    for j, s in enumerate(STRIDES):
        b = b + factors[2 * j] * shift(b, s, 0) + factors[2 * j + 1] * shift(b, -s, 0)
    return b * factors[2 * len(STRIDES)]


def load_kernel(t_hbm, k_hbm, t_ref, k_ref, across_ref, inside_ref, zp_ref, zn_ref, sems):
    odd = lax.rem(lax.axis_index("gy"), 2)
    copies = [pltpu.make_async_copy(t_hbm, t_ref, sems.at[0]), pltpu.make_async_copy(k_hbm, k_ref, sems.at[1])]
    for copy in copies:
        copy.start()
    for j, (copy, ref) in enumerate(zip(copies, (t_ref, k_ref))):
        copy.wait()
        across_ref[j] = ref[odd * (NB - 1)]
        inside_ref[j] = ref[(1 - odd) * (NB - 1)]
        for y in range(NB):
            zp_ref[j, y:y + 1] = ref[y, NZB - 1:]
            zn_ref[j, y:y + 1] = ref[y, :1]


def block_row(ref, *at):
    return chunked(lambda rows: ref[at + (rows, slice(None))], ZC)


def inner_kernel(t_ref, k_ref, inner_ref, faces_ref, x_plan_ref, x_ends_ref, z_plan_ref, z_ends_ref, spikes_ref,
                 coeffs_ref, turned):
    lane = rows_of((NZB, NX), 1)
    row = rows_of((NZB, NX), 0)
    chunk = rows_of((LANES, NX), 0)
    ts = [block_row(t_ref, y) for y in range(NB)]
    ks = [block_row(k_ref, y) for y in range(NB)]
    flux_y = None
    for y in range(NB):
        k, t = ks[y], ts[y]
        low = jnp.where(lane > 0, face(k, shift(k, 1, 1)), 0.0)
        flux = low * (t - shift(t, 1, 1))
        total = shift(flux, -1, 1) - flux
        face_z = jnp.where(row > 0, face(k, before(k)), 0.0)
        flux = face_z * (t - before(t))
        total = total + (after(flux) - flux)
        if y > 0:
            total = total - flux_y
        if y < NB - 1:
            next_face = face(ks[y + 1], k)
            faces_ref[y] = next_face
            flux_y = next_face * (ts[y + 1] - t)
            total = total + flux_y
        inner_ref[y] = total

        ones = [jnp.ones((LANES, NX), jnp.float32)] * ZC
        plan, leak, over, couple = fold(ones, split(after(face_z)), chunk == LANES - 1)
        put_plan(z_plan_ref, (y,), plan)
        over = shift(over, 1, 0)
        leak_end = over[:1]
        leak = leak + jnp.where(chunk > 0, over, 0.0)
        low = shift(couple, 1, 0)
        at_first = jnp.where(chunk == 1, low, 0.0)
        at_last = jnp.where(chunk == LANES - 1, couple, 0.0)
        factors = separator_factors(leak + at_first + at_last, jnp.where(chunk > 1, low, 0.0),
                                    jnp.where((chunk > 0) & (chunk < LANES - 1), couple, 0.0))
        for j, factor in enumerate(factors):
            z_ends_ref[y, j] = factor
        lam = jnp.where(chunk == 0, 1.0, separator_solve(factors, at_first))
        rho = separator_solve(factors, at_last)
        coeffs_ref[0, y:y + 1] = jnp.sum(lam * leak, axis=0, keepdims=True)
        coeffs_ref[1, y:y + 1] = jnp.sum(rho * leak, axis=0, keepdims=True) + leak_end
        coeffs_ref[2, y:y + 1] = couple[LANES - 1:] * lam[LANES - 1:]
        following = jnp.where(chunk == LANES - 1, 0.0, shift(lam, -1, 0))
        spikes_ref[0, y] = jnp.concatenate(unfold(plan, None, lam, following), axis=0)
        following = jnp.where(chunk == LANES - 1, 1.0, shift(rho, -1, 0))
        spikes_ref[1, y] = jnp.concatenate(unfold(plan, None, rho, following), axis=0)

    for h in range(NB // 2):
        turned[h] = jnp.concatenate(ks[2 * h:2 * h + 2], axis=0).T
        k = block_line(turned, h)
        couples = face(k, after(k))
        couples = jnp.where((rows_of(couples.shape, 0) == NX - 1), 0.0, couples)
        ones = [jnp.ones((LANES, 2 * NZB), jnp.float32)] * XC
        plan, leak, over, couple = fold(ones, split(couples))
        put_plan(x_plan_ref, (h,), plan)
        factors = separator_factors(leak + shift(over, 1, 0), shift(couple, 1, 0), couple)
        for j, factor in enumerate(factors):
            x_ends_ref[h, j] = factor


def block_line(ref, h):
    return chunked(lambda rows: ref[h, rows, :], XC)


def first_kernel(t_ref, k_ref, inner_ref, faces_ref, x_plan_ref, x_ends_ref, across_ref, inside_ref, zp_ref, zn_ref,
                 bundle_ref, back_ref, top_ref, turned):
    gy = lax.axis_index("gy")
    zg = lax.axis_index("zg")
    odd = lax.rem(gy, 2) == 1
    across = [block_row(across_ref, j) for j in range(2)]
    inside = [block_row(inside_ref, j) for j in range(2)]
    yp = [jnp.where(odd, b, a) for a, b in zip(across, inside)]
    yn = [jnp.where(odd, a, b) for a, b in zip(across, inside)]
    has_south = jnp.where(gy > 0, 1.0, 0.0)
    has_north = jnp.where(gy < NGY - 1, 1.0, 0.0)
    has_below = jnp.where(zg > 0, 1.0, 0.0)
    has_above = jnp.where(zg < NZG - 1, 1.0, 0.0)
    row = rows_of((NZB, NX), 0)
    sources = []
    g4 = None
    for y in range(NB):
        b = inner_ref[y]
        if y == 0:
            b = b + face(block_row(k_ref, y), yp[1] * has_south) * (yp[0] - block_row(t_ref, y))
        if y == NB - 1:
            g4 = face(block_row(k_ref, y), yn[1] * has_north)
            b = b + g4 * (yn[0] - block_row(t_ref, y))
        k_low, k_high = k_ref[y, :1], k_ref[y, NZB - 1:]
        below = face(k_low, zp_ref[1, y:y + 1] * has_below) * (zp_ref[0, y:y + 1] - t_ref[y, :1])
        top = face(k_high, zn_ref[1, y:y + 1] * has_above)
        top_ref[y:y + 1] = top
        above = top * (zn_ref[0, y:y + 1] - t_ref[y, NZB - 1:])
        b = b + jnp.where(row == 0, below, 0.0) + jnp.where(row == NZB - 1, above, 0.0)
        sources.append(b)
    solved = []
    for h in range(NB // 2):
        turned[h] = jnp.concatenate(sources[2 * h:2 * h + 2], axis=0).T
        plan = get_plan(x_plan_ref, (h,), XC)
        b, over = fold_sources(plan, split(block_line(turned, h)))
        head = separator_solve([x_ends_ref[h, j] for j in range(2 * len(STRIDES) + 1)], b[0] + shift(over, 1, 0))
        for a, x in enumerate(unfold(plan, b, head, shift(head, -1, 0))):
            turned[h, pl.ds(a, LANES, stride=XC), :] = x
        b = turned[h].T
        solved += [b[:NZB], b[NZB:]]
    b0, b1, b2, b3 = solved
    g1, g2, g3 = faces_ref[0], faces_ref[1], faces_ref[2]
    i1 = 1.0 / (1.0 + g1 + g2)
    left, right = g1 * i1, g2 * i1
    source = b0 + left * b1
    b2 = b2 + right * b1
    leak = 1.0 + left
    m2 = 1.0 + right
    a2 = g1 * right
    i2 = 1.0 / (m2 + a2 + g3)
    left, right = a2 * i2, g3 * i2
    source = source + left * b2
    b3 = b3 + right * b2
    leak = leak + left * m2
    m3 = 1.0 + right * m2
    a3 = a2 * right
    i3 = 1.0 / (m3 + a3 + g4)
    left, right = a3 * i3, g4 * i3

    def put(v, x):
        for a, part in enumerate(split(x)):
            bundle_ref[pl.ds(VALUES * a + v, LANES, stride=VALUES * ZC), :] = part

    put(0, leak + left * m3)
    put(1, right * m3)
    put(2, a3 * right)
    put(3, source + left * b3)
    put(4, right * b3)
    beta, lam, rho = b3 * i3, left, right
    back_ref[0, 2], back_ref[1, 2], back_ref[2, 2] = beta, lam, rho
    beta, lam, rho = (b2 + g3 * beta) * i2, (a2 + g3 * lam) * i2, g3 * rho * i2
    back_ref[0, 1], back_ref[1, 1], back_ref[2, 1] = beta, lam, rho
    beta, lam, rho = (b1 + g2 * beta) * i1, (g1 + g2 * lam) * i1, g2 * rho * i1
    back_ref[0, 0], back_ref[1, 0], back_ref[2, 0] = beta, lam, rho


def column_kernel(bundle_ref, out_ref):
    get = lambda v: [bundle_ref[pl.ds(VALUES * a + v, LANES, stride=VALUES * YC), :] for a in range(YC)]
    joined = lambda own, pushed: split(jnp.concatenate(own, axis=0) + before(jnp.concatenate(pushed, axis=0)))
    plan, leak, over, couple = fold(joined(get(0), get(1)), get(2))
    b, over_source = fold_sources(plan, joined(get(3), get(4)))
    factors = separator_factors(leak + shift(over, 1, 0), shift(couple, 1, 0), couple)
    head = separator_solve(factors, b[0] + shift(over_source, 1, 0))
    following = shift(head, -1, 0)
    x = unfold(plan, b, head, following) + [following]
    for a in range(YC):
        out_ref[pl.ds(2 * a, LANES, stride=2 * YC), :] = x[a]
        out_ref[pl.ds(2 * a + 1, LANES, stride=2 * YC), :] = x[a + 1]


def second_kernel(ends_ref, back_ref, spikes_ref, coeffs_ref, top_ref, second_ref, sums_ref, last_row_ref):
    get = lambda v: jnp.concatenate(
        [ends_ref[pl.ds(2 * a + v, LANES, stride=2 * ZC), :] for a in range(ZC)], axis=0)
    own, following = get(0), get(1)
    firsts, lasts = [], []
    for y in range(NB):
        if y == 0:
            u = own
        else:
            u = back_ref[0, y - 1] + back_ref[1, y - 1] * own + back_ref[2, y - 1] * following
        second_ref[y] = u
        firsts.append(jnp.sum(spikes_ref[0, y] * u, axis=0, keepdims=True))
        lasts.append(jnp.sum(spikes_ref[1, y] * u, axis=0, keepdims=True))
    first, last = jnp.concatenate(firsts, axis=0), jnp.concatenate(lasts, axis=0)
    leak, couple, top = coeffs_ref[1], coeffs_ref[2], top_ref[...]
    inverse = 1.0 / (leak + couple + top)
    left, right = couple * inverse, top * inverse
    sums_ref[0] = coeffs_ref[0] + left * leak
    sums_ref[1] = right * leak
    sums_ref[2] = left * top
    sums_ref[3] = first + left * last
    sums_ref[4] = right * last
    last_row_ref[0] = last * inverse
    last_row_ref[1] = left
    last_row_ref[2] = right


def local_z_kernel(second_ref, z_plan_ref, z_ends_ref, t_ref, out_ref):
    chunk = rows_of((LANES, NX), 0)
    for y in range(NB):
        plan = get_plan(z_plan_ref, (y,), ZC)
        b, over = fold_sources(plan, split(second_ref[y]))
        b0 = jnp.where(chunk > 0, b[0] + shift(over, 1, 0), 0.0)
        head = separator_solve([z_ends_ref[y, j] for j in range(2 * len(STRIDES) + 1)], b0)
        following = jnp.where(chunk == LANES - 1, 0.0, shift(head, -1, 0))
        x = jnp.concatenate(unfold(plan, b, head, following), axis=0)
        out_ref[y] = block_row(t_ref, y) + x


def last_kernel(local_ref, spikes_ref, last_row_ref, e0_ref, e1_ref, e2_ref, e3_ref, out_ref, line, ends):
    zg = lax.axis_index("zg")
    for j, e_ref in enumerate((e0_ref, e1_ref, e2_ref, e3_ref)):
        line[lax.rem(zg + (NZG - j), NZG)] = e_ref[...]
    inverses, sources = [], []
    leak, source = line[0, 0], line[0, 3]
    for d in range(NZG):
        couple = line[d, 2]
        inverse = 1.0 / (leak + couple)
        inverses.append(inverse)
        sources.append(source)
        if d + 1 < NZG:
            passed = couple * inverse
            leak = line[d + 1, 0] + line[d, 1] + passed * leak
            source = line[d + 1, 3] + line[d, 4] + passed * source
    value = jnp.zeros_like(source)
    ends[NZG] = value
    for d in reversed(range(NZG)):
        value = (sources[d] + line[d, 2] * value) * inverses[d]
        ends[d] = value
    own = ends[zg]
    following = last_row_ref[0] + last_row_ref[1] * own + last_row_ref[2] * ends[zg + 1]
    for y in range(NB):
        x = local_ref[y] + spikes_ref[0, y] * own[y:y + 1] + spikes_ref[1, y] * following[y:y + 1]
        for a, part in enumerate(split(x)):
            out_ref[y, pl.ds(a, LANES, stride=ZC), :] = part


def call(kernel, name, outs, args, scratch=(), cost=2000000, granted=0):
    shapes = [jax.ShapeDtypeStruct(o, jnp.float32) for o in outs]
    vmem = pl.BlockSpec(memory_space=pltpu.VMEM)
    return pl.pallas_call(
        kernel,
        name=name,
        out_shape=shapes,
        in_specs=[pl.BlockSpec(memory_space=pltpu.HBM)] * len(args) if granted else [vmem] * len(args),
        out_specs=[vmem] * len(outs),
        scratch_shapes=scratch,
        cost_estimate=pl.CostEstimate(flops=cost, bytes_accessed=cost, transcendentals=0),
        compiler_params=pltpu.CompilerParams(vmem_limit_bytes=(granted or 24576) * 1024),
    )(*args)


def around(x, axis, by):
    count = lax.axis_size(axis)
    return lax.ppermute(x, axis, [(i, (i + by) % count) for i in range(count)])


def swapped(x, axis, first):
    count = lax.axis_size(axis)
    return lax.ppermute(x, axis, [(i, (((i - first) ^ 1) + first) % count) for i in range(count)])


def shards(t, k):
    block = (NB, NZB, NX)
    t, k, across, inside, zp, zn = call(
        load_kernel, "load", [block, block, (2, NZB, NX), (2, NZB, NX), (2, NB, NX), (2, NB, NX)], [t, k],
        scratch=[pltpu.SemaphoreType.DMA((2,))], granted=LOAD_GRANT)
    across = swapped(across, "gy", 1)
    zp = around(zp, "zg", 1)
    zn = around(zn, "zg", -1)
    inside = swapped(inside, "gy", 0)
    turned = pltpu.VMEM((NB // 2, NX, 2 * NZB), jnp.float32)
    ends = (2 * len(STRIDES) + 1, LANES, NX)
    inner, faces, x_plan, x_ends, z_plan, z_ends, spikes, coeffs = call(
        inner_kernel, "inner",
        [block, (NB - 1, NZB, NX), (NB // 2, XC - 1, 3, LANES, 2 * NZB), (NB // 2,) + ends,
         (NB, ZC - 1, 3, LANES, NX), (NB,) + ends, (2,) + block, (3, NB, NX)], [t, k], scratch=[turned])
    bundle, back, top = call(
        first_kernel, "first", [(NZB * VALUES, NX), (3, NB - 1, NZB, NX), (NB, NX)],
        [t, k, inner, faces, x_plan, x_ends, across, inside, zp, zn], scratch=[turned])
    columns = lax.all_to_all(bundle.reshape(NZB * VALUES, 1, NX), "gy", split_axis=0, concat_axis=0, tiled=True)
    (ends,) = call(column_kernel, "column", [(2 * NGY, NX)], [columns.reshape(NGY * VALUES, NX)])
    ends = lax.all_to_all(ends, "gy", split_axis=0, concat_axis=0, tiled=True)
    second, sums, last_row = call(
        second_kernel, "second", [block, (5, NB, NX), (3, NB, NX)], [ends, back, spikes, coeffs, top])
    sums = [sums] + [around(sums, "zg", j) for j in range(1, NZG)]
    (local,) = call(local_z_kernel, "local_z", [block], [second, z_plan, z_ends, t])
    (out,) = call(last_kernel, "last", [block], [local, spikes, last_row] + sums,
                  scratch=[pltpu.VMEM((NZG, 5, NB, NX), jnp.float32), pltpu.VMEM((NZG + 1, NB, NX), jnp.float32)])
    return out


def solution(mesh):
    return jax.shard_map(
        shards,
        mesh=mesh,
        in_specs=(P("gy", "zg", None), P("gy", "zg", None)),
        out_specs=P("gy", "zg", None),
        check_vma=False,
    )
```

time: 56 us -> 54.2 us (0.968)
  blocking collectives: 38.9 us -> 31.5 us
  starting transfers between devices: 9.52 us -> 15.4 us
  Pallas kernels: 4.14 us -> 2.87 us
  waiting for transfers between devices: 3.29 us -> 4.16 us
    ppermute x0 -> x2, starting transfers between devices: none -> 9.34 us  [swapped(): lax.ppermute(x, axis, [(i, ((i - first ^ 1) + first) % count) for i in ra...]
    all_to_all x1, blocking collectives: 23.9 us -> 16.6 us  [shards(): lax.all_to_all(bundle.reshape(NZB * VALUES, 1, NX), 'gy', split_axis=0, c...]
    ppermute x7 -> x5, starting transfers between devices: 9.52 us -> 6.11 us  [around(): return lax.ppermute(x, axis, [(i, (i + by) % count) for i in range(count)])]
    pallas_call x7, Pallas kernels: 4.14 us -> 2.87 us  [call(): pl.pallas_call(kernel, name=name, out_shape=shapes, in_specs=[pl.BlockSpe...]
    ppermute x7 -> x5, waiting for transfers between devices: 3.29 us -> 4.16 us  [around(): return lax.ppermute(x, axis, [(i, (i + by) % count) for i in range(count)])]
  transfers between devices with their start and end apart: 7 -> 7, of which waited for: 2 -> 4; matrix products, arithmetic and copies ran while one was open for 0% -> 0% of each run, Pallas kernels for 3% -> 1%
where the time goes in v5:
time: 54.2 us; the launch traced here: 54 us
  blocking collectives  31.5 us (58%)
  starting transfers between devices  15.4 us (28%)
  waiting for transfers between devices  4.16 us (8%)
  Pallas kernels  2.87 us (5%)
    all_to_all x1, blocking collectives, shards(): lax.all_to_all(bundle.reshape(NZB * VALUES, 1, NX), 'gy', split_axis=0, c...  16.6 us
    all_to_all x1, blocking collectives, shards(): ends = lax.all_to_all(ends, 'gy', split_axis=0, concat_axis=0, tiled=True)  14.9 us
    ppermute x2, starting transfers between devices, swapped(): lax.ppermute(x, axis, [(i, ((i - first ^ 1) + first) % count) for i in ra...  9.34 us
    ppermute x5, starting transfers between devices, around(): return lax.ppermute(x, axis, [(i, (i + by) % count) for i in range(count)])  6.11 us
    ppermute x5, waiting for transfers between devices, around(): return lax.ppermute(x, axis, [(i, (i + by) % count) for i in range(count)])  4.16 us
    pallas_call x7, Pallas kernels, call(): pl.pallas_call(kernel, name=name, out_shape=shapes, in_specs=[pl.BlockSpe...  2.87 us
  transfers between devices with their start and end apart: 7, of which 4 were waited for; matrix products, arithmetic and copies ran while one was open for 0% of the time, Pallas kernels for 1%

profile of v5, /device:TPU:1, one launch (start us, length us, event | category | flops | bytes accessed | tf_op | source)
XLA Modules:
  0.0 54.0 jit_solution(4502620525903945833)
XLA Ops:
  0.0 1.0 %load.1 = (f32[4,64,128]{2,1,0:T(8,128)S(1)}, f32[4,64,128]{2,1,0:T(8,128)S(1)}, f32[2,64,128]{2,1,0:T(8,128)S(1)}, f32[2,64,128]{2,1,0:T(8,128)S(1)}, f32[2,4,1...) custom-call(f32[4,64,128]{2,1,0:T(8,128)} %t_hbm.1, f32[4,64,128]{2,1,0:T(8,128)} %k_hbm.1), custom_call_target="tpu_custom_call" | custom-call | flops 2000000 | bytes 2000000 | tf_op jit(solution)/shard_map/load/pallas_call | solution.py:372
  1.0 3.1 %collective-permute-start = (f32[2,64,128]{2,1,0:T(8,128)S(1)}, f32[2,64,128]{2,1,0:T(8,128)S(1)}, u32[]{:S(2)}, u32[]{:S(2)}) collective-permute-start(f32[2,64,128]{2,1,0:T(8,128)S(1)} %get-tuple-element.31), channel_id=1, source_target_pairs={{0,63},{1,2},{2,1},{3,4},{4,3},{5,6},{6,5},{7,8},{8,7},{9,10},{10,... | collective-permute-start | bytes 196616 | tf_op jit(solution)/shard_map/ppermute | solution.py:391
  4.1 6.2 %collective-permute-start.1 = (f32[2,64,128]{2,1,0:T(8,128)S(1)}, f32[2,64,128]{2,1,0:T(8,128)S(1)}, u32[]{:S(2)}, u32[]{:S(2)}) collective-permute-start(f32[2,64,128]{2,1,0:T(8,128)S(1)} %get-tuple-element.32), channel_id=1, source_target_pairs={{0,1},{1,0},{2,3},{3,2},{4,5},{5,4},{6,7},{7,6},{8,9},{9,8},{10,11... | collective-permute-start | bytes 196616 | tf_op jit(solution)/shard_map/ppermute | solution.py:391
  10.3 1.2 %collective-permute-start.2 = (f32[2,4,128]{2,1,0:T(4,128)S(1)}, f32[2,4,128]{2,1,0:T(4,128)S(1)}, u32[]{:S(2)}, u32[]{:S(2)}) collective-permute-start(f32[2,4,128]{2,1,0:T(4,128)S(1)} %get-tuple-element.33), channel_id=1, source_target_pairs={{0,64},{64,128},{128,192},{192,0},{1,65},{65,129},{129,193},{193,1... | collective-permute-start | bytes 12296 | tf_op jit(solution)/shard_map/ppermute | solution.py:386
  11.5 1.5 %collective-permute-start.3 = (f32[2,4,128]{2,1,0:T(4,128)S(1)}, f32[2,4,128]{2,1,0:T(4,128)S(1)}, u32[]{:S(2)}, u32[]{:S(2)}) collective-permute-start(f32[2,4,128]{2,1,0:T(4,128)S(1)} %get-tuple-element.34), channel_id=1, source_target_pairs={{0,192},{64,0},{128,64},{192,128},{1,193},{65,1},{129,65},{193,129... | collective-permute-start | bytes 12296 | tf_op jit(solution)/shard_map/ppermute | solution.py:386
  13.0 0.5 inner.1
  13.5 0.5 collective-permute-done.2.zp_ref
  14.0 0.3 collective-permute-done.3.zn_ref
  14.3 0.0 collective-permute-done.across_ref
  14.3 0.0 collective-permute-done.1.inside_ref
  14.3 0.4 first.1
  14.7 16.6 %all_to_all.16 = f32[320,1,128]{2,1,0:T(1,128)S(1)} all-to-all(f32[320,1,128]{2,1,0:T(1,128)S(1)} %bitcast.9), channel_id=1, replica_groups=mesh['zg'=4,'gy'=64] {'gy'}, dimensions={0} | all-to-all | bytes 327680 | tf_op jit(solution)/shard_map/all_to_all | solution.py:412
  31.2 0.1 column.1
  31.4 14.9 %all_to_all.17 = f32[64,2,128]{2,1,0:T(2,128)S(1)} all-to-all(f32[64,2,128]{2,1,0:T(2,128)S(1)} %bitcast.8), channel_id=1, replica_groups=mesh['zg'=4,'gy'=64] {'gy'}, dimensions={0} | all-to-all | bytes 131072 | tf_op jit(solution)/shard_map/all_to_all | solution.py:414
  46.3 0.1 second.1
  46.4 2.8 %collective-permute-start.6 = (f32[5,4,128]{2,1,0:T(4,128)S(1)}, f32[5,4,128]{2,1,0:T(4,128)S(1)}, u32[]{:S(2)}, u32[]{:S(2)}) collective-permute-start(f32[5,4,128]{2,1,0:T(4,128)S(1)} %get-tuple-element.44.e0_ref), channel_id=1, source_target_pairs={{0,192},{64,0},{128,64},{192,128},{1,193},{65,1},{129,65},{193,129... | collective-permute-start | bytes 30728 | tf_op jit(solution)/shard_map/ppermute | solution.py:386
  49.1 0.3 collective-permute-start.5
  49.5 0.4 collective-permute-start.4
  49.8 0.1 local_z.1.local_ref
  49.9 0.0 collective-permute-done.6.e3_ref
  49.9 3.2 %collective-permute-done.5.e2_ref = f32[5,4,128]{2,1,0:T(4,128)S(1)} collective-permute-done((f32[5,4,128]{2,1,0:T(4,128)S(1)}, f32[5,4,128]{2,1,0:T(4,128)S(1)}, u32[]{:S(2)}, u32[]{:S(2)}) %collective-permute-start.5) | collective-permute-done | bytes 10272 | tf_op jit(solution)/shard_map/ppermute | solution.py:386
  53.2 0.1 collective-permute-done.4.e1_ref
  53.3 0.8 %last.1 = f32[4,64,128]{2,1,0:T(8,128)} custom-call(f32[4,64,128]{2,1,0:T(8,128)S(1)} %local_z.1.local_ref, f32[2,4,64,128]{3,2,1,0:T(8,128)S(1)} %get-tuple-element.37.spikes_ref, f32[3,4,128]{2,1,0:T(4,128)S(1)} %get-tuple-element.43.last_row_ref, f32[5,4,128]{2,1,0:T(4,128)S(1)} %get-tuple-element.44.e0_ref, ...), custom_call_target="tpu_custom_call" | custom-call | flops 2000000 | bytes 2000000 | tf_op jit(solution)/shard_map/last/pallas_call | solution.py:372
Async XLA Ops:
  1.0 13.3 %collective-permute-start = (f32[2,64,128]{2,1,0:T(8,128)S(1)}, f32[2,64,128]{2,1,0:T(8,128)S(1)}, u32[]{:S(2)}, u32[]{:S(2)}) collective-permute-start(f32[2,64,128]{2,1,0:T(8,128)S(1)} %get-tuple-element.31), channel_id=1, source_target_pairs={{0,63},{1,2},{2,1},{3,4},{4,3},{5,6},{6,5},{7,8},{8,7},{9,10},{10,... | collective-permute-start | bytes 196616 | tf_op jit(solution)/shard_map/ppermute | solution.py:391
  4.1 10.2 %collective-permute-start.1 = (f32[2,64,128]{2,1,0:T(8,128)S(1)}, f32[2,64,128]{2,1,0:T(8,128)S(1)}, u32[]{:S(2)}, u32[]{:S(2)}) collective-permute-start(f32[2,64,128]{2,1,0:T(8,128)S(1)} %get-tuple-element.32), channel_id=1, source_target_pairs={{0,1},{1,0},{2,3},{3,2},{4,5},{5,4},{6,7},{7,6},{8,9},{9,8},{10,11... | collective-permute-start | bytes 196616 | tf_op jit(solution)/shard_map/ppermute | solution.py:391
  10.3 3.7 %collective-permute-start.2 = (f32[2,4,128]{2,1,0:T(4,128)S(1)}, f32[2,4,128]{2,1,0:T(4,128)S(1)}, u32[]{:S(2)}, u32[]{:S(2)}) collective-permute-start(f32[2,4,128]{2,1,0:T(4,128)S(1)} %get-tuple-element.33), channel_id=1, source_target_pairs={{0,64},{64,128},{128,192},{192,0},{1,65},{65,129},{129,193},{193,1... | collective-permute-start | bytes 12296 | tf_op jit(solution)/shard_map/ppermute | solution.py:386
  11.5 2.8 %collective-permute-start.3 = (f32[2,4,128]{2,1,0:T(4,128)S(1)}, f32[2,4,128]{2,1,0:T(4,128)S(1)}, u32[]{:S(2)}, u32[]{:S(2)}) collective-permute-start(f32[2,4,128]{2,1,0:T(4,128)S(1)} %get-tuple-element.34), channel_id=1, source_target_pairs={{0,192},{64,0},{128,64},{192,128},{1,193},{65,1},{129,65},{193,129... | collective-permute-start | bytes 12296 | tf_op jit(solution)/shard_map/ppermute | solution.py:386
  46.4 3.6 %collective-permute-start.6 = (f32[5,4,128]{2,1,0:T(4,128)S(1)}, f32[5,4,128]{2,1,0:T(4,128)S(1)}, u32[]{:S(2)}, u32[]{:S(2)}) collective-permute-start(f32[5,4,128]{2,1,0:T(4,128)S(1)} %get-tuple-element.44.e0_ref), channel_id=1, source_target_pairs={{0,192},{64,0},{128,64},{192,128},{1,193},{65,1},{129,65},{193,129... | collective-permute-start | bytes 30728 | tf_op jit(solution)/shard_map/ppermute | solution.py:386
  49.1 4.0 %collective-permute-start.5 = (f32[5,4,128]{2,1,0:T(4,128)S(1)}, f32[5,4,128]{2,1,0:T(4,128)S(1)}, u32[]{:S(2)}, u32[]{:S(2)}) collective-permute-start(f32[5,4,128]{2,1,0:T(4,128)S(1)} %get-tuple-element.44.e0_ref), channel_id=1, source_target_pairs={{0,128},{64,192},{128,0},{192,64},{1,129},{65,193},{129,1},{193,65... | collective-permute-start | bytes 30728 | tf_op jit(solution)/shard_map/ppermute | solution.py:386
  49.5 3.8 %collective-permute-start.4 = (f32[5,4,128]{2,1,0:T(4,128)S(1)}, f32[5,4,128]{2,1,0:T(4,128)S(1)}, u32[]{:S(2)}, u32[]{:S(2)}) collective-permute-start(f32[5,4,128]{2,1,0:T(4,128)S(1)} %get-tuple-element.44.e0_ref), channel_id=1, source_target_pairs={{0,64},{64,128},{128,192},{192,0},{1,65},{65,129},{129,193},{193,1... | collective-permute-start | bytes 30728 | tf_op jit(solution)/shard_map/ppermute | solution.py:386

commit v6 on v5

--- a/solution.py
+++ b/solution.py
@@ -126,8 +126,9 @@
     return b * factors[2 * len(STRIDES)]
 
 
-def load_kernel(t_hbm, k_hbm, t_ref, k_ref, across_ref, inside_ref, zp_ref, zn_ref, sems):
+def load_kernel(t_hbm, k_hbm, t_ref, k_ref, across_ref, inside_ref, z_even_ref, z_odd_ref, sems):
     odd = lax.rem(lax.axis_index("gy"), 2)
+    upper = lax.rem(lax.axis_index("zg"), 2) == 1
     copies = [pltpu.make_async_copy(t_hbm, t_ref, sems.at[0]), pltpu.make_async_copy(k_hbm, k_ref, sems.at[1])]
     for copy in copies:
         copy.start()
@@ -136,8 +137,9 @@
         across_ref[j] = ref[odd * (NB - 1)]
         inside_ref[j] = ref[(1 - odd) * (NB - 1)]
         for y in range(NB):
-            zp_ref[j, y:y + 1] = ref[y, NZB - 1:]
-            zn_ref[j, y:y + 1] = ref[y, :1]
+            first, last = ref[y, :1], ref[y, NZB - 1:]
+            z_even_ref[j, y:y + 1] = jnp.where(upper, first, last)
+            z_odd_ref[j, y:y + 1] = jnp.where(upper, last, first)
 
 
 def block_row(ref, *at):
@@ -209,7 +211,7 @@
     return chunked(lambda rows: ref[h, rows, :], XC)
 
 
-def first_kernel(t_ref, k_ref, inner_ref, faces_ref, x_plan_ref, x_ends_ref, across_ref, inside_ref, zp_ref, zn_ref,
+def first_kernel(t_ref, k_ref, inner_ref, faces_ref, x_plan_ref, x_ends_ref, across_ref, inside_ref, z_even_ref, z_odd_ref,
                  bundle_ref, back_ref, top_ref, turned):
     gy = lax.axis_index("gy")
     zg = lax.axis_index("zg")
@@ -218,6 +220,9 @@
     inside = [block_row(inside_ref, j) for j in range(2)]
     yp = [jnp.where(odd, b, a) for a, b in zip(across, inside)]
     yn = [jnp.where(odd, a, b) for a, b in zip(across, inside)]
+    upper = lax.rem(zg, 2) == 1
+    zp = jnp.where(upper, z_even_ref[...], z_odd_ref[...])
+    zn = jnp.where(upper, z_odd_ref[...], z_even_ref[...])
     has_south = jnp.where(gy > 0, 1.0, 0.0)
     has_north = jnp.where(gy < NGY - 1, 1.0, 0.0)
     has_below = jnp.where(zg > 0, 1.0, 0.0)
@@ -233,10 +238,10 @@
             g4 = face(block_row(k_ref, y), yn[1] * has_north)
             b = b + g4 * (yn[0] - block_row(t_ref, y))
         k_low, k_high = k_ref[y, :1], k_ref[y, NZB - 1:]
-        below = face(k_low, zp_ref[1, y:y + 1] * has_below) * (zp_ref[0, y:y + 1] - t_ref[y, :1])
-        top = face(k_high, zn_ref[1, y:y + 1] * has_above)
+        below = face(k_low, zp[1, y:y + 1] * has_below) * (zp[0, y:y + 1] - t_ref[y, :1])
+        top = face(k_high, zn[1, y:y + 1] * has_above)
         top_ref[y:y + 1] = top
-        above = top * (zn_ref[0, y:y + 1] - t_ref[y, NZB - 1:])
+        above = top * (zn[0, y:y + 1] - t_ref[y, NZB - 1:])
         b = b + jnp.where(row == 0, below, 0.0) + jnp.where(row == NZB - 1, above, 0.0)
         sources.append(b)
     solved = []
@@ -341,7 +346,7 @@
 def last_kernel(local_ref, spikes_ref, last_row_ref, e0_ref, e1_ref, e2_ref, e3_ref, out_ref, line, ends):
     zg = lax.axis_index("zg")
     for j, e_ref in enumerate((e0_ref, e1_ref, e2_ref, e3_ref)):
-        line[lax.rem(zg + (NZG - j), NZG)] = e_ref[...]
+        line[lax.bitwise_xor(zg, j)] = e_ref[...]
     inverses, sources = [], []
     leak, source = line[0, 0], line[0, 3]
     for d in range(NZG):
@@ -381,24 +386,24 @@
     )(*args)
 
 
-def around(x, axis, by):
-    count = lax.axis_size(axis)
-    return lax.ppermute(x, axis, [(i, (i + by) % count) for i in range(count)])
-
-
 def swapped(x, axis, first):
     count = lax.axis_size(axis)
-    return lax.ppermute(x, axis, [(i, (((i - first) ^ 1) + first) % count) for i in range(count)])
+    partner = lambda i: ((i - first) ^ 1) + first
+    return lax.ppermute(x, axis, [(i, partner(i) if 0 <= partner(i) < count else i) for i in range(count)])
+
+
+def crossed(x, axis, by):
+    return lax.ppermute(x, axis, [(i, i ^ by) for i in range(lax.axis_size(axis))])
 
 
 def shards(t, k):
     block = (NB, NZB, NX)
-    t, k, across, inside, zp, zn = call(
+    t, k, across, inside, z_even, z_odd = call(
         load_kernel, "load", [block, block, (2, NZB, NX), (2, NZB, NX), (2, NB, NX), (2, NB, NX)], [t, k],
         scratch=[pltpu.SemaphoreType.DMA((2,))], granted=LOAD_GRANT)
     across = swapped(across, "gy", 1)
-    zp = around(zp, "zg", 1)
-    zn = around(zn, "zg", -1)
+    z_odd = swapped(z_odd, "zg", 1)
+    z_even = swapped(z_even, "zg", 0)
     inside = swapped(inside, "gy", 0)
     turned = pltpu.VMEM((NB // 2, NX, 2 * NZB), jnp.float32)
     ends = (2 * len(STRIDES) + 1, LANES, NX)
@@ -408,13 +413,13 @@
          (NB, ZC - 1, 3, LANES, NX), (NB,) + ends, (2,) + block, (3, NB, NX)], [t, k], scratch=[turned])
     bundle, back, top = call(
         first_kernel, "first", [(NZB * VALUES, NX), (3, NB - 1, NZB, NX), (NB, NX)],
-        [t, k, inner, faces, x_plan, x_ends, across, inside, zp, zn], scratch=[turned])
+        [t, k, inner, faces, x_plan, x_ends, across, inside, z_even, z_odd], scratch=[turned])
     columns = lax.all_to_all(bundle.reshape(NZB * VALUES, 1, NX), "gy", split_axis=0, concat_axis=0, tiled=True)
     (ends,) = call(column_kernel, "column", [(2 * NGY, NX)], [columns.reshape(NGY * VALUES, NX)])
     ends = lax.all_to_all(ends, "gy", split_axis=0, concat_axis=0, tiled=True)
     second, sums, last_row = call(
         second_kernel, "second", [block, (5, NB, NX), (3, NB, NX)], [ends, back, spikes, coeffs, top])
-    sums = [sums] + [around(sums, "zg", j) for j in range(1, NZG)]
+    sums = [sums] + [crossed(sums, "zg", j) for j in range(1, NZG)]
     (local,) = call(local_z_kernel, "local_z", [block], [second, z_plan, z_ends, t])
     (out,) = call(last_kernel, "last", [block], [local, spikes, last_row] + sums,
                   scratch=[pltpu.VMEM((NZG, 5, NB, NX), jnp.float32), pltpu.VMEM((NZG + 1, NB, NX), jnp.float32)])

time: 54.2 us -> 56.5 us (1.042)
  blocking collectives: 31.5 us -> 37.7 us
  starting transfers between devices: 15.4 us -> 12.9 us
  waiting for transfers between devices: 4.16 us -> 2.52 us
    all_to_all x1, blocking collectives: 16.6 us -> 22.7 us  [shards(): lax.all_to_all(bundle.reshape(NZB * VALUES, 1, NX), 'gy', split_axis=0, c...]
    ppermute x7, starting transfers between devices: 15.4 us -> 12.9 us  [the longest x4 6.98 us: swapped(): lax.ppermute(x, axis, [(i, partner(i) if 0 <= partner(i) < count else i)...]
    ppermute x7, waiting for transfers between devices: 4.16 us -> 2.52 us  [the longest x3 2.42 us: crossed(): lax.ppermute(x, axis, [(i, i ^ by) for i in range(lax.axis_size(axis))])]
  transfers between devices with their start and end apart: 7 -> 7, of which waited for: 4 -> 3; matrix products, arithmetic and copies ran while one was open for 0% -> 0% of each run, Pallas kernels for 1% -> 1%
where the time goes in v6:
time: 56.5 us; the launch traced here: 56.1 us
  blocking collectives  37.7 us (67%)
  starting transfers between devices  12.9 us (23%)
  Pallas kernels  2.87 us (5%)
  waiting for transfers between devices  2.52 us (4%)
    all_to_all x1, blocking collectives, shards(): lax.all_to_all(bundle.reshape(NZB * VALUES, 1, NX), 'gy', split_axis=0, c...  22.7 us
    all_to_all x1, blocking collectives, shards(): ends = lax.all_to_all(ends, 'gy', split_axis=0, concat_axis=0, tiled=True)  14.9 us
    ppermute x4, starting transfers between devices, swapped(): lax.ppermute(x, axis, [(i, partner(i) if 0 <= partner(i) < count else i)...  6.98 us
    ppermute x3, starting transfers between devices, crossed(): lax.ppermute(x, axis, [(i, i ^ by) for i in range(lax.axis_size(axis))])  5.97 us
    pallas_call x7, Pallas kernels, call(): pl.pallas_call(kernel, name=name, out_shape=shapes, in_specs=[pl.BlockSpe...  2.87 us
    ppermute x3, waiting for transfers between devices, crossed(): lax.ppermute(x, axis, [(i, i ^ by) for i in range(lax.axis_size(axis))])  2.42 us
  transfers between devices with their start and end apart: 7, of which 3 were waited for; matrix products, arithmetic and copies ran while one was open for 0% of the time, Pallas kernels for 1%

profile of v6, /device:TPU:1, one launch (start us, length us, event | category | flops | bytes accessed | tf_op | source)
XLA Modules:
  0.0 56.1 jit_solution(9740751481050448586)
XLA Ops:
  0.0 1.0 %load.1 = (f32[4,64,128]{2,1,0:T(8,128)S(1)}, f32[4,64,128]{2,1,0:T(8,128)S(1)}, f32[2,64,128]{2,1,0:T(8,128)S(1)}, f32[2,64,128]{2,1,0:T(8,128)S(1)}, f32[2,4,1...) custom-call(f32[4,64,128]{2,1,0:T(8,128)} %t_hbm.1, f32[4,64,128]{2,1,0:T(8,128)} %k_hbm.1), custom_call_target="tpu_custom_call" | custom-call | flops 2000000 | bytes 2000000 | tf_op jit(solution)/shard_map/load/pallas_call | solution.py:377
  1.0 4.9 %collective-permute-start = (f32[2,64,128]{2,1,0:T(8,128)S(1)}, f32[2,64,128]{2,1,0:T(8,128)S(1)}, u32[]{:S(2)}, u32[]{:S(2)}) collective-permute-start(f32[2,64,128]{2,1,0:T(8,128)S(1)} %get-tuple-element.31), channel_id=1, source_target_pairs={{0,0},{1,2},{2,1},{3,4},{4,3},{5,6},{6,5},{7,8},{8,7},{9,10},{10,9... | collective-permute-start | bytes 196616 | tf_op jit(solution)/shard_map/ppermute | solution.py:392
  5.9 0.1 collective-permute-start.1
  6.0 1.3 %collective-permute-start.2 = (f32[2,4,128]{2,1,0:T(4,128)S(1)}, f32[2,4,128]{2,1,0:T(4,128)S(1)}, u32[]{:S(2)}, u32[]{:S(2)}) collective-permute-start(f32[2,4,128]{2,1,0:T(4,128)S(1)} %get-tuple-element.33), channel_id=1, source_target_pairs={{0,64},{64,0},{128,192},{192,128},{1,65},{65,1},{129,193},{193,129... | collective-permute-start | bytes 12296 | tf_op jit(solution)/shard_map/ppermute | solution.py:392
  7.3 0.6 %collective-permute-start.3 = (f32[2,4,128]{2,1,0:T(4,128)S(1)}, f32[2,4,128]{2,1,0:T(4,128)S(1)}, u32[]{:S(2)}, u32[]{:S(2)}) collective-permute-start(f32[2,4,128]{2,1,0:T(4,128)S(1)} %get-tuple-element.34), channel_id=1, source_target_pairs={{0,0},{64,128},{128,64},{192,192},{1,1},{65,129},{129,65},{193,193... | collective-permute-start | bytes 12296 | tf_op jit(solution)/shard_map/ppermute | solution.py:392
  8.0 0.5 inner.1
  8.5 0.1 collective-permute-done.2.z_even_ref
  8.6 0.0 collective-permute-done.3.z_odd_ref
  8.6 0.0 collective-permute-done.across_ref
  8.6 0.0 collective-permute-done.1.inside_ref
  8.6 0.4 first.1
  9.0 22.7 %all_to_all.16 = f32[320,1,128]{2,1,0:T(1,128)S(1)} all-to-all(f32[320,1,128]{2,1,0:T(1,128)S(1)} %bitcast.9), channel_id=1, replica_groups=mesh['zg'=4,'gy'=64] {'gy'}, dimensions={0} | all-to-all | bytes 327680 | tf_op jit(solution)/shard_map/all_to_all | solution.py:417
  31.7 0.1 column.1
  31.8 14.9 %all_to_all.17 = f32[64,2,128]{2,1,0:T(2,128)S(1)} all-to-all(f32[64,2,128]{2,1,0:T(2,128)S(1)} %bitcast.8), channel_id=1, replica_groups=mesh['zg'=4,'gy'=64] {'gy'}, dimensions={0} | all-to-all | bytes 131072 | tf_op jit(solution)/shard_map/all_to_all | solution.py:419
  46.8 0.1 second.1
  46.8 2.6 %collective-permute-start.6 = (f32[5,4,128]{2,1,0:T(4,128)S(1)}, f32[5,4,128]{2,1,0:T(4,128)S(1)}, u32[]{:S(2)}, u32[]{:S(2)}) collective-permute-start(f32[5,4,128]{2,1,0:T(4,128)S(1)} %get-tuple-element.44.e0_ref), channel_id=1, source_target_pairs={{0,192},{64,128},{128,64},{192,0},{1,193},{65,129},{129,65},{193,1... | collective-permute-start | bytes 30728 | tf_op jit(solution)/shard_map/ppermute | solution.py:396
  49.4 3.4 %collective-permute-start.5 = (f32[5,4,128]{2,1,0:T(4,128)S(1)}, f32[5,4,128]{2,1,0:T(4,128)S(1)}, u32[]{:S(2)}, u32[]{:S(2)}) collective-permute-start(f32[5,4,128]{2,1,0:T(4,128)S(1)} %get-tuple-element.44.e0_ref), channel_id=1, source_target_pairs={{0,128},{64,192},{128,0},{192,64},{1,129},{65,193},{129,1},{193,65... | collective-permute-start | bytes 30728 | tf_op jit(solution)/shard_map/ppermute | solution.py:396
  52.8 0.0 collective-permute-start.4
  52.8 0.1 local_z.1.local_ref
  52.9 0.0 collective-permute-done.6.e3_ref
  52.9 1.0 %collective-permute-done.5.e2_ref = f32[5,4,128]{2,1,0:T(4,128)S(1)} collective-permute-done((f32[5,4,128]{2,1,0:T(4,128)S(1)}, f32[5,4,128]{2,1,0:T(4,128)S(1)}, u32[]{:S(2)}, u32[]{:S(2)}) %collective-permute-start.5) | collective-permute-done | bytes 10272 | tf_op jit(solution)/shard_map/ppermute | solution.py:396
  53.9 1.5 %collective-permute-done.4.e1_ref = f32[5,4,128]{2,1,0:T(4,128)S(1)} collective-permute-done((f32[5,4,128]{2,1,0:T(4,128)S(1)}, f32[5,4,128]{2,1,0:T(4,128)S(1)}, u32[]{:S(2)}, u32[]{:S(2)}) %collective-permute-start.4) | collective-permute-done | bytes 10272 | tf_op jit(solution)/shard_map/ppermute | solution.py:396
  55.3 0.8 %last.1 = f32[4,64,128]{2,1,0:T(8,128)} custom-call(f32[4,64,128]{2,1,0:T(8,128)S(1)} %local_z.1.local_ref, f32[2,4,64,128]{3,2,1,0:T(8,128)S(1)} %get-tuple-element.37.spikes_ref, f32[3,4,128]{2,1,0:T(4,128)S(1)} %get-tuple-element.43.last_row_ref, f32[5,4,128]{2,1,0:T(4,128)S(1)} %get-tuple-element.44.e0_ref, ...), custom_call_target="tpu_custom_call" | custom-call | flops 2000000 | bytes 2000000 | tf_op jit(solution)/shard_map/last/pallas_call | solution.py:377
Async XLA Ops:
  1.0 7.6 %collective-permute-start = (f32[2,64,128]{2,1,0:T(8,128)S(1)}, f32[2,64,128]{2,1,0:T(8,128)S(1)}, u32[]{:S(2)}, u32[]{:S(2)}) collective-permute-start(f32[2,64,128]{2,1,0:T(8,128)S(1)} %get-tuple-element.31), channel_id=1, source_target_pairs={{0,0},{1,2},{2,1},{3,4},{4,3},{5,6},{6,5},{7,8},{8,7},{9,10},{10,9... | collective-permute-start | bytes 196616 | tf_op jit(solution)/shard_map/ppermute | solution.py:392
  5.9 2.7 %collective-permute-start.1 = (f32[2,64,128]{2,1,0:T(8,128)S(1)}, f32[2,64,128]{2,1,0:T(8,128)S(1)}, u32[]{:S(2)}, u32[]{:S(2)}) collective-permute-start(f32[2,64,128]{2,1,0:T(8,128)S(1)} %get-tuple-element.32), channel_id=1, source_target_pairs={{0,1},{1,0},{2,3},{3,2},{4,5},{5,4},{6,7},{7,6},{8,9},{9,8},{10,11... | collective-permute-start | bytes 196616 | tf_op jit(solution)/shard_map/ppermute | solution.py:392
  6.0 2.5 %collective-permute-start.2 = (f32[2,4,128]{2,1,0:T(4,128)S(1)}, f32[2,4,128]{2,1,0:T(4,128)S(1)}, u32[]{:S(2)}, u32[]{:S(2)}) collective-permute-start(f32[2,4,128]{2,1,0:T(4,128)S(1)} %get-tuple-element.33), channel_id=1, source_target_pairs={{0,64},{64,0},{128,192},{192,128},{1,65},{65,1},{129,193},{193,129... | collective-permute-start | bytes 12296 | tf_op jit(solution)/shard_map/ppermute | solution.py:392
  7.3 1.2 %collective-permute-start.3 = (f32[2,4,128]{2,1,0:T(4,128)S(1)}, f32[2,4,128]{2,1,0:T(4,128)S(1)}, u32[]{:S(2)}, u32[]{:S(2)}) collective-permute-start(f32[2,4,128]{2,1,0:T(4,128)S(1)} %get-tuple-element.34), channel_id=1, source_target_pairs={{0,0},{64,128},{128,64},{192,192},{1,1},{65,129},{129,65},{193,193... | collective-permute-start | bytes 12296 | tf_op jit(solution)/shard_map/ppermute | solution.py:392
  46.8 6.1 %collective-permute-start.6 = (f32[5,4,128]{2,1,0:T(4,128)S(1)}, f32[5,4,128]{2,1,0:T(4,128)S(1)}, u32[]{:S(2)}, u32[]{:S(2)}) collective-permute-start(f32[5,4,128]{2,1,0:T(4,128)S(1)} %get-tuple-element.44.e0_ref), channel_id=1, source_target_pairs={{0,192},{64,128},{128,64},{192,0},{1,193},{65,129},{129,65},{193,1... | collective-permute-start | bytes 30728 | tf_op jit(solution)/shard_map/ppermute | solution.py:396
  49.4 4.5 %collective-permute-start.5 = (f32[5,4,128]{2,1,0:T(4,128)S(1)}, f32[5,4,128]{2,1,0:T(4,128)S(1)}, u32[]{:S(2)}, u32[]{:S(2)}) collective-permute-start(f32[5,4,128]{2,1,0:T(4,128)S(1)} %get-tuple-element.44.e0_ref), channel_id=1, source_target_pairs={{0,128},{64,192},{128,0},{192,64},{1,129},{65,193},{129,1},{193,65... | collective-permute-start | bytes 30728 | tf_op jit(solution)/shard_map/ppermute | solution.py:396
  52.8 2.5 %collective-permute-start.4 = (f32[5,4,128]{2,1,0:T(4,128)S(1)}, f32[5,4,128]{2,1,0:T(4,128)S(1)}, u32[]{:S(2)}, u32[]{:S(2)}) collective-permute-start(f32[5,4,128]{2,1,0:T(4,128)S(1)} %get-tuple-element.44.e0_ref), channel_id=1, source_target_pairs={{0,64},{64,0},{128,192},{192,128},{1,65},{65,1},{129,193},{193,129... | collective-permute-start | bytes 30728 | tf_op jit(solution)/shard_map/ppermute | solution.py:396

commit v7 on v6

--- a/solution.py
+++ b/solution.py
@@ -346,7 +346,7 @@
 def last_kernel(local_ref, spikes_ref, last_row_ref, e0_ref, e1_ref, e2_ref, e3_ref, out_ref, line, ends):
     zg = lax.axis_index("zg")
     for j, e_ref in enumerate((e0_ref, e1_ref, e2_ref, e3_ref)):
-        line[lax.bitwise_xor(zg, j)] = e_ref[...]
+        line[lax.rem(zg + (NZG - j), NZG)] = e_ref[...]
     inverses, sources = [], []
     leak, source = line[0, 0], line[0, 3]
     for d in range(NZG):
@@ -387,13 +387,22 @@
 
 
 def swapped(x, axis, first):
+    pairs = []
+    for zg in range(NZG):
+        for gy in range(NGY):
+            place, count = (zg, NZG) if axis == "zg" else (gy, NGY)
+            partner = ((place - first) ^ 1) + first
+            if not 0 <= partner < count:
+                target = (zg, gy ^ 1) if axis == "zg" else (zg ^ 1, gy)
+            else:
+                target = (partner, gy) if axis == "zg" else (zg, partner)
+            pairs.append((zg * NGY + gy, target[0] * NGY + target[1]))
+    return lax.ppermute(x, ("zg", "gy"), pairs)
+
+
+def around(x, axis, by):
     count = lax.axis_size(axis)
-    partner = lambda i: ((i - first) ^ 1) + first
-    return lax.ppermute(x, axis, [(i, partner(i) if 0 <= partner(i) < count else i) for i in range(count)])
-
-
-def crossed(x, axis, by):
-    return lax.ppermute(x, axis, [(i, i ^ by) for i in range(lax.axis_size(axis))])
+    return lax.ppermute(x, axis, [(i, (i + by) % count) for i in range(count)])
 
 
 def shards(t, k):
@@ -419,7 +428,7 @@
     ends = lax.all_to_all(ends, "gy", split_axis=0, concat_axis=0, tiled=True)
     second, sums, last_row = call(
         second_kernel, "second", [block, (5, NB, NX), (3, NB, NX)], [ends, back, spikes, coeffs, top])
-    sums = [sums] + [crossed(sums, "zg", j) for j in range(1, NZG)]
+    sums = [sums] + [around(sums, "zg", j) for j in range(1, NZG)]
     (local,) = call(local_z_kernel, "local_z", [block], [second, z_plan, z_ends, t])
     (out,) = call(last_kernel, "last", [block], [local, spikes, last_row] + sums,
                   scratch=[pltpu.VMEM((NZG, 5, NB, NX), jnp.float32), pltpu.VMEM((NZG + 1, NB, NX), jnp.float32)])

time: 56.5 us -> 54 us (0.956)
  starting transfers between devices: 12.9 us -> 10.1 us
  waiting for transfers between devices: 2.52 us -> 3.57 us
    ppermute x7, starting transfers between devices: 12.9 us -> 10.1 us  [the longest x4 5.36 us: swapped(): return lax.ppermute(x, ('zg', 'gy'), pairs)]
    ppermute x7, waiting for transfers between devices: 2.52 us -> 3.57 us  [the longest x3 3.18 us: around(): return lax.ppermute(x, axis, [(i, (i + by) % count) for i in range(count)])]
  transfers between devices with their start and end apart: 7 -> 7, of which waited for: 3 -> 4; matrix products, arithmetic and copies ran while one was open for 0% -> 0% of each run, Pallas kernels for 1% -> 1%
where the time goes in v7:
time: 54 us; the launch traced here: 53.8 us
  blocking collectives  37.2 us (69%)
  starting transfers between devices  10.1 us (19%)
  waiting for transfers between devices  3.57 us (7%)
  Pallas kernels  2.87 us (5%)
    all_to_all x1, blocking collectives, shards(): lax.all_to_all(bundle.reshape(NZB * VALUES, 1, NX), 'gy', split_axis=0, c...  22.3 us
    all_to_all x1, blocking collectives, shards(): ends = lax.all_to_all(ends, 'gy', split_axis=0, concat_axis=0, tiled=True)  14.9 us
    ppermute x4, starting transfers between devices, swapped(): return lax.ppermute(x, ('zg', 'gy'), pairs)  5.36 us
    ppermute x3, starting transfers between devices, around(): return lax.ppermute(x, axis, [(i, (i + by) % count) for i in range(count)])  4.72 us
    ppermute x3, waiting for transfers between devices, around(): return lax.ppermute(x, axis, [(i, (i + by) % count) for i in range(count)])  3.18 us
    pallas_call x7, Pallas kernels, call(): pl.pallas_call(kernel, name=name, out_shape=shapes, in_specs=[pl.BlockSpe...  2.87 us
  transfers between devices with their start and end apart: 7, of which 4 were waited for; matrix products, arithmetic and copies ran while one was open for 0% of the time, Pallas kernels for 1%

profile of v7, /device:TPU:1, one launch (start us, length us, event | category | flops | bytes accessed | tf_op | source)
XLA Modules:
  0.0 53.8 jit_solution(5574759462790967694)
XLA Ops:
  0.0 1.0 %load.1 = (f32[4,64,128]{2,1,0:T(8,128)S(1)}, f32[4,64,128]{2,1,0:T(8,128)S(1)}, f32[2,64,128]{2,1,0:T(8,128)S(1)}, f32[2,64,128]{2,1,0:T(8,128)S(1)}, f32[2,4,1...) custom-call(f32[4,64,128]{2,1,0:T(8,128)} %t_hbm.1, f32[4,64,128]{2,1,0:T(8,128)} %k_hbm.1), custom_call_target="tpu_custom_call" | custom-call | flops 2000000 | bytes 2000000 | tf_op jit(solution)/shard_map/load/pallas_call | solution.py:377
  1.0 3.1 %collective-permute-start = (f32[2,64,128]{2,1,0:T(8,128)S(1)}, f32[2,64,128]{2,1,0:T(8,128)S(1)}, u32[]{:S(2)}, u32[]{:S(2)}) collective-permute-start(f32[2,64,128]{2,1,0:T(8,128)S(1)} %get-tuple-element.31), channel_id=1, source_target_pairs={{0,64},{1,2},{2,1},{3,4},{4,3},{5,6},{6,5},{7,8},{8,7},{9,10},{10,... | collective-permute-start | bytes 196616 | tf_op jit(solution)/shard_map/ppermute | solution.py:400
  4.1 0.3 collective-permute-start.1
  4.4 1.6 %collective-permute-start.2 = (f32[2,4,128]{2,1,0:T(4,128)S(1)}, f32[2,4,128]{2,1,0:T(4,128)S(1)}, u32[]{:S(2)}, u32[]{:S(2)}) collective-permute-start(f32[2,4,128]{2,1,0:T(4,128)S(1)} %get-tuple-element.33), channel_id=1, source_target_pairs={{0,64},{1,65},{2,66},{3,67},{4,68},{5,69},{6,70},{7,71},{8,72},{9,... | collective-permute-start | bytes 12296 | tf_op jit(solution)/shard_map/ppermute | solution.py:400
  6.1 0.3 collective-permute-start.3
  6.4 0.5 inner.1
  6.9 0.2 collective-permute-done.2.z_even_ref
  7.1 0.2 collective-permute-done.3.z_odd_ref
  7.2 0.0 collective-permute-done.across_ref
  7.2 0.0 collective-permute-done.1.inside_ref
  7.2 0.4 first.1
  7.6 22.3 %all_to_all.16 = f32[320,1,128]{2,1,0:T(1,128)S(1)} all-to-all(f32[320,1,128]{2,1,0:T(1,128)S(1)} %bitcast.9), channel_id=1, replica_groups=mesh['zg'=4,'gy'=64] {'gy'}, dimensions={0} | all-to-all | bytes 327680 | tf_op jit(solution)/shard_map/all_to_all | solution.py:426
  29.9 0.1 column.1
  30.0 14.9 %all_to_all.17 = f32[64,2,128]{2,1,0:T(2,128)S(1)} all-to-all(f32[64,2,128]{2,1,0:T(2,128)S(1)} %bitcast.8), channel_id=1, replica_groups=mesh['zg'=4,'gy'=64] {'gy'}, dimensions={0} | all-to-all | bytes 131072 | tf_op jit(solution)/shard_map/all_to_all | solution.py:428
  45.0 0.1 second.1
  45.0 2.6 %collective-permute-start.6 = (f32[5,4,128]{2,1,0:T(4,128)S(1)}, f32[5,4,128]{2,1,0:T(4,128)S(1)}, u32[]{:S(2)}, u32[]{:S(2)}) collective-permute-start(f32[5,4,128]{2,1,0:T(4,128)S(1)} %get-tuple-element.44.e0_ref), channel_id=1, source_target_pairs={{0,192},{64,0},{128,64},{192,128},{1,193},{65,1},{129,65},{193,129... | collective-permute-start | bytes 30728 | tf_op jit(solution)/shard_map/ppermute | solution.py:405
  47.6 1.4 %collective-permute-start.5 = (f32[5,4,128]{2,1,0:T(4,128)S(1)}, f32[5,4,128]{2,1,0:T(4,128)S(1)}, u32[]{:S(2)}, u32[]{:S(2)}) collective-permute-start(f32[5,4,128]{2,1,0:T(4,128)S(1)} %get-tuple-element.44.e0_ref), channel_id=1, source_target_pairs={{0,128},{64,192},{128,0},{192,64},{1,129},{65,193},{129,1},{193,65... | collective-permute-start | bytes 30728 | tf_op jit(solution)/shard_map/ppermute | solution.py:405
  49.0 0.8 %collective-permute-start.4 = (f32[5,4,128]{2,1,0:T(4,128)S(1)}, f32[5,4,128]{2,1,0:T(4,128)S(1)}, u32[]{:S(2)}, u32[]{:S(2)}) collective-permute-start(f32[5,4,128]{2,1,0:T(4,128)S(1)} %get-tuple-element.44.e0_ref), channel_id=1, source_target_pairs={{0,64},{64,128},{128,192},{192,0},{1,65},{65,129},{129,193},{193,1... | collective-permute-start | bytes 30728 | tf_op jit(solution)/shard_map/ppermute | solution.py:405
  49.8 0.1 local_z.1.local_ref
  49.9 0.0 collective-permute-done.6.e3_ref
  49.9 1.8 %collective-permute-done.5.e2_ref = f32[5,4,128]{2,1,0:T(4,128)S(1)} collective-permute-done((f32[5,4,128]{2,1,0:T(4,128)S(1)}, f32[5,4,128]{2,1,0:T(4,128)S(1)}, u32[]{:S(2)}, u32[]{:S(2)}) %collective-permute-start.5) | collective-permute-done | bytes 10272 | tf_op jit(solution)/shard_map/ppermute | solution.py:405
  51.6 1.4 %collective-permute-done.4.e1_ref = f32[5,4,128]{2,1,0:T(4,128)S(1)} collective-permute-done((f32[5,4,128]{2,1,0:T(4,128)S(1)}, f32[5,4,128]{2,1,0:T(4,128)S(1)}, u32[]{:S(2)}, u32[]{:S(2)}) %collective-permute-start.4) | collective-permute-done | bytes 10272 | tf_op jit(solution)/shard_map/ppermute | solution.py:405
  53.0 0.8 %last.1 = f32[4,64,128]{2,1,0:T(8,128)} custom-call(f32[4,64,128]{2,1,0:T(8,128)S(1)} %local_z.1.local_ref, f32[2,4,64,128]{3,2,1,0:T(8,128)S(1)} %get-tuple-element.37.spikes_ref, f32[3,4,128]{2,1,0:T(4,128)S(1)} %get-tuple-element.43.last_row_ref, f32[5,4,128]{2,1,0:T(4,128)S(1)} %get-tuple-element.44.e0_ref, ...), custom_call_target="tpu_custom_call" | custom-call | flops 2000000 | bytes 2000000 | tf_op jit(solution)/shard_map/last/pallas_call | solution.py:377
Async XLA Ops:
  1.0 6.2 %collective-permute-start = (f32[2,64,128]{2,1,0:T(8,128)S(1)}, f32[2,64,128]{2,1,0:T(8,128)S(1)}, u32[]{:S(2)}, u32[]{:S(2)}) collective-permute-start(f32[2,64,128]{2,1,0:T(8,128)S(1)} %get-tuple-element.31), channel_id=1, source_target_pairs={{0,64},{1,2},{2,1},{3,4},{4,3},{5,6},{6,5},{7,8},{8,7},{9,10},{10,... | collective-permute-start | bytes 196616 | tf_op jit(solution)/shard_map/ppermute | solution.py:400
  4.1 3.1 %collective-permute-start.1 = (f32[2,64,128]{2,1,0:T(8,128)S(1)}, f32[2,64,128]{2,1,0:T(8,128)S(1)}, u32[]{:S(2)}, u32[]{:S(2)}) collective-permute-start(f32[2,64,128]{2,1,0:T(8,128)S(1)} %get-tuple-element.32), channel_id=1, source_target_pairs={{0,1},{1,0},{2,3},{3,2},{4,5},{5,4},{6,7},{7,6},{8,9},{9,8},{10,11... | collective-permute-start | bytes 196616 | tf_op jit(solution)/shard_map/ppermute | solution.py:400
  4.4 2.6 %collective-permute-start.2 = (f32[2,4,128]{2,1,0:T(4,128)S(1)}, f32[2,4,128]{2,1,0:T(4,128)S(1)}, u32[]{:S(2)}, u32[]{:S(2)}) collective-permute-start(f32[2,4,128]{2,1,0:T(4,128)S(1)} %get-tuple-element.33), channel_id=1, source_target_pairs={{0,64},{1,65},{2,66},{3,67},{4,68},{5,69},{6,70},{7,71},{8,72},{9,... | collective-permute-start | bytes 12296 | tf_op jit(solution)/shard_map/ppermute | solution.py:400
  6.1 1.2 %collective-permute-start.3 = (f32[2,4,128]{2,1,0:T(4,128)S(1)}, f32[2,4,128]{2,1,0:T(4,128)S(1)}, u32[]{:S(2)}, u32[]{:S(2)}) collective-permute-start(f32[2,4,128]{2,1,0:T(4,128)S(1)} %get-tuple-element.34), channel_id=1, source_target_pairs={{0,1},{1,0},{2,3},{3,2},{4,5},{5,4},{6,7},{7,6},{8,9},{9,8},{10,11... | collective-permute-start | bytes 12296 | tf_op jit(solution)/shard_map/ppermute | solution.py:400
  45.0 4.8 %collective-permute-start.6 = (f32[5,4,128]{2,1,0:T(4,128)S(1)}, f32[5,4,128]{2,1,0:T(4,128)S(1)}, u32[]{:S(2)}, u32[]{:S(2)}) collective-permute-start(f32[5,4,128]{2,1,0:T(4,128)S(1)} %get-tuple-element.44.e0_ref), channel_id=1, source_target_pairs={{0,192},{64,0},{128,64},{192,128},{1,193},{65,1},{129,65},{193,129... | collective-permute-start | bytes 30728 | tf_op jit(solution)/shard_map/ppermute | solution.py:405
  47.6 4.0 %collective-permute-start.5 = (f32[5,4,128]{2,1,0:T(4,128)S(1)}, f32[5,4,128]{2,1,0:T(4,128)S(1)}, u32[]{:S(2)}, u32[]{:S(2)}) collective-permute-start(f32[5,4,128]{2,1,0:T(4,128)S(1)} %get-tuple-element.44.e0_ref), channel_id=1, source_target_pairs={{0,128},{64,192},{128,0},{192,64},{1,129},{65,193},{129,1},{193,65... | collective-permute-start | bytes 30728 | tf_op jit(solution)/shard_map/ppermute | solution.py:405
  49.0 4.0 %collective-permute-start.4 = (f32[5,4,128]{2,1,0:T(4,128)S(1)}, f32[5,4,128]{2,1,0:T(4,128)S(1)}, u32[]{:S(2)}, u32[]{:S(2)}) collective-permute-start(f32[5,4,128]{2,1,0:T(4,128)S(1)} %get-tuple-element.44.e0_ref), channel_id=1, source_target_pairs={{0,64},{64,128},{128,192},{192,0},{1,65},{65,129},{129,193},{193,1... | collective-permute-start | bytes 30728 | tf_op jit(solution)/shard_map/ppermute | solution.py:405

commit v8 on v7

--- a/solution.py
+++ b/solution.py
@@ -13,6 +13,7 @@
 XC, ZC, YC = NX // LANES, NZB // LANES, NGY // LANES
 STRIDES = (1, 2, 4)
 VALUES = 5
+SHIFTS = (1, 3, 2)
 
 LOAD_GRANT = 54816
 
@@ -345,7 +346,7 @@
 
 def last_kernel(local_ref, spikes_ref, last_row_ref, e0_ref, e1_ref, e2_ref, e3_ref, out_ref, line, ends):
     zg = lax.axis_index("zg")
-    for j, e_ref in enumerate((e0_ref, e1_ref, e2_ref, e3_ref)):
+    for j, e_ref in zip((0,) + SHIFTS, (e0_ref, e1_ref, e2_ref, e3_ref)):
         line[lax.rem(zg + (NZG - j), NZG)] = e_ref[...]
     inverses, sources = [], []
     leak, source = line[0, 0], line[0, 3]
@@ -428,7 +429,7 @@
     ends = lax.all_to_all(ends, "gy", split_axis=0, concat_axis=0, tiled=True)
     second, sums, last_row = call(
         second_kernel, "second", [block, (5, NB, NX), (3, NB, NX)], [ends, back, spikes, coeffs, top])
-    sums = [sums] + [around(sums, "zg", j) for j in range(1, NZG)]
+    sums = [sums] + [around(sums, "zg", j) for j in SHIFTS]
     (local,) = call(local_z_kernel, "local_z", [block], [second, z_plan, z_ends, t])
     (out,) = call(last_kernel, "last", [block], [local, spikes, last_row] + sums,
                   scratch=[pltpu.VMEM((NZG, 5, NB, NX), jnp.float32), pltpu.VMEM((NZG + 1, NB, NX), jnp.float32)])

time: 54 us -> 53.9 us (level)
  waiting for transfers between devices: 3.57 us -> 2.89 us
  starting transfers between devices: 10.1 us -> 10.7 us
    ppermute x3, waiting for transfers between devices: 3.18 us -> 2.5 us  [around(): return lax.ppermute(x, axis, [(i, (i + by) % count) for i in range(count)])]
    ppermute x3, starting transfers between devices: 4.72 us -> 5.34 us  [around(): return lax.ppermute(x, axis, [(i, (i + by) % count) for i in range(count)])]
where the time goes in v8:
time: 53.9 us; the launch traced here: 53.7 us
  blocking collectives  37.2 us (69%)
  starting transfers between devices  10.7 us (20%)
  waiting for transfers between devices  2.89 us (5%)
  Pallas kernels  2.86 us (5%)
    all_to_all x1, blocking collectives, shards(): lax.all_to_all(bundle.reshape(NZB * VALUES, 1, NX), 'gy', split_axis=0, c...  22.3 us
    all_to_all x1, blocking collectives, shards(): ends = lax.all_to_all(ends, 'gy', split_axis=0, concat_axis=0, tiled=True)  14.9 us
    ppermute x4, starting transfers between devices, swapped(): return lax.ppermute(x, ('zg', 'gy'), pairs)  5.36 us
    ppermute x3, starting transfers between devices, around(): return lax.ppermute(x, axis, [(i, (i + by) % count) for i in range(count)])  5.34 us
    pallas_call x7, Pallas kernels, call(): pl.pallas_call(kernel, name=name, out_shape=shapes, in_specs=[pl.BlockSpe...  2.86 us
    ppermute x3, waiting for transfers between devices, around(): return lax.ppermute(x, axis, [(i, (i + by) % count) for i in range(count)])  2.5 us
  transfers between devices with their start and end apart: 7, of which 4 were waited for; matrix products, arithmetic and copies ran while one was open for 0% of the time, Pallas kernels for 1%

profile of v8, /device:TPU:1, one launch (start us, length us, event | category | flops | bytes accessed | tf_op | source)
XLA Modules:
  0.0 53.7 jit_solution(14207340063536344622)
XLA Ops:
  0.0 1.0 %load.1 = (f32[4,64,128]{2,1,0:T(8,128)S(1)}, f32[4,64,128]{2,1,0:T(8,128)S(1)}, f32[2,64,128]{2,1,0:T(8,128)S(1)}, f32[2,64,128]{2,1,0:T(8,128)S(1)}, f32[2,4,1...) custom-call(f32[4,64,128]{2,1,0:T(8,128)} %t_hbm.1, f32[4,64,128]{2,1,0:T(8,128)} %k_hbm.1), custom_call_target="tpu_custom_call" | custom-call | flops 2000000 | bytes 2000000 | tf_op jit(solution)/shard_map/load/pallas_call | solution.py:378
  1.0 3.1 %collective-permute-start = (f32[2,64,128]{2,1,0:T(8,128)S(1)}, f32[2,64,128]{2,1,0:T(8,128)S(1)}, u32[]{:S(2)}, u32[]{:S(2)}) collective-permute-start(f32[2,64,128]{2,1,0:T(8,128)S(1)} %get-tuple-element.31), channel_id=1, source_target_pairs={{0,64},{1,2},{2,1},{3,4},{4,3},{5,6},{6,5},{7,8},{8,7},{9,10},{10,... | collective-permute-start | bytes 196616 | tf_op jit(solution)/shard_map/ppermute | solution.py:401
  4.1 0.3 collective-permute-start.1
  4.4 1.6 %collective-permute-start.2 = (f32[2,4,128]{2,1,0:T(4,128)S(1)}, f32[2,4,128]{2,1,0:T(4,128)S(1)}, u32[]{:S(2)}, u32[]{:S(2)}) collective-permute-start(f32[2,4,128]{2,1,0:T(4,128)S(1)} %get-tuple-element.33), channel_id=1, source_target_pairs={{0,64},{1,65},{2,66},{3,67},{4,68},{5,69},{6,70},{7,71},{8,72},{9,... | collective-permute-start | bytes 12296 | tf_op jit(solution)/shard_map/ppermute | solution.py:401
  6.1 0.3 collective-permute-start.3
  6.4 0.5 inner.1
  6.9 0.2 collective-permute-done.2.z_even_ref
  7.1 0.2 collective-permute-done.3.z_odd_ref
  7.2 0.0 collective-permute-done.across_ref
  7.2 0.0 collective-permute-done.1.inside_ref
  7.2 0.4 first.1
  7.6 22.3 %all_to_all.16 = f32[320,1,128]{2,1,0:T(1,128)S(1)} all-to-all(f32[320,1,128]{2,1,0:T(1,128)S(1)} %bitcast.9), channel_id=1, replica_groups=mesh['zg'=4,'gy'=64] {'gy'}, dimensions={0} | all-to-all | bytes 327680 | tf_op jit(solution)/shard_map/all_to_all | solution.py:427
  29.9 0.1 column.1
  30.0 14.9 %all_to_all.17 = f32[64,2,128]{2,1,0:T(2,128)S(1)} all-to-all(f32[64,2,128]{2,1,0:T(2,128)S(1)} %bitcast.8), channel_id=1, replica_groups=mesh['zg'=4,'gy'=64] {'gy'}, dimensions={0} | all-to-all | bytes 131072 | tf_op jit(solution)/shard_map/all_to_all | solution.py:429
  45.0 0.1 second.1
  45.0 3.9 %collective-permute-start.6 = (f32[5,4,128]{2,1,0:T(4,128)S(1)}, f32[5,4,128]{2,1,0:T(4,128)S(1)}, u32[]{:S(2)}, u32[]{:S(2)}) collective-permute-start(f32[5,4,128]{2,1,0:T(4,128)S(1)} %get-tuple-element.44.e0_ref), channel_id=1, source_target_pairs={{0,128},{64,192},{128,0},{192,64},{1,129},{65,193},{129,1},{193,65... | collective-permute-start | bytes 30728 | tf_op jit(solution)/shard_map/ppermute | solution.py:406
  48.9 0.3 collective-permute-start.5
  49.2 1.1 %collective-permute-start.4 = (f32[5,4,128]{2,1,0:T(4,128)S(1)}, f32[5,4,128]{2,1,0:T(4,128)S(1)}, u32[]{:S(2)}, u32[]{:S(2)}) collective-permute-start(f32[5,4,128]{2,1,0:T(4,128)S(1)} %get-tuple-element.44.e0_ref), channel_id=1, source_target_pairs={{0,64},{64,128},{128,192},{192,0},{1,65},{65,129},{129,193},{193,1... | collective-permute-start | bytes 30728 | tf_op jit(solution)/shard_map/ppermute | solution.py:406
  50.4 0.1 local_z.1.local_ref
  50.5 0.0 collective-permute-done.6.e3_ref
  50.5 1.0 %collective-permute-done.5.e2_ref = f32[5,4,128]{2,1,0:T(4,128)S(1)} collective-permute-done((f32[5,4,128]{2,1,0:T(4,128)S(1)}, f32[5,4,128]{2,1,0:T(4,128)S(1)}, u32[]{:S(2)}, u32[]{:S(2)}) %collective-permute-start.5) | collective-permute-done | bytes 10272 | tf_op jit(solution)/shard_map/ppermute | solution.py:406
  51.4 1.5 %collective-permute-done.4.e1_ref = f32[5,4,128]{2,1,0:T(4,128)S(1)} collective-permute-done((f32[5,4,128]{2,1,0:T(4,128)S(1)}, f32[5,4,128]{2,1,0:T(4,128)S(1)}, u32[]{:S(2)}, u32[]{:S(2)}) %collective-permute-start.4) | collective-permute-done | bytes 10272 | tf_op jit(solution)/shard_map/ppermute | solution.py:406
  53.0 0.8 %last.1 = f32[4,64,128]{2,1,0:T(8,128)} custom-call(f32[4,64,128]{2,1,0:T(8,128)S(1)} %local_z.1.local_ref, f32[2,4,64,128]{3,2,1,0:T(8,128)S(1)} %get-tuple-element.37.spikes_ref, f32[3,4,128]{2,1,0:T(4,128)S(1)} %get-tuple-element.43.last_row_ref, f32[5,4,128]{2,1,0:T(4,128)S(1)} %get-tuple-element.44.e0_ref, ...), custom_call_target="tpu_custom_call" | custom-call | flops 2000000 | bytes 2000000 | tf_op jit(solution)/shard_map/last/pallas_call | solution.py:378
Async XLA Ops:
  1.0 6.2 %collective-permute-start = (f32[2,64,128]{2,1,0:T(8,128)S(1)}, f32[2,64,128]{2,1,0:T(8,128)S(1)}, u32[]{:S(2)}, u32[]{:S(2)}) collective-permute-start(f32[2,64,128]{2,1,0:T(8,128)S(1)} %get-tuple-element.31), channel_id=1, source_target_pairs={{0,64},{1,2},{2,1},{3,4},{4,3},{5,6},{6,5},{7,8},{8,7},{9,10},{10,... | collective-permute-start | bytes 196616 | tf_op jit(solution)/shard_map/ppermute | solution.py:401
  4.1 3.1 %collective-permute-start.1 = (f32[2,64,128]{2,1,0:T(8,128)S(1)}, f32[2,64,128]{2,1,0:T(8,128)S(1)}, u32[]{:S(2)}, u32[]{:S(2)}) collective-permute-start(f32[2,64,128]{2,1,0:T(8,128)S(1)} %get-tuple-element.32), channel_id=1, source_target_pairs={{0,1},{1,0},{2,3},{3,2},{4,5},{5,4},{6,7},{7,6},{8,9},{9,8},{10,11... | collective-permute-start | bytes 196616 | tf_op jit(solution)/shard_map/ppermute | solution.py:401
  4.4 2.6 %collective-permute-start.2 = (f32[2,4,128]{2,1,0:T(4,128)S(1)}, f32[2,4,128]{2,1,0:T(4,128)S(1)}, u32[]{:S(2)}, u32[]{:S(2)}) collective-permute-start(f32[2,4,128]{2,1,0:T(4,128)S(1)} %get-tuple-element.33), channel_id=1, source_target_pairs={{0,64},{1,65},{2,66},{3,67},{4,68},{5,69},{6,70},{7,71},{8,72},{9,... | collective-permute-start | bytes 12296 | tf_op jit(solution)/shard_map/ppermute | solution.py:401
  6.1 1.2 %collective-permute-start.3 = (f32[2,4,128]{2,1,0:T(4,128)S(1)}, f32[2,4,128]{2,1,0:T(4,128)S(1)}, u32[]{:S(2)}, u32[]{:S(2)}) collective-permute-start(f32[2,4,128]{2,1,0:T(4,128)S(1)} %get-tuple-element.34), channel_id=1, source_target_pairs={{0,1},{1,0},{2,3},{3,2},{4,5},{5,4},{6,7},{7,6},{8,9},{9,8},{10,11... | collective-permute-start | bytes 12296 | tf_op jit(solution)/shard_map/ppermute | solution.py:401
  45.0 5.4 %collective-permute-start.6 = (f32[5,4,128]{2,1,0:T(4,128)S(1)}, f32[5,4,128]{2,1,0:T(4,128)S(1)}, u32[]{:S(2)}, u32[]{:S(2)}) collective-permute-start(f32[5,4,128]{2,1,0:T(4,128)S(1)} %get-tuple-element.44.e0_ref), channel_id=1, source_target_pairs={{0,128},{64,192},{128,0},{192,64},{1,129},{65,193},{129,1},{193,65... | collective-permute-start | bytes 30728 | tf_op jit(solution)/shard_map/ppermute | solution.py:406
  48.9 2.5 %collective-permute-start.5 = (f32[5,4,128]{2,1,0:T(4,128)S(1)}, f32[5,4,128]{2,1,0:T(4,128)S(1)}, u32[]{:S(2)}, u32[]{:S(2)}) collective-permute-start(f32[5,4,128]{2,1,0:T(4,128)S(1)} %get-tuple-element.44.e0_ref), channel_id=1, source_target_pairs={{0,192},{64,0},{128,64},{192,128},{1,193},{65,1},{129,65},{193,129... | collective-permute-start | bytes 30728 | tf_op jit(solution)/shard_map/ppermute | solution.py:406
  49.2 3.7 %collective-permute-start.4 = (f32[5,4,128]{2,1,0:T(4,128)S(1)}, f32[5,4,128]{2,1,0:T(4,128)S(1)}, u32[]{:S(2)}, u32[]{:S(2)}) collective-permute-start(f32[5,4,128]{2,1,0:T(4,128)S(1)} %get-tuple-element.44.e0_ref), channel_id=1, source_target_pairs={{0,64},{64,128},{128,192},{192,0},{1,65},{65,129},{129,193},{193,1... | collective-permute-start | bytes 30728 | tf_op jit(solution)/shard_map/ppermute | solution.py:406

commit v9 on v7

--- a/solution.py
+++ b/solution.py
@@ -321,52 +321,49 @@
     leak, couple, top = coeffs_ref[1], coeffs_ref[2], top_ref[...]
     inverse = 1.0 / (leak + couple + top)
     left, right = couple * inverse, top * inverse
-    sums_ref[0] = coeffs_ref[0] + left * leak
-    sums_ref[1] = right * leak
-    sums_ref[2] = left * top
-    sums_ref[3] = first + left * last
-    sums_ref[4] = right * last
+    sums = (coeffs_ref[0] + left * leak, right * leak, left * top, first + left * last, right * last)
+    for d in range(NZG):
+        for j, entry in enumerate(sums):
+            sums_ref[VALUES * d + j] = entry
     last_row_ref[0] = last * inverse
     last_row_ref[1] = left
     last_row_ref[2] = right
 
 
-def local_z_kernel(second_ref, z_plan_ref, z_ends_ref, t_ref, out_ref):
+def local_z(second, plan, factors):
     chunk = rows_of((LANES, NX), 0)
-    for y in range(NB):
-        plan = get_plan(z_plan_ref, (y,), ZC)
-        b, over = fold_sources(plan, split(second_ref[y]))
-        b0 = jnp.where(chunk > 0, b[0] + shift(over, 1, 0), 0.0)
-        head = separator_solve([z_ends_ref[y, j] for j in range(2 * len(STRIDES) + 1)], b0)
-        following = jnp.where(chunk == LANES - 1, 0.0, shift(head, -1, 0))
-        x = jnp.concatenate(unfold(plan, b, head, following), axis=0)
-        out_ref[y] = block_row(t_ref, y) + x
-
-
-def last_kernel(local_ref, spikes_ref, last_row_ref, e0_ref, e1_ref, e2_ref, e3_ref, out_ref, line, ends):
+    b, over = fold_sources(plan, split(second))
+    head = separator_solve(factors, jnp.where(chunk > 0, b[0] + shift(over, 1, 0), 0.0))
+    following = jnp.where(chunk == LANES - 1, 0.0, shift(head, -1, 0))
+    return jnp.concatenate(unfold(plan, b, head, following), axis=0)
+
+
+def last_kernel(t_ref, second_ref, z_plan_ref, z_ends_ref, spikes_ref, last_row_ref, line_ref, out_ref, ends):
     zg = lax.axis_index("zg")
-    for j, e_ref in enumerate((e0_ref, e1_ref, e2_ref, e3_ref)):
-        line[lax.rem(zg + (NZG - j), NZG)] = e_ref[...]
+    line = [[line_ref[VALUES * d + j] for j in range(VALUES)] for d in range(NZG)]
     inverses, sources = [], []
-    leak, source = line[0, 0], line[0, 3]
+    leak, source = line[0][0], line[0][3]
     for d in range(NZG):
-        couple = line[d, 2]
+        couple = line[d][2]
         inverse = 1.0 / (leak + couple)
         inverses.append(inverse)
         sources.append(source)
         if d + 1 < NZG:
             passed = couple * inverse
-            leak = line[d + 1, 0] + line[d, 1] + passed * leak
-            source = line[d + 1, 3] + line[d, 4] + passed * source
+            leak = line[d + 1][0] + line[d][1] + passed * leak
+            source = line[d + 1][3] + line[d][4] + passed * source
     value = jnp.zeros_like(source)
     ends[NZG] = value
     for d in reversed(range(NZG)):
-        value = (sources[d] + line[d, 2] * value) * inverses[d]
+        value = (sources[d] + line[d][2] * value) * inverses[d]
         ends[d] = value
     own = ends[zg]
     following = last_row_ref[0] + last_row_ref[1] * own + last_row_ref[2] * ends[zg + 1]
     for y in range(NB):
-        x = local_ref[y] + spikes_ref[0, y] * own[y:y + 1] + spikes_ref[1, y] * following[y:y + 1]
+        x = local_z(second_ref[y], get_plan(z_plan_ref, (y,), ZC),
+                    [z_ends_ref[y, j] for j in range(2 * len(STRIDES) + 1)])
+        x = block_row(t_ref, y) + x
+        x = x + spikes_ref[0, y] * own[y:y + 1] + spikes_ref[1, y] * following[y:y + 1]
         for a, part in enumerate(split(x)):
             out_ref[y, pl.ds(a, LANES, stride=ZC), :] = part
 
@@ -398,11 +395,6 @@
                 target = (partner, gy) if axis == "zg" else (zg, partner)
             pairs.append((zg * NGY + gy, target[0] * NGY + target[1]))
     return lax.ppermute(x, ("zg", "gy"), pairs)
-
-
-def around(x, axis, by):
-    count = lax.axis_size(axis)
-    return lax.ppermute(x, axis, [(i, (i + by) % count) for i in range(count)])
 
 
 def shards(t, k):
@@ -427,11 +419,10 @@
     (ends,) = call(column_kernel, "column", [(2 * NGY, NX)], [columns.reshape(NGY * VALUES, NX)])
     ends = lax.all_to_all(ends, "gy", split_axis=0, concat_axis=0, tiled=True)
     second, sums, last_row = call(
-        second_kernel, "second", [block, (5, NB, NX), (3, NB, NX)], [ends, back, spikes, coeffs, top])
-    sums = [sums] + [around(sums, "zg", j) for j in range(1, NZG)]
-    (local,) = call(local_z_kernel, "local_z", [block], [second, z_plan, z_ends, t])
-    (out,) = call(last_kernel, "last", [block], [local, spikes, last_row] + sums,
-                  scratch=[pltpu.VMEM((NZG, 5, NB, NX), jnp.float32), pltpu.VMEM((NZG + 1, NB, NX), jnp.float32)])
+        second_kernel, "second", [block, (NZG * VALUES, NB, NX), (3, NB, NX)], [ends, back, spikes, coeffs, top])
+    line = lax.all_to_all(sums, "zg", split_axis=0, concat_axis=0, tiled=True)
+    (out,) = call(last_kernel, "last", [block], [t, second, z_plan, z_ends, spikes, last_row, line],
+                  scratch=[pltpu.VMEM((NZG + 1, NB, NX), jnp.float32)])
     return out
 
 

time: 54 us -> 55.2 us (1.022)
  blocking collectives: 37.2 us -> 46.4 us
  starting transfers between devices: 10.1 us -> 5.36 us
  waiting for transfers between devices: 3.57 us -> 0.39 us
    all_to_all x0 -> x1, blocking collectives: none -> 9.2 us  [shards(): line = lax.all_to_all(sums, 'zg', split_axis=0, concat_axis=0, tiled=True)]
    ppermute x3 -> x0, starting transfers between devices: 4.72 us -> none  [around(): return lax.ppermute(x, axis, [(i, (i + by) % count) for i in range(count)])]
    ppermute x3 -> x0, waiting for transfers between devices: 3.18 us -> none  [around(): return lax.ppermute(x, axis, [(i, (i + by) % count) for i in range(count)])]
    pallas_call x7 -> x6, Pallas kernels: 2.87 us -> 2.81 us  [call(): pl.pallas_call(kernel, name=name, out_shape=shapes, in_specs=[pl.BlockSpe...]
  transfers between devices with their start and end apart: 7 -> 4, of which waited for: 4 -> 2; matrix products, arithmetic and copies ran while one was open for 0% -> 0% of each run, Pallas kernels for 1% -> 1%
where the time goes in v9:
time: 55.2 us; the launch traced here: 55 us
  blocking collectives  46.4 us (84%)
  starting transfers between devices  5.36 us (10%)
  Pallas kernels  2.81 us (5%)
    all_to_all x1, blocking collectives, shards(): lax.all_to_all(bundle.reshape(NZB * VALUES, 1, NX), 'gy', split_axis=0, c...  22.3 us
    all_to_all x1, blocking collectives, shards(): ends = lax.all_to_all(ends, 'gy', split_axis=0, concat_axis=0, tiled=True)  14.9 us
    all_to_all x1, blocking collectives, shards(): line = lax.all_to_all(sums, 'zg', split_axis=0, concat_axis=0, tiled=True)  9.2 us
    ppermute x4, starting transfers between devices, swapped(): return lax.ppermute(x, ('zg', 'gy'), pairs)  5.36 us
    pallas_call x6, Pallas kernels, call(): pl.pallas_call(kernel, name=name, out_shape=shapes, in_specs=[pl.BlockSpe...  2.81 us
  transfers between devices with their start and end apart: 4, of which 2 were waited for; matrix products, arithmetic and copies ran while one was open for 0% of the time, Pallas kernels for 1%

profile of v9, /device:TPU:1, one launch (start us, length us, event | category | flops | bytes accessed | tf_op | source)
XLA Modules:
  0.0 55.0 jit_solution(3661687210954917154)
XLA Ops:
  0.0 1.0 %load.1 = (f32[4,64,128]{2,1,0:T(8,128)S(1)}, f32[4,64,128]{2,1,0:T(8,128)S(1)}, f32[2,64,128]{2,1,0:T(8,128)S(1)}, f32[2,64,128]{2,1,0:T(8,128)S(1)}, f32[2,4,1...) custom-call(f32[4,64,128]{2,1,0:T(8,128)} %t_hbm.1, f32[4,64,128]{2,1,0:T(8,128)} %k_hbm.1), custom_call_target="tpu_custom_call" | custom-call | flops 2000000 | bytes 2000000 | tf_op jit(solution)/shard_map/load/pallas_call | solution.py:374
  1.0 3.1 %collective-permute-start = (f32[2,64,128]{2,1,0:T(8,128)S(1)}, f32[2,64,128]{2,1,0:T(8,128)S(1)}, u32[]{:S(2)}, u32[]{:S(2)}) collective-permute-start(f32[2,64,128]{2,1,0:T(8,128)S(1)} %get-tuple-element.31), channel_id=1, source_target_pairs={{0,64},{1,2},{2,1},{3,4},{4,3},{5,6},{6,5},{7,8},{8,7},{9,10},{10,... | collective-permute-start | bytes 196616 | tf_op jit(solution)/shard_map/ppermute | solution.py:397
  4.1 0.3 collective-permute-start.1
  4.4 1.6 %collective-permute-start.2 = (f32[2,4,128]{2,1,0:T(4,128)S(1)}, f32[2,4,128]{2,1,0:T(4,128)S(1)}, u32[]{:S(2)}, u32[]{:S(2)}) collective-permute-start(f32[2,4,128]{2,1,0:T(4,128)S(1)} %get-tuple-element.33), channel_id=1, source_target_pairs={{0,64},{1,65},{2,66},{3,67},{4,68},{5,69},{6,70},{7,71},{8,72},{9,... | collective-permute-start | bytes 12296 | tf_op jit(solution)/shard_map/ppermute | solution.py:397
  6.1 0.3 collective-permute-start.3
  6.4 0.5 inner.1
  6.9 0.2 collective-permute-done.2.z_even_ref
  7.1 0.2 collective-permute-done.3.z_odd_ref
  7.2 0.0 collective-permute-done.across_ref
  7.2 0.0 collective-permute-done.1.inside_ref
  7.2 0.4 first.1
  7.6 22.3 %all_to_all.21 = f32[320,1,128]{2,1,0:T(1,128)S(1)} all-to-all(f32[320,1,128]{2,1,0:T(1,128)S(1)} %bitcast.9), channel_id=1, replica_groups=mesh['zg'=4,'gy'=64] {'gy'}, dimensions={0} | all-to-all | bytes 327680 | tf_op jit(solution)/shard_map/all_to_all | solution.py:418
  29.9 0.1 column.1
  30.0 14.9 %all_to_all.22 = f32[64,2,128]{2,1,0:T(2,128)S(1)} all-to-all(f32[64,2,128]{2,1,0:T(2,128)S(1)} %bitcast.8), channel_id=1, replica_groups=mesh['zg'=4,'gy'=64] {'gy'}, dimensions={0} | all-to-all | bytes 131072 | tf_op jit(solution)/shard_map/all_to_all | solution.py:420
  45.0 0.1 second.1
  45.0 9.2 %all_to_all.23.line_ref = f32[20,4,128]{2,1,0:T(4,128)S(1)} all-to-all(f32[20,4,128]{2,1,0:T(4,128)S(1)} %get-tuple-element.44), channel_id=1, replica_groups=mesh['zg'=4,'gy'=64] {'zg'}, dimensions={0} | all-to-all | bytes 81920 | tf_op jit(solution)/shard_map/all_to_all | solution.py:423
  54.2 0.8 %last.1 = f32[4,64,128]{2,1,0:T(8,128)} custom-call(f32[4,64,128]{2,1,0:T(8,128)S(1)} %get-tuple-element.25.t_ref, f32[4,64,128]{2,1,0:T(8,128)S(1)} %get-tuple-element.40.second_ref, f32[4,7,3,8,128]{4,3,2,1,0:T(8,128)S(1)} %get-tuple-element.41.z_plan_ref, f32[4,7,8,128]{3,2,1,0:T(8,128)S(1)} %get-tuple-element.42.z_ends_ref, ...), custom_call_target="tpu_custom_call" | custom-call | flops 2000000 | bytes 2000000 | tf_op jit(solution)/shard_map/last/pallas_call | solution.py:374
Async XLA Ops:
  1.0 6.2 %collective-permute-start = (f32[2,64,128]{2,1,0:T(8,128)S(1)}, f32[2,64,128]{2,1,0:T(8,128)S(1)}, u32[]{:S(2)}, u32[]{:S(2)}) collective-permute-start(f32[2,64,128]{2,1,0:T(8,128)S(1)} %get-tuple-element.31), channel_id=1, source_target_pairs={{0,64},{1,2},{2,1},{3,4},{4,3},{5,6},{6,5},{7,8},{8,7},{9,10},{10,... | collective-permute-start | bytes 196616 | tf_op jit(solution)/shard_map/ppermute | solution.py:397
  4.1 3.1 %collective-permute-start.1 = (f32[2,64,128]{2,1,0:T(8,128)S(1)}, f32[2,64,128]{2,1,0:T(8,128)S(1)}, u32[]{:S(2)}, u32[]{:S(2)}) collective-permute-start(f32[2,64,128]{2,1,0:T(8,128)S(1)} %get-tuple-element.32), channel_id=1, source_target_pairs={{0,1},{1,0},{2,3},{3,2},{4,5},{5,4},{6,7},{7,6},{8,9},{9,8},{10,11... | collective-permute-start | bytes 196616 | tf_op jit(solution)/shard_map/ppermute | solution.py:397
  4.4 2.6 %collective-permute-start.2 = (f32[2,4,128]{2,1,0:T(4,128)S(1)}, f32[2,4,128]{2,1,0:T(4,128)S(1)}, u32[]{:S(2)}, u32[]{:S(2)}) collective-permute-start(f32[2,4,128]{2,1,0:T(4,128)S(1)} %get-tuple-element.33), channel_id=1, source_target_pairs={{0,64},{1,65},{2,66},{3,67},{4,68},{5,69},{6,70},{7,71},{8,72},{9,... | collective-permute-start | bytes 12296 | tf_op jit(solution)/shard_map/ppermute | solution.py:397
  6.1 1.2 %collective-permute-start.3 = (f32[2,4,128]{2,1,0:T(4,128)S(1)}, f32[2,4,128]{2,1,0:T(4,128)S(1)}, u32[]{:S(2)}, u32[]{:S(2)}) collective-permute-start(f32[2,4,128]{2,1,0:T(4,128)S(1)} %get-tuple-element.34), channel_id=1, source_target_pairs={{0,1},{1,0},{2,3},{3,2},{4,5},{5,4},{6,7},{7,6},{8,9},{9,8},{10,11... | collective-permute-start | bytes 12296 | tf_op jit(solution)/shard_map/ppermute | solution.py:397

commit v10 on v7

--- a/solution.py
+++ b/solution.py
@@ -346,7 +346,7 @@
 def last_kernel(local_ref, spikes_ref, last_row_ref, e0_ref, e1_ref, e2_ref, e3_ref, out_ref, line, ends):
     zg = lax.axis_index("zg")
     for j, e_ref in enumerate((e0_ref, e1_ref, e2_ref, e3_ref)):
-        line[lax.rem(zg + (NZG - j), NZG)] = e_ref[...]
+        line[lax.bitwise_xor(zg, j)] = e_ref[...]
     inverses, sources = [], []
     leak, source = line[0, 0], line[0, 3]
     for d in range(NZG):
@@ -400,9 +400,8 @@
     return lax.ppermute(x, ("zg", "gy"), pairs)
 
 
-def around(x, axis, by):
-    count = lax.axis_size(axis)
-    return lax.ppermute(x, axis, [(i, (i + by) % count) for i in range(count)])
+def crossed(x, axis, by):
+    return lax.ppermute(x, axis, [(i, i ^ by) for i in range(lax.axis_size(axis))])
 
 
 def shards(t, k):
@@ -428,7 +427,7 @@
     ends = lax.all_to_all(ends, "gy", split_axis=0, concat_axis=0, tiled=True)
     second, sums, last_row = call(
         second_kernel, "second", [block, (5, NB, NX), (3, NB, NX)], [ends, back, spikes, coeffs, top])
-    sums = [sums] + [around(sums, "zg", j) for j in range(1, NZG)]
+    sums = [sums] + [crossed(sums, "zg", j) for j in range(1, NZG)]
     (local,) = call(local_z_kernel, "local_z", [block], [second, z_plan, z_ends, t])
     (out,) = call(last_kernel, "last", [block], [local, spikes, last_row] + sums,
                   scratch=[pltpu.VMEM((NZG, 5, NB, NX), jnp.float32), pltpu.VMEM((NZG + 1, NB, NX), jnp.float32)])

time: 54 us -> 52.6 us (0.974)
  starting transfers between devices: 10.1 us -> 9.33 us
  waiting for transfers between devices: 3.57 us -> 2.91 us
    ppermute x3, starting transfers between devices: 4.72 us -> 3.98 us  [crossed(): lax.ppermute(x, axis, [(i, i ^ by) for i in range(lax.axis_size(axis))])]
    ppermute x3, waiting for transfers between devices: 3.18 us -> 2.52 us  [crossed(): lax.ppermute(x, axis, [(i, i ^ by) for i in range(lax.axis_size(axis))])]
  transfers between devices with their start and end apart: 7 -> 7, of which waited for: 4 -> 3; matrix products, arithmetic and copies ran while one was open for 0% -> 0% of each run, Pallas kernels for 1% -> 1%
where the time goes in v10:
time: 52.6 us; the launch traced here: 52.4 us
  blocking collectives  37.2 us (71%)
  starting transfers between devices  9.33 us (18%)
  waiting for transfers between devices  2.91 us (6%)
  Pallas kernels  2.86 us (5%)
    all_to_all x1, blocking collectives, shards(): lax.all_to_all(bundle.reshape(NZB * VALUES, 1, NX), 'gy', split_axis=0, c...  22.3 us
    all_to_all x1, blocking collectives, shards(): ends = lax.all_to_all(ends, 'gy', split_axis=0, concat_axis=0, tiled=True)  14.9 us
    ppermute x4, starting transfers between devices, swapped(): return lax.ppermute(x, ('zg', 'gy'), pairs)  5.36 us
    ppermute x3, starting transfers between devices, crossed(): lax.ppermute(x, axis, [(i, i ^ by) for i in range(lax.axis_size(axis))])  3.98 us
    pallas_call x7, Pallas kernels, call(): pl.pallas_call(kernel, name=name, out_shape=shapes, in_specs=[pl.BlockSpe...  2.86 us
    ppermute x3, waiting for transfers between devices, crossed(): lax.ppermute(x, axis, [(i, i ^ by) for i in range(lax.axis_size(axis))])  2.52 us
  transfers between devices with their start and end apart: 7, of which 3 were waited for; matrix products, arithmetic and copies ran while one was open for 0% of the time, Pallas kernels for 1%

profile of v10, /device:TPU:1, one launch (start us, length us, event | category | flops | bytes accessed | tf_op | source)
XLA Modules:
  0.0 52.4 jit_solution(3542319803431983065)
XLA Ops:
  0.0 1.0 %load.1 = (f32[4,64,128]{2,1,0:T(8,128)S(1)}, f32[4,64,128]{2,1,0:T(8,128)S(1)}, f32[2,64,128]{2,1,0:T(8,128)S(1)}, f32[2,64,128]{2,1,0:T(8,128)S(1)}, f32[2,4,1...) custom-call(f32[4,64,128]{2,1,0:T(8,128)} %t_hbm.1, f32[4,64,128]{2,1,0:T(8,128)} %k_hbm.1), custom_call_target="tpu_custom_call" | custom-call | flops 2000000 | bytes 2000000 | tf_op jit(solution)/shard_map/load/pallas_call | solution.py:377
  1.0 3.1 %collective-permute-start = (f32[2,64,128]{2,1,0:T(8,128)S(1)}, f32[2,64,128]{2,1,0:T(8,128)S(1)}, u32[]{:S(2)}, u32[]{:S(2)}) collective-permute-start(f32[2,64,128]{2,1,0:T(8,128)S(1)} %get-tuple-element.31), channel_id=1, source_target_pairs={{0,64},{1,2},{2,1},{3,4},{4,3},{5,6},{6,5},{7,8},{8,7},{9,10},{10,... | collective-permute-start | bytes 196616 | tf_op jit(solution)/shard_map/ppermute | solution.py:400
  4.1 0.3 collective-permute-start.1
  4.4 1.6 %collective-permute-start.2 = (f32[2,4,128]{2,1,0:T(4,128)S(1)}, f32[2,4,128]{2,1,0:T(4,128)S(1)}, u32[]{:S(2)}, u32[]{:S(2)}) collective-permute-start(f32[2,4,128]{2,1,0:T(4,128)S(1)} %get-tuple-element.33), channel_id=1, source_target_pairs={{0,64},{1,65},{2,66},{3,67},{4,68},{5,69},{6,70},{7,71},{8,72},{9,... | collective-permute-start | bytes 12296 | tf_op jit(solution)/shard_map/ppermute | solution.py:400
  6.1 0.3 collective-permute-start.3
  6.4 0.5 inner.1
  6.9 0.2 collective-permute-done.2.z_even_ref
  7.1 0.2 collective-permute-done.3.z_odd_ref
  7.2 0.0 collective-permute-done.across_ref
  7.2 0.0 collective-permute-done.1.inside_ref
  7.2 0.4 first.1
  7.6 22.3 %all_to_all.16 = f32[320,1,128]{2,1,0:T(1,128)S(1)} all-to-all(f32[320,1,128]{2,1,0:T(1,128)S(1)} %bitcast.9), channel_id=1, replica_groups=mesh['zg'=4,'gy'=64] {'gy'}, dimensions={0} | all-to-all | bytes 327680 | tf_op jit(solution)/shard_map/all_to_all | solution.py:425
  29.9 0.1 column.1
  30.0 14.9 %all_to_all.17 = f32[64,2,128]{2,1,0:T(2,128)S(1)} all-to-all(f32[64,2,128]{2,1,0:T(2,128)S(1)} %bitcast.8), channel_id=1, replica_groups=mesh['zg'=4,'gy'=64] {'gy'}, dimensions={0} | all-to-all | bytes 131072 | tf_op jit(solution)/shard_map/all_to_all | solution.py:427
  45.0 0.1 second.1
  45.0 2.6 %collective-permute-start.6 = (f32[5,4,128]{2,1,0:T(4,128)S(1)}, f32[5,4,128]{2,1,0:T(4,128)S(1)}, u32[]{:S(2)}, u32[]{:S(2)}) collective-permute-start(f32[5,4,128]{2,1,0:T(4,128)S(1)} %get-tuple-element.44.e0_ref), channel_id=1, source_target_pairs={{0,192},{64,128},{128,64},{192,0},{1,193},{65,129},{129,65},{193,1... | collective-permute-start | bytes 30728 | tf_op jit(solution)/shard_map/ppermute | solution.py:404
  47.6 1.4 %collective-permute-start.5 = (f32[5,4,128]{2,1,0:T(4,128)S(1)}, f32[5,4,128]{2,1,0:T(4,128)S(1)}, u32[]{:S(2)}, u32[]{:S(2)}) collective-permute-start(f32[5,4,128]{2,1,0:T(4,128)S(1)} %get-tuple-element.44.e0_ref), channel_id=1, source_target_pairs={{0,128},{64,192},{128,0},{192,64},{1,129},{65,193},{129,1},{193,65... | collective-permute-start | bytes 30728 | tf_op jit(solution)/shard_map/ppermute | solution.py:404
  49.0 0.0 collective-permute-start.4
  49.0 0.1 local_z.1.local_ref
  49.1 0.0 collective-permute-done.6.e3_ref
  49.1 2.5 %collective-permute-done.5.e2_ref = f32[5,4,128]{2,1,0:T(4,128)S(1)} collective-permute-done((f32[5,4,128]{2,1,0:T(4,128)S(1)}, f32[5,4,128]{2,1,0:T(4,128)S(1)}, u32[]{:S(2)}, u32[]{:S(2)}) %collective-permute-start.5) | collective-permute-done | bytes 10272 | tf_op jit(solution)/shard_map/ppermute | solution.py:404
  51.6 0.0 collective-permute-done.4.e1_ref
  51.6 0.8 %last.1 = f32[4,64,128]{2,1,0:T(8,128)} custom-call(f32[4,64,128]{2,1,0:T(8,128)S(1)} %local_z.1.local_ref, f32[2,4,64,128]{3,2,1,0:T(8,128)S(1)} %get-tuple-element.37.spikes_ref, f32[3,4,128]{2,1,0:T(4,128)S(1)} %get-tuple-element.43.last_row_ref, f32[5,4,128]{2,1,0:T(4,128)S(1)} %get-tuple-element.44.e0_ref, ...), custom_call_target="tpu_custom_call" | custom-call | flops 2000000 | bytes 2000000 | tf_op jit(solution)/shard_map/last/pallas_call | solution.py:377
Async XLA Ops:
  1.0 6.2 %collective-permute-start = (f32[2,64,128]{2,1,0:T(8,128)S(1)}, f32[2,64,128]{2,1,0:T(8,128)S(1)}, u32[]{:S(2)}, u32[]{:S(2)}) collective-permute-start(f32[2,64,128]{2,1,0:T(8,128)S(1)} %get-tuple-element.31), channel_id=1, source_target_pairs={{0,64},{1,2},{2,1},{3,4},{4,3},{5,6},{6,5},{7,8},{8,7},{9,10},{10,... | collective-permute-start | bytes 196616 | tf_op jit(solution)/shard_map/ppermute | solution.py:400
  4.1 3.1 %collective-permute-start.1 = (f32[2,64,128]{2,1,0:T(8,128)S(1)}, f32[2,64,128]{2,1,0:T(8,128)S(1)}, u32[]{:S(2)}, u32[]{:S(2)}) collective-permute-start(f32[2,64,128]{2,1,0:T(8,128)S(1)} %get-tuple-element.32), channel_id=1, source_target_pairs={{0,1},{1,0},{2,3},{3,2},{4,5},{5,4},{6,7},{7,6},{8,9},{9,8},{10,11... | collective-permute-start | bytes 196616 | tf_op jit(solution)/shard_map/ppermute | solution.py:400
  4.4 2.6 %collective-permute-start.2 = (f32[2,4,128]{2,1,0:T(4,128)S(1)}, f32[2,4,128]{2,1,0:T(4,128)S(1)}, u32[]{:S(2)}, u32[]{:S(2)}) collective-permute-start(f32[2,4,128]{2,1,0:T(4,128)S(1)} %get-tuple-element.33), channel_id=1, source_target_pairs={{0,64},{1,65},{2,66},{3,67},{4,68},{5,69},{6,70},{7,71},{8,72},{9,... | collective-permute-start | bytes 12296 | tf_op jit(solution)/shard_map/ppermute | solution.py:400
  6.1 1.2 %collective-permute-start.3 = (f32[2,4,128]{2,1,0:T(4,128)S(1)}, f32[2,4,128]{2,1,0:T(4,128)S(1)}, u32[]{:S(2)}, u32[]{:S(2)}) collective-permute-start(f32[2,4,128]{2,1,0:T(4,128)S(1)} %get-tuple-element.34), channel_id=1, source_target_pairs={{0,1},{1,0},{2,3},{3,2},{4,5},{5,4},{6,7},{7,6},{8,9},{9,8},{10,11... | collective-permute-start | bytes 12296 | tf_op jit(solution)/shard_map/ppermute | solution.py:400
  45.0 4.1 %collective-permute-start.6 = (f32[5,4,128]{2,1,0:T(4,128)S(1)}, f32[5,4,128]{2,1,0:T(4,128)S(1)}, u32[]{:S(2)}, u32[]{:S(2)}) collective-permute-start(f32[5,4,128]{2,1,0:T(4,128)S(1)} %get-tuple-element.44.e0_ref), channel_id=1, source_target_pairs={{0,192},{64,128},{128,64},{192,0},{1,193},{65,129},{129,65},{193,1... | collective-permute-start | bytes 30728 | tf_op jit(solution)/shard_map/ppermute | solution.py:404
  47.6 4.0 %collective-permute-start.5 = (f32[5,4,128]{2,1,0:T(4,128)S(1)}, f32[5,4,128]{2,1,0:T(4,128)S(1)}, u32[]{:S(2)}, u32[]{:S(2)}) collective-permute-start(f32[5,4,128]{2,1,0:T(4,128)S(1)} %get-tuple-element.44.e0_ref), channel_id=1, source_target_pairs={{0,128},{64,192},{128,0},{192,64},{1,129},{65,193},{129,1},{193,65... | collective-permute-start | bytes 30728 | tf_op jit(solution)/shard_map/ppermute | solution.py:404
  49.0 2.6 %collective-permute-start.4 = (f32[5,4,128]{2,1,0:T(4,128)S(1)}, f32[5,4,128]{2,1,0:T(4,128)S(1)}, u32[]{:S(2)}, u32[]{:S(2)}) collective-permute-start(f32[5,4,128]{2,1,0:T(4,128)S(1)} %get-tuple-element.44.e0_ref), channel_id=1, source_target_pairs={{0,64},{64,0},{128,192},{192,128},{1,65},{65,1},{129,193},{193,129... | collective-permute-start | bytes 30728 | tf_op jit(solution)/shard_map/ppermute | solution.py:404

commit v11 on v10

--- a/solution.py
+++ b/solution.py
@@ -13,6 +13,7 @@
 XC, ZC, YC = NX // LANES, NZB // LANES, NGY // LANES
 STRIDES = (1, 2, 4)
 VALUES = 5
+CROSSINGS = (1, 3, 2)
 
 LOAD_GRANT = 54816
 
@@ -345,7 +346,7 @@
 
 def last_kernel(local_ref, spikes_ref, last_row_ref, e0_ref, e1_ref, e2_ref, e3_ref, out_ref, line, ends):
     zg = lax.axis_index("zg")
-    for j, e_ref in enumerate((e0_ref, e1_ref, e2_ref, e3_ref)):
+    for j, e_ref in zip((0,) + CROSSINGS, (e0_ref, e1_ref, e2_ref, e3_ref)):
         line[lax.bitwise_xor(zg, j)] = e_ref[...]
     inverses, sources = [], []
     leak, source = line[0, 0], line[0, 3]
@@ -427,7 +428,7 @@
     ends = lax.all_to_all(ends, "gy", split_axis=0, concat_axis=0, tiled=True)
     second, sums, last_row = call(
         second_kernel, "second", [block, (5, NB, NX), (3, NB, NX)], [ends, back, spikes, coeffs, top])
-    sums = [sums] + [crossed(sums, "zg", j) for j in range(1, NZG)]
+    sums = [sums] + [crossed(sums, "zg", j) for j in CROSSINGS]
     (local,) = call(local_z_kernel, "local_z", [block], [second, z_plan, z_ends, t])
     (out,) = call(last_kernel, "last", [block], [local, spikes, last_row] + sums,
                   scratch=[pltpu.VMEM((NZG, 5, NB, NX), jnp.float32), pltpu.VMEM((NZG + 1, NB, NX), jnp.float32)])

time: 52.6 us -> 53.6 us (1.019)
  waiting for transfers between devices: 2.91 us -> 3.7 us
    ppermute x3, waiting for transfers between devices: 2.52 us -> 3.31 us  [crossed(): lax.ppermute(x, axis, [(i, i ^ by) for i in range(lax.axis_size(axis))])]
  transfers between devices with their start and end apart: 7 -> 7, of which waited for: 3 -> 4; matrix products, arithmetic and copies ran while one was open for 0% -> 0% of each run, Pallas kernels for 1% -> 1%
where the time goes in v11:
time: 53.6 us; the launch traced here: 53.4 us
  blocking collectives  37.2 us (69%)
  starting transfers between devices  9.56 us (18%)
  waiting for transfers between devices  3.7 us (7%)
  Pallas kernels  2.87 us (5%)
    all_to_all x1, blocking collectives, shards(): lax.all_to_all(bundle.reshape(NZB * VALUES, 1, NX), 'gy', split_axis=0, c...  22.3 us
    all_to_all x1, blocking collectives, shards(): ends = lax.all_to_all(ends, 'gy', split_axis=0, concat_axis=0, tiled=True)  14.9 us
    ppermute x4, starting transfers between devices, swapped(): return lax.ppermute(x, ('zg', 'gy'), pairs)  5.36 us
    ppermute x3, starting transfers between devices, crossed(): lax.ppermute(x, axis, [(i, i ^ by) for i in range(lax.axis_size(axis))])  4.2 us
    ppermute x3, waiting for transfers between devices, crossed(): lax.ppermute(x, axis, [(i, i ^ by) for i in range(lax.axis_size(axis))])  3.31 us
    pallas_call x7, Pallas kernels, call(): pl.pallas_call(kernel, name=name, out_shape=shapes, in_specs=[pl.BlockSpe...  2.87 us
  transfers between devices with their start and end apart: 7, of which 4 were waited for; matrix products, arithmetic and copies ran while one was open for 0% of the time, Pallas kernels for 1%

profile of v11, /device:TPU:1, one launch (start us, length us, event | category | flops | bytes accessed | tf_op | source)
XLA Modules:
  0.0 53.4 jit_solution(12011144711053852078)
XLA Ops:
  0.0 1.0 %load.1 = (f32[4,64,128]{2,1,0:T(8,128)S(1)}, f32[4,64,128]{2,1,0:T(8,128)S(1)}, f32[2,64,128]{2,1,0:T(8,128)S(1)}, f32[2,64,128]{2,1,0:T(8,128)S(1)}, f32[2,4,1...) custom-call(f32[4,64,128]{2,1,0:T(8,128)} %t_hbm.1, f32[4,64,128]{2,1,0:T(8,128)} %k_hbm.1), custom_call_target="tpu_custom_call" | custom-call | flops 2000000 | bytes 2000000 | tf_op jit(solution)/shard_map/load/pallas_call | solution.py:378
  1.0 3.1 %collective-permute-start = (f32[2,64,128]{2,1,0:T(8,128)S(1)}, f32[2,64,128]{2,1,0:T(8,128)S(1)}, u32[]{:S(2)}, u32[]{:S(2)}) collective-permute-start(f32[2,64,128]{2,1,0:T(8,128)S(1)} %get-tuple-element.31), channel_id=1, source_target_pairs={{0,64},{1,2},{2,1},{3,4},{4,3},{5,6},{6,5},{7,8},{8,7},{9,10},{10,... | collective-permute-start | bytes 196616 | tf_op jit(solution)/shard_map/ppermute | solution.py:401
  4.1 0.3 collective-permute-start.1
  4.4 1.6 %collective-permute-start.2 = (f32[2,4,128]{2,1,0:T(4,128)S(1)}, f32[2,4,128]{2,1,0:T(4,128)S(1)}, u32[]{:S(2)}, u32[]{:S(2)}) collective-permute-start(f32[2,4,128]{2,1,0:T(4,128)S(1)} %get-tuple-element.33), channel_id=1, source_target_pairs={{0,64},{1,65},{2,66},{3,67},{4,68},{5,69},{6,70},{7,71},{8,72},{9,... | collective-permute-start | bytes 12296 | tf_op jit(solution)/shard_map/ppermute | solution.py:401
  6.1 0.3 collective-permute-start.3
  6.4 0.5 inner.1
  6.9 0.2 collective-permute-done.2.z_even_ref
  7.1 0.2 collective-permute-done.3.z_odd_ref
  7.2 0.0 collective-permute-done.across_ref
  7.2 0.0 collective-permute-done.1.inside_ref
  7.2 0.4 first.1
  7.6 22.3 %all_to_all.16 = f32[320,1,128]{2,1,0:T(1,128)S(1)} all-to-all(f32[320,1,128]{2,1,0:T(1,128)S(1)} %bitcast.9), channel_id=1, replica_groups=mesh['zg'=4,'gy'=64] {'gy'}, dimensions={0} | all-to-all | bytes 327680 | tf_op jit(solution)/shard_map/all_to_all | solution.py:426
  29.9 0.1 column.1
  30.0 14.9 %all_to_all.17 = f32[64,2,128]{2,1,0:T(2,128)S(1)} all-to-all(f32[64,2,128]{2,1,0:T(2,128)S(1)} %bitcast.8), channel_id=1, replica_groups=mesh['zg'=4,'gy'=64] {'gy'}, dimensions={0} | all-to-all | bytes 131072 | tf_op jit(solution)/shard_map/all_to_all | solution.py:428
  45.0 0.1 second.1
  45.0 3.9 %collective-permute-start.6 = (f32[5,4,128]{2,1,0:T(4,128)S(1)}, f32[5,4,128]{2,1,0:T(4,128)S(1)}, u32[]{:S(2)}, u32[]{:S(2)}) collective-permute-start(f32[5,4,128]{2,1,0:T(4,128)S(1)} %get-tuple-element.44.e0_ref), channel_id=1, source_target_pairs={{0,128},{64,192},{128,0},{192,64},{1,129},{65,193},{129,1},{193,65... | collective-permute-start | bytes 30728 | tf_op jit(solution)/shard_map/ppermute | solution.py:405
  48.9 0.3 collective-permute-start.5
  49.2 0.0 collective-permute-start.4
  49.2 0.1 local_z.1.local_ref
  49.3 0.6 %collective-permute-done.6.e3_ref = f32[5,4,128]{2,1,0:T(4,128)S(1)} collective-permute-done((f32[5,4,128]{2,1,0:T(4,128)S(1)}, f32[5,4,128]{2,1,0:T(4,128)S(1)}, u32[]{:S(2)}, u32[]{:S(2)}) %collective-permute-start.6) | collective-permute-done | bytes 10272 | tf_op jit(solution)/shard_map/ppermute | solution.py:405
  50.0 2.7 %collective-permute-done.5.e2_ref = f32[5,4,128]{2,1,0:T(4,128)S(1)} collective-permute-done((f32[5,4,128]{2,1,0:T(4,128)S(1)}, f32[5,4,128]{2,1,0:T(4,128)S(1)}, u32[]{:S(2)}, u32[]{:S(2)}) %collective-permute-start.5) | collective-permute-done | bytes 10272 | tf_op jit(solution)/shard_map/ppermute | solution.py:405
  52.6 0.0 collective-permute-done.4.e1_ref
  52.6 0.8 %last.1 = f32[4,64,128]{2,1,0:T(8,128)} custom-call(f32[4,64,128]{2,1,0:T(8,128)S(1)} %local_z.1.local_ref, f32[2,4,64,128]{3,2,1,0:T(8,128)S(1)} %get-tuple-element.37.spikes_ref, f32[3,4,128]{2,1,0:T(4,128)S(1)} %get-tuple-element.43.last_row_ref, f32[5,4,128]{2,1,0:T(4,128)S(1)} %get-tuple-element.44.e0_ref, ...), custom_call_target="tpu_custom_call" | custom-call | flops 2000000 | bytes 2000000 | tf_op jit(solution)/shard_map/last/pallas_call | solution.py:378
Async XLA Ops:
  1.0 6.2 %collective-permute-start = (f32[2,64,128]{2,1,0:T(8,128)S(1)}, f32[2,64,128]{2,1,0:T(8,128)S(1)}, u32[]{:S(2)}, u32[]{:S(2)}) collective-permute-start(f32[2,64,128]{2,1,0:T(8,128)S(1)} %get-tuple-element.31), channel_id=1, source_target_pairs={{0,64},{1,2},{2,1},{3,4},{4,3},{5,6},{6,5},{7,8},{8,7},{9,10},{10,... | collective-permute-start | bytes 196616 | tf_op jit(solution)/shard_map/ppermute | solution.py:401
  4.1 3.1 %collective-permute-start.1 = (f32[2,64,128]{2,1,0:T(8,128)S(1)}, f32[2,64,128]{2,1,0:T(8,128)S(1)}, u32[]{:S(2)}, u32[]{:S(2)}) collective-permute-start(f32[2,64,128]{2,1,0:T(8,128)S(1)} %get-tuple-element.32), channel_id=1, source_target_pairs={{0,1},{1,0},{2,3},{3,2},{4,5},{5,4},{6,7},{7,6},{8,9},{9,8},{10,11... | collective-permute-start | bytes 196616 | tf_op jit(solution)/shard_map/ppermute | solution.py:401
  4.4 2.6 %collective-permute-start.2 = (f32[2,4,128]{2,1,0:T(4,128)S(1)}, f32[2,4,128]{2,1,0:T(4,128)S(1)}, u32[]{:S(2)}, u32[]{:S(2)}) collective-permute-start(f32[2,4,128]{2,1,0:T(4,128)S(1)} %get-tuple-element.33), channel_id=1, source_target_pairs={{0,64},{1,65},{2,66},{3,67},{4,68},{5,69},{6,70},{7,71},{8,72},{9,... | collective-permute-start | bytes 12296 | tf_op jit(solution)/shard_map/ppermute | solution.py:401
  6.1 1.2 %collective-permute-start.3 = (f32[2,4,128]{2,1,0:T(4,128)S(1)}, f32[2,4,128]{2,1,0:T(4,128)S(1)}, u32[]{:S(2)}, u32[]{:S(2)}) collective-permute-start(f32[2,4,128]{2,1,0:T(4,128)S(1)} %get-tuple-element.34), channel_id=1, source_target_pairs={{0,1},{1,0},{2,3},{3,2},{4,5},{5,4},{6,7},{7,6},{8,9},{9,8},{10,11... | collective-permute-start | bytes 12296 | tf_op jit(solution)/shard_map/ppermute | solution.py:401
  45.0 4.9 %collective-permute-start.6 = (f32[5,4,128]{2,1,0:T(4,128)S(1)}, f32[5,4,128]{2,1,0:T(4,128)S(1)}, u32[]{:S(2)}, u32[]{:S(2)}) collective-permute-start(f32[5,4,128]{2,1,0:T(4,128)S(1)} %get-tuple-element.44.e0_ref), channel_id=1, source_target_pairs={{0,128},{64,192},{128,0},{192,64},{1,129},{65,193},{129,1},{193,65... | collective-permute-start | bytes 30728 | tf_op jit(solution)/shard_map/ppermute | solution.py:405
  48.9 3.7 %collective-permute-start.5 = (f32[5,4,128]{2,1,0:T(4,128)S(1)}, f32[5,4,128]{2,1,0:T(4,128)S(1)}, u32[]{:S(2)}, u32[]{:S(2)}) collective-permute-start(f32[5,4,128]{2,1,0:T(4,128)S(1)} %get-tuple-element.44.e0_ref), channel_id=1, source_target_pairs={{0,192},{64,128},{128,64},{192,0},{1,193},{65,129},{129,65},{193,1... | collective-permute-start | bytes 30728 | tf_op jit(solution)/shard_map/ppermute | solution.py:405
  49.2 3.4 %collective-permute-start.4 = (f32[5,4,128]{2,1,0:T(4,128)S(1)}, f32[5,4,128]{2,1,0:T(4,128)S(1)}, u32[]{:S(2)}, u32[]{:S(2)}) collective-permute-start(f32[5,4,128]{2,1,0:T(4,128)S(1)} %get-tuple-element.44.e0_ref), channel_id=1, source_target_pairs={{0,64},{64,0},{128,192},{192,128},{1,65},{65,1},{129,193},{193,129... | collective-permute-start | bytes 30728 | tf_op jit(solution)/shard_map/ppermute | solution.py:405

commit v12 on v10

--- a/solution.py
+++ b/solution.py
@@ -211,7 +211,7 @@
     return chunked(lambda rows: ref[h, rows, :], XC)
 
 
-def first_kernel(t_ref, k_ref, inner_ref, faces_ref, x_plan_ref, x_ends_ref, across_ref, inside_ref, z_even_ref, z_odd_ref,
+def first_kernel(t_ref, k_ref, inner_ref, faces_ref, x_plan_ref, x_ends_ref, across_ref, inside_ref, z_odd_ref, z_even_ref,
                  bundle_ref, back_ref, top_ref, turned):
     gy = lax.axis_index("gy")
     zg = lax.axis_index("zg")
@@ -421,7 +421,7 @@
          (NB, ZC - 1, 3, LANES, NX), (NB,) + ends, (2,) + block, (3, NB, NX)], [t, k], scratch=[turned])
     bundle, back, top = call(
         first_kernel, "first", [(NZB * VALUES, NX), (3, NB - 1, NZB, NX), (NB, NX)],
-        [t, k, inner, faces, x_plan, x_ends, across, inside, z_even, z_odd], scratch=[turned])
+        [t, k, inner, faces, x_plan, x_ends, across, inside, z_odd, z_even], scratch=[turned])
     columns = lax.all_to_all(bundle.reshape(NZB * VALUES, 1, NX), "gy", split_axis=0, concat_axis=0, tiled=True)
     (ends,) = call(column_kernel, "column", [(2 * NGY, NX)], [columns.reshape(NGY * VALUES, NX)])
     ends = lax.all_to_all(ends, "gy", split_axis=0, concat_axis=0, tiled=True)

time: 52.6 us -> 53.2 us (1.011)
  waiting for transfers between devices: 2.91 us -> 3.55 us
  transfers between devices with their start and end apart: 7 -> 7, of which waited for: 3 -> 4; matrix products, arithmetic and copies ran while one was open for 0% -> 0% of each run, Pallas kernels for 1% -> 1%
where the time goes in v12:
time: 53.2 us; the launch traced here: 53 us
  blocking collectives  37.4 us (70%)
  starting transfers between devices  9.16 us (17%)
  waiting for transfers between devices  3.55 us (7%)
  Pallas kernels  2.86 us (5%)
    all_to_all x1, blocking collectives, shards(): lax.all_to_all(bundle.reshape(NZB * VALUES, 1, NX), 'gy', split_axis=0, c...  22.5 us
    all_to_all x1, blocking collectives, shards(): ends = lax.all_to_all(ends, 'gy', split_axis=0, concat_axis=0, tiled=True)  14.9 us
    ppermute x4, starting transfers between devices, swapped(): return lax.ppermute(x, ('zg', 'gy'), pairs)  5.54 us
    ppermute x3, starting transfers between devices, crossed(): lax.ppermute(x, axis, [(i, i ^ by) for i in range(lax.axis_size(axis))])  3.62 us
    pallas_call x7, Pallas kernels, call(): pl.pallas_call(kernel, name=name, out_shape=shapes, in_specs=[pl.BlockSpe...  2.86 us
    ppermute x3, waiting for transfers between devices, crossed(): lax.ppermute(x, axis, [(i, i ^ by) for i in range(lax.axis_size(axis))])  2.72 us
  transfers between devices with their start and end apart: 7, of which 4 were waited for; matrix products, arithmetic and copies ran while one was open for 0% of the time, Pallas kernels for 1%

profile of v12, /device:TPU:1, one launch (start us, length us, event | category | flops | bytes accessed | tf_op | source)
XLA Modules:
  0.0 53.0 jit_solution(10944113046742903992)
XLA Ops:
  0.0 1.0 %load.1 = (f32[4,64,128]{2,1,0:T(8,128)S(1)}, f32[4,64,128]{2,1,0:T(8,128)S(1)}, f32[2,64,128]{2,1,0:T(8,128)S(1)}, f32[2,64,128]{2,1,0:T(8,128)S(1)}, f32[2,4,1...) custom-call(f32[4,64,128]{2,1,0:T(8,128)} %t_hbm.1, f32[4,64,128]{2,1,0:T(8,128)} %k_hbm.1), custom_call_target="tpu_custom_call" | custom-call | flops 2000000 | bytes 2000000 | tf_op jit(solution)/shard_map/load/pallas_call | solution.py:377
  1.0 3.1 %collective-permute-start = (f32[2,64,128]{2,1,0:T(8,128)S(1)}, f32[2,64,128]{2,1,0:T(8,128)S(1)}, u32[]{:S(2)}, u32[]{:S(2)}) collective-permute-start(f32[2,64,128]{2,1,0:T(8,128)S(1)} %get-tuple-element.31), channel_id=1, source_target_pairs={{0,64},{1,2},{2,1},{3,4},{4,3},{5,6},{6,5},{7,8},{8,7},{9,10},{10,... | collective-permute-start | bytes 196616 | tf_op jit(solution)/shard_map/ppermute | solution.py:400
  4.1 0.3 collective-permute-start.1
  4.4 0.2 collective-permute-start.2
  4.6 1.9 %collective-permute-start.3 = (f32[2,4,128]{2,1,0:T(4,128)S(1)}, f32[2,4,128]{2,1,0:T(4,128)S(1)}, u32[]{:S(2)}, u32[]{:S(2)}) collective-permute-start(f32[2,4,128]{2,1,0:T(4,128)S(1)} %get-tuple-element.34), channel_id=1, source_target_pairs={{0,64},{1,65},{2,66},{3,67},{4,68},{5,69},{6,70},{7,71},{8,72},{9,... | collective-permute-start | bytes 12296 | tf_op jit(solution)/shard_map/ppermute | solution.py:400
  6.5 0.5 inner.1
  7.0 0.0 collective-permute-done.2.z_odd_ref
  7.0 0.8 %collective-permute-done.3.z_even_ref = f32[2,4,128]{2,1,0:T(4,128)S(1)} collective-permute-done((f32[2,4,128]{2,1,0:T(4,128)S(1)}, f32[2,4,128]{2,1,0:T(4,128)S(1)}, u32[]{:S(2)}, u32[]{:S(2)}) %collective-permute-start.3) | collective-permute-done | bytes 4128 | tf_op jit(solution)/shard_map/ppermute | solution.py:400
  7.9 0.0 collective-permute-done.across_ref
  7.9 0.0 collective-permute-done.1.inside_ref
  7.9 0.4 first.1
  8.2 22.5 %all_to_all.16 = f32[320,1,128]{2,1,0:T(1,128)S(1)} all-to-all(f32[320,1,128]{2,1,0:T(1,128)S(1)} %bitcast.9), channel_id=1, replica_groups=mesh['zg'=4,'gy'=64] {'gy'}, dimensions={0} | all-to-all | bytes 327680 | tf_op jit(solution)/shard_map/all_to_all | solution.py:425
  30.7 0.1 column.1
  30.8 14.9 %all_to_all.17 = f32[64,2,128]{2,1,0:T(2,128)S(1)} all-to-all(f32[64,2,128]{2,1,0:T(2,128)S(1)} %bitcast.8), channel_id=1, replica_groups=mesh['zg'=4,'gy'=64] {'gy'}, dimensions={0} | all-to-all | bytes 131072 | tf_op jit(solution)/shard_map/all_to_all | solution.py:427
  45.8 0.1 second.1
  45.8 1.8 %collective-permute-start.6 = (f32[5,4,128]{2,1,0:T(4,128)S(1)}, f32[5,4,128]{2,1,0:T(4,128)S(1)}, u32[]{:S(2)}, u32[]{:S(2)}) collective-permute-start(f32[5,4,128]{2,1,0:T(4,128)S(1)} %get-tuple-element.44.e0_ref), channel_id=1, source_target_pairs={{0,192},{64,128},{128,64},{192,0},{1,193},{65,129},{129,65},{193,1... | collective-permute-start | bytes 30728 | tf_op jit(solution)/shard_map/ppermute | solution.py:404
  47.6 1.9 %collective-permute-start.5 = (f32[5,4,128]{2,1,0:T(4,128)S(1)}, f32[5,4,128]{2,1,0:T(4,128)S(1)}, u32[]{:S(2)}, u32[]{:S(2)}) collective-permute-start(f32[5,4,128]{2,1,0:T(4,128)S(1)} %get-tuple-element.44.e0_ref), channel_id=1, source_target_pairs={{0,128},{64,192},{128,0},{192,64},{1,129},{65,193},{129,1},{193,65... | collective-permute-start | bytes 30728 | tf_op jit(solution)/shard_map/ppermute | solution.py:404
  49.5 0.0 collective-permute-start.4
  49.5 0.1 local_z.1.local_ref
  49.6 0.1 collective-permute-done.6.e3_ref
  49.7 2.0 %collective-permute-done.5.e2_ref = f32[5,4,128]{2,1,0:T(4,128)S(1)} collective-permute-done((f32[5,4,128]{2,1,0:T(4,128)S(1)}, f32[5,4,128]{2,1,0:T(4,128)S(1)}, u32[]{:S(2)}, u32[]{:S(2)}) %collective-permute-start.5) | collective-permute-done | bytes 10272 | tf_op jit(solution)/shard_map/ppermute | solution.py:404
  51.6 0.6 %collective-permute-done.4.e1_ref = f32[5,4,128]{2,1,0:T(4,128)S(1)} collective-permute-done((f32[5,4,128]{2,1,0:T(4,128)S(1)}, f32[5,4,128]{2,1,0:T(4,128)S(1)}, u32[]{:S(2)}, u32[]{:S(2)}) %collective-permute-start.4) | collective-permute-done | bytes 10272 | tf_op jit(solution)/shard_map/ppermute | solution.py:404
  52.3 0.8 %last.1 = f32[4,64,128]{2,1,0:T(8,128)} custom-call(f32[4,64,128]{2,1,0:T(8,128)S(1)} %local_z.1.local_ref, f32[2,4,64,128]{3,2,1,0:T(8,128)S(1)} %get-tuple-element.37.spikes_ref, f32[3,4,128]{2,1,0:T(4,128)S(1)} %get-tuple-element.43.last_row_ref, f32[5,4,128]{2,1,0:T(4,128)S(1)} %get-tuple-element.44.e0_ref, ...), custom_call_target="tpu_custom_call" | custom-call | flops 2000000 | bytes 2000000 | tf_op jit(solution)/shard_map/last/pallas_call | solution.py:377
Async XLA Ops:
  1.0 6.9 %collective-permute-start = (f32[2,64,128]{2,1,0:T(8,128)S(1)}, f32[2,64,128]{2,1,0:T(8,128)S(1)}, u32[]{:S(2)}, u32[]{:S(2)}) collective-permute-start(f32[2,64,128]{2,1,0:T(8,128)S(1)} %get-tuple-element.31), channel_id=1, source_target_pairs={{0,64},{1,2},{2,1},{3,4},{4,3},{5,6},{6,5},{7,8},{8,7},{9,10},{10,... | collective-permute-start | bytes 196616 | tf_op jit(solution)/shard_map/ppermute | solution.py:400
  4.1 3.8 %collective-permute-start.1 = (f32[2,64,128]{2,1,0:T(8,128)S(1)}, f32[2,64,128]{2,1,0:T(8,128)S(1)}, u32[]{:S(2)}, u32[]{:S(2)}) collective-permute-start(f32[2,64,128]{2,1,0:T(8,128)S(1)} %get-tuple-element.32), channel_id=1, source_target_pairs={{0,1},{1,0},{2,3},{3,2},{4,5},{5,4},{6,7},{7,6},{8,9},{9,8},{10,11... | collective-permute-start | bytes 196616 | tf_op jit(solution)/shard_map/ppermute | solution.py:400
  4.4 2.6 %collective-permute-start.2 = (f32[2,4,128]{2,1,0:T(4,128)S(1)}, f32[2,4,128]{2,1,0:T(4,128)S(1)}, u32[]{:S(2)}, u32[]{:S(2)}) collective-permute-start(f32[2,4,128]{2,1,0:T(4,128)S(1)} %get-tuple-element.33), channel_id=1, source_target_pairs={{0,1},{1,0},{2,3},{3,2},{4,5},{5,4},{6,7},{7,6},{8,9},{9,8},{10,11... | collective-permute-start | bytes 12296 | tf_op jit(solution)/shard_map/ppermute | solution.py:400
  4.6 3.2 %collective-permute-start.3 = (f32[2,4,128]{2,1,0:T(4,128)S(1)}, f32[2,4,128]{2,1,0:T(4,128)S(1)}, u32[]{:S(2)}, u32[]{:S(2)}) collective-permute-start(f32[2,4,128]{2,1,0:T(4,128)S(1)} %get-tuple-element.34), channel_id=1, source_target_pairs={{0,64},{1,65},{2,66},{3,67},{4,68},{5,69},{6,70},{7,71},{8,72},{9,... | collective-permute-start | bytes 12296 | tf_op jit(solution)/shard_map/ppermute | solution.py:400
  45.8 3.8 %collective-permute-start.6 = (f32[5,4,128]{2,1,0:T(4,128)S(1)}, f32[5,4,128]{2,1,0:T(4,128)S(1)}, u32[]{:S(2)}, u32[]{:S(2)}) collective-permute-start(f32[5,4,128]{2,1,0:T(4,128)S(1)} %get-tuple-element.44.e0_ref), channel_id=1, source_target_pairs={{0,192},{64,128},{128,64},{192,0},{1,193},{65,129},{129,65},{193,1... | collective-permute-start | bytes 30728 | tf_op jit(solution)/shard_map/ppermute | solution.py:404
  47.6 4.0 %collective-permute-start.5 = (f32[5,4,128]{2,1,0:T(4,128)S(1)}, f32[5,4,128]{2,1,0:T(4,128)S(1)}, u32[]{:S(2)}, u32[]{:S(2)}) collective-permute-start(f32[5,4,128]{2,1,0:T(4,128)S(1)} %get-tuple-element.44.e0_ref), channel_id=1, source_target_pairs={{0,128},{64,192},{128,0},{192,64},{1,129},{65,193},{129,1},{193,65... | collective-permute-start | bytes 30728 | tf_op jit(solution)/shard_map/ppermute | solution.py:404
  49.5 2.8 %collective-permute-start.4 = (f32[5,4,128]{2,1,0:T(4,128)S(1)}, f32[5,4,128]{2,1,0:T(4,128)S(1)}, u32[]{:S(2)}, u32[]{:S(2)}) collective-permute-start(f32[5,4,128]{2,1,0:T(4,128)S(1)} %get-tuple-element.44.e0_ref), channel_id=1, source_target_pairs={{0,64},{64,0},{128,192},{192,128},{1,65},{65,1},{129,193},{193,129... | collective-permute-start | bytes 30728 | tf_op jit(solution)/shard_map/ppermute | solution.py:404

commit v13 on v12

--- a/solution.py
+++ b/solution.py
@@ -211,7 +211,7 @@
     return chunked(lambda rows: ref[h, rows, :], XC)
 
 
-def first_kernel(t_ref, k_ref, inner_ref, faces_ref, x_plan_ref, x_ends_ref, across_ref, inside_ref, z_odd_ref, z_even_ref,
+def first_kernel(t_ref, k_ref, inner_ref, faces_ref, x_plan_ref, x_ends_ref, inside_ref, across_ref, z_even_ref, z_odd_ref,
                  bundle_ref, back_ref, top_ref, turned):
     gy = lax.axis_index("gy")
     zg = lax.axis_index("zg")
@@ -421,7 +421,7 @@
          (NB, ZC - 1, 3, LANES, NX), (NB,) + ends, (2,) + block, (3, NB, NX)], [t, k], scratch=[turned])
     bundle, back, top = call(
         first_kernel, "first", [(NZB * VALUES, NX), (3, NB - 1, NZB, NX), (NB, NX)],
-        [t, k, inner, faces, x_plan, x_ends, across, inside, z_odd, z_even], scratch=[turned])
+        [t, k, inner, faces, x_plan, x_ends, inside, across, z_even, z_odd], scratch=[turned])
     columns = lax.all_to_all(bundle.reshape(NZB * VALUES, 1, NX), "gy", split_axis=0, concat_axis=0, tiled=True)
     (ends,) = call(column_kernel, "column", [(2 * NGY, NX)], [columns.reshape(NGY * VALUES, NX)])
     ends = lax.all_to_all(ends, "gy", split_axis=0, concat_axis=0, tiled=True)

time: 53.2 us -> 52.6 us (0.989)
  blocking collectives: 37.4 us -> 36.3 us
  waiting for transfers between devices: 3.55 us -> 4.43 us
    all_to_all x1, blocking collectives: 22.5 us -> 21.3 us  [shards(): lax.all_to_all(bundle.reshape(NZB * VALUES, 1, NX), 'gy', split_axis=0, c...]
where the time goes in v13:
time: 52.6 us; the launch traced here: 52.5 us
  blocking collectives  36.3 us (69%)
  starting transfers between devices  8.88 us (17%)
  waiting for transfers between devices  4.43 us (8%)
  Pallas kernels  2.86 us (5%)
    all_to_all x1, blocking collectives, shards(): lax.all_to_all(bundle.reshape(NZB * VALUES, 1, NX), 'gy', split_axis=0, c...  21.3 us
    all_to_all x1, blocking collectives, shards(): ends = lax.all_to_all(ends, 'gy', split_axis=0, concat_axis=0, tiled=True)  14.9 us
    ppermute x4, starting transfers between devices, swapped(): return lax.ppermute(x, ('zg', 'gy'), pairs)  5.45 us
    ppermute x3, starting transfers between devices, crossed(): lax.ppermute(x, axis, [(i, i ^ by) for i in range(lax.axis_size(axis))])  3.42 us
    ppermute x3, waiting for transfers between devices, crossed(): lax.ppermute(x, axis, [(i, i ^ by) for i in range(lax.axis_size(axis))])  3.08 us
    pallas_call x7, Pallas kernels, call(): pl.pallas_call(kernel, name=name, out_shape=shapes, in_specs=[pl.BlockSpe...  2.86 us
    ppermute x4, waiting for transfers between devices, swapped(): return lax.ppermute(x, ('zg', 'gy'), pairs)  1.35 us
  transfers between devices with their start and end apart: 7, of which 4 were waited for; matrix products, arithmetic and copies ran while one was open for 0% of the time, Pallas kernels for 1%

profile of v13, /device:TPU:1, one launch (start us, length us, event | category | flops | bytes accessed | tf_op | source)
XLA Modules:
  0.0 52.5 jit_solution(5129194548411023381)
XLA Ops:
  0.0 1.0 %load.1 = (f32[4,64,128]{2,1,0:T(8,128)S(1)}, f32[4,64,128]{2,1,0:T(8,128)S(1)}, f32[2,64,128]{2,1,0:T(8,128)S(1)}, f32[2,64,128]{2,1,0:T(8,128)S(1)}, f32[2,4,1...) custom-call(f32[4,64,128]{2,1,0:T(8,128)} %t_hbm.1, f32[4,64,128]{2,1,0:T(8,128)} %k_hbm.1), custom_call_target="tpu_custom_call" | custom-call | flops 2000000 | bytes 2000000 | tf_op jit(solution)/shard_map/load/pallas_call | solution.py:377
  1.0 3.3 %collective-permute-start = (f32[2,64,128]{2,1,0:T(8,128)S(1)}, f32[2,64,128]{2,1,0:T(8,128)S(1)}, u32[]{:S(2)}, u32[]{:S(2)}) collective-permute-start(f32[2,64,128]{2,1,0:T(8,128)S(1)} %get-tuple-element.31), channel_id=1, source_target_pairs={{0,1},{1,0},{2,3},{3,2},{4,5},{5,4},{6,7},{7,6},{8,9},{9,8},{10,11... | collective-permute-start | bytes 196616 | tf_op jit(solution)/shard_map/ppermute | solution.py:400
  4.3 0.0 collective-permute-start.1
  4.3 1.1 %collective-permute-start.2 = (f32[2,4,128]{2,1,0:T(4,128)S(1)}, f32[2,4,128]{2,1,0:T(4,128)S(1)}, u32[]{:S(2)}, u32[]{:S(2)}) collective-permute-start(f32[2,4,128]{2,1,0:T(4,128)S(1)} %get-tuple-element.33), channel_id=1, source_target_pairs={{0,64},{1,65},{2,66},{3,67},{4,68},{5,69},{6,70},{7,71},{8,72},{9,... | collective-permute-start | bytes 12296 | tf_op jit(solution)/shard_map/ppermute | solution.py:400
  5.4 1.0 %collective-permute-start.3 = (f32[2,4,128]{2,1,0:T(4,128)S(1)}, f32[2,4,128]{2,1,0:T(4,128)S(1)}, u32[]{:S(2)}, u32[]{:S(2)}) collective-permute-start(f32[2,4,128]{2,1,0:T(4,128)S(1)} %get-tuple-element.34), channel_id=1, source_target_pairs={{0,1},{1,0},{2,3},{3,2},{4,5},{5,4},{6,7},{7,6},{8,9},{9,8},{10,11... | collective-permute-start | bytes 12296 | tf_op jit(solution)/shard_map/ppermute | solution.py:400
  6.5 0.5 inner.1
  7.0 0.0 collective-permute-done.2.z_even_ref
  7.0 0.3 collective-permute-done.3.z_odd_ref
  7.3 0.0 collective-permute-done.inside_ref
  7.3 1.0 %collective-permute-done.1.across_ref = f32[2,64,128]{2,1,0:T(8,128)S(1)} collective-permute-done((f32[2,64,128]{2,1,0:T(8,128)S(1)}, f32[2,64,128]{2,1,0:T(8,128)S(1)}, u32[]{:S(2)}, u32[]{:S(2)}) %collective-permute-start.1) | collective-permute-done | bytes 65568 | tf_op jit(solution)/shard_map/ppermute | solution.py:400
  8.3 0.4 first.1
  8.7 21.3 %all_to_all.16 = f32[320,1,128]{2,1,0:T(1,128)S(1)} all-to-all(f32[320,1,128]{2,1,0:T(1,128)S(1)} %bitcast.9), channel_id=1, replica_groups=mesh['zg'=4,'gy'=64] {'gy'}, dimensions={0} | all-to-all | bytes 327680 | tf_op jit(solution)/shard_map/all_to_all | solution.py:425
  30.0 0.1 column.1
  30.1 14.9 %all_to_all.17 = f32[64,2,128]{2,1,0:T(2,128)S(1)} all-to-all(f32[64,2,128]{2,1,0:T(2,128)S(1)} %bitcast.8), channel_id=1, replica_groups=mesh['zg'=4,'gy'=64] {'gy'}, dimensions={0} | all-to-all | bytes 131072 | tf_op jit(solution)/shard_map/all_to_all | solution.py:427
  45.1 0.1 second.1
  45.1 2.6 %collective-permute-start.6 = (f32[5,4,128]{2,1,0:T(4,128)S(1)}, f32[5,4,128]{2,1,0:T(4,128)S(1)}, u32[]{:S(2)}, u32[]{:S(2)}) collective-permute-start(f32[5,4,128]{2,1,0:T(4,128)S(1)} %get-tuple-element.44.e0_ref), channel_id=1, source_target_pairs={{0,192},{64,128},{128,64},{192,0},{1,193},{65,129},{129,65},{193,1... | collective-permute-start | bytes 30728 | tf_op jit(solution)/shard_map/ppermute | solution.py:404
  47.7 0.9 %collective-permute-start.5 = (f32[5,4,128]{2,1,0:T(4,128)S(1)}, f32[5,4,128]{2,1,0:T(4,128)S(1)}, u32[]{:S(2)}, u32[]{:S(2)}) collective-permute-start(f32[5,4,128]{2,1,0:T(4,128)S(1)} %get-tuple-element.44.e0_ref), channel_id=1, source_target_pairs={{0,128},{64,192},{128,0},{192,64},{1,129},{65,193},{129,1},{193,65... | collective-permute-start | bytes 30728 | tf_op jit(solution)/shard_map/ppermute | solution.py:404
  48.6 0.0 collective-permute-start.4
  48.6 0.1 local_z.1.local_ref
  48.6 0.3 collective-permute-done.6.e3_ref
  49.0 2.8 %collective-permute-done.5.e2_ref = f32[5,4,128]{2,1,0:T(4,128)S(1)} collective-permute-done((f32[5,4,128]{2,1,0:T(4,128)S(1)}, f32[5,4,128]{2,1,0:T(4,128)S(1)}, u32[]{:S(2)}, u32[]{:S(2)}) %collective-permute-start.5) | collective-permute-done | bytes 10272 | tf_op jit(solution)/shard_map/ppermute | solution.py:404
  51.7 0.0 collective-permute-done.4.e1_ref
  51.7 0.8 %last.1 = f32[4,64,128]{2,1,0:T(8,128)} custom-call(f32[4,64,128]{2,1,0:T(8,128)S(1)} %local_z.1.local_ref, f32[2,4,64,128]{3,2,1,0:T(8,128)S(1)} %get-tuple-element.37.spikes_ref, f32[3,4,128]{2,1,0:T(4,128)S(1)} %get-tuple-element.43.last_row_ref, f32[5,4,128]{2,1,0:T(4,128)S(1)} %get-tuple-element.44.e0_ref, ...), custom_call_target="tpu_custom_call" | custom-call | flops 2000000 | bytes 2000000 | tf_op jit(solution)/shard_map/last/pallas_call | solution.py:377
Async XLA Ops:
  1.0 6.3 %collective-permute-start = (f32[2,64,128]{2,1,0:T(8,128)S(1)}, f32[2,64,128]{2,1,0:T(8,128)S(1)}, u32[]{:S(2)}, u32[]{:S(2)}) collective-permute-start(f32[2,64,128]{2,1,0:T(8,128)S(1)} %get-tuple-element.31), channel_id=1, source_target_pairs={{0,1},{1,0},{2,3},{3,2},{4,5},{5,4},{6,7},{7,6},{8,9},{9,8},{10,11... | collective-permute-start | bytes 196616 | tf_op jit(solution)/shard_map/ppermute | solution.py:400
  4.3 4.0 %collective-permute-start.1 = (f32[2,64,128]{2,1,0:T(8,128)S(1)}, f32[2,64,128]{2,1,0:T(8,128)S(1)}, u32[]{:S(2)}, u32[]{:S(2)}) collective-permute-start(f32[2,64,128]{2,1,0:T(8,128)S(1)} %get-tuple-element.32), channel_id=1, source_target_pairs={{0,64},{1,2},{2,1},{3,4},{4,3},{5,6},{6,5},{7,8},{8,7},{9,10},{10,... | collective-permute-start | bytes 196616 | tf_op jit(solution)/shard_map/ppermute | solution.py:400
  4.3 2.6 %collective-permute-start.2 = (f32[2,4,128]{2,1,0:T(4,128)S(1)}, f32[2,4,128]{2,1,0:T(4,128)S(1)}, u32[]{:S(2)}, u32[]{:S(2)}) collective-permute-start(f32[2,4,128]{2,1,0:T(4,128)S(1)} %get-tuple-element.33), channel_id=1, source_target_pairs={{0,64},{1,65},{2,66},{3,67},{4,68},{5,69},{6,70},{7,71},{8,72},{9,... | collective-permute-start | bytes 12296 | tf_op jit(solution)/shard_map/ppermute | solution.py:400
  5.4 1.9 %collective-permute-start.3 = (f32[2,4,128]{2,1,0:T(4,128)S(1)}, f32[2,4,128]{2,1,0:T(4,128)S(1)}, u32[]{:S(2)}, u32[]{:S(2)}) collective-permute-start(f32[2,4,128]{2,1,0:T(4,128)S(1)} %get-tuple-element.34), channel_id=1, source_target_pairs={{0,1},{1,0},{2,3},{3,2},{4,5},{5,4},{6,7},{7,6},{8,9},{9,8},{10,11... | collective-permute-start | bytes 12296 | tf_op jit(solution)/shard_map/ppermute | solution.py:400
  45.1 3.8 %collective-permute-start.6 = (f32[5,4,128]{2,1,0:T(4,128)S(1)}, f32[5,4,128]{2,1,0:T(4,128)S(1)}, u32[]{:S(2)}, u32[]{:S(2)}) collective-permute-start(f32[5,4,128]{2,1,0:T(4,128)S(1)} %get-tuple-element.44.e0_ref), channel_id=1, source_target_pairs={{0,192},{64,128},{128,64},{192,0},{1,193},{65,129},{129,65},{193,1... | collective-permute-start | bytes 30728 | tf_op jit(solution)/shard_map/ppermute | solution.py:404
  47.7 4.0 %collective-permute-start.5 = (f32[5,4,128]{2,1,0:T(4,128)S(1)}, f32[5,4,128]{2,1,0:T(4,128)S(1)}, u32[]{:S(2)}, u32[]{:S(2)}) collective-permute-start(f32[5,4,128]{2,1,0:T(4,128)S(1)} %get-tuple-element.44.e0_ref), channel_id=1, source_target_pairs={{0,128},{64,192},{128,0},{192,64},{1,129},{65,193},{129,1},{193,65... | collective-permute-start | bytes 30728 | tf_op jit(solution)/shard_map/ppermute | solution.py:404
  48.6 3.2 %collective-permute-start.4 = (f32[5,4,128]{2,1,0:T(4,128)S(1)}, f32[5,4,128]{2,1,0:T(4,128)S(1)}, u32[]{:S(2)}, u32[]{:S(2)}) collective-permute-start(f32[5,4,128]{2,1,0:T(4,128)S(1)} %get-tuple-element.44.e0_ref), channel_id=1, source_target_pairs={{0,64},{64,0},{128,192},{192,128},{1,65},{65,1},{129,193},{193,129... | collective-permute-start | bytes 30728 | tf_op jit(solution)/shard_map/ppermute | solution.py:404

commit v14 on v13

--- a/solution.py
+++ b/solution.py
@@ -343,7 +343,8 @@
         out_ref[y] = block_row(t_ref, y) + x
 
 
-def last_kernel(local_ref, spikes_ref, last_row_ref, e0_ref, e1_ref, e2_ref, e3_ref, out_ref, line, ends):
+def last_kernel(local_ref, spikes_ref, last_row_ref, e0_ref, e1_ref, e2_ref, e3_ref, out_hbm, line, ends,
+                rows, sems):
     zg = lax.axis_index("zg")
     for j, e_ref in enumerate((e0_ref, e1_ref, e2_ref, e3_ref)):
         line[lax.bitwise_xor(zg, j)] = e_ref[...]
@@ -365,13 +366,18 @@
         ends[d] = value
     own = ends[zg]
     following = last_row_ref[0] + last_row_ref[1] * own + last_row_ref[2] * ends[zg + 1]
+    copies = []
     for y in range(NB):
         x = local_ref[y] + spikes_ref[0, y] * own[y:y + 1] + spikes_ref[1, y] * following[y:y + 1]
         for a, part in enumerate(split(x)):
-            out_ref[y, pl.ds(a, LANES, stride=ZC), :] = part
-
-
-def call(kernel, name, outs, args, scratch=(), cost=2000000, granted=0):
+            rows[y, pl.ds(a, LANES, stride=ZC), :] = part
+        copies.append(pltpu.make_async_copy(rows.at[y], out_hbm.at[y], sems.at[y]))
+        copies[-1].start()
+    for copy in copies:
+        copy.wait()
+
+
+def call(kernel, name, outs, args, scratch=(), cost=2000000, granted=0, result=False):
     shapes = [jax.ShapeDtypeStruct(o, jnp.float32) for o in outs]
     vmem = pl.BlockSpec(memory_space=pltpu.VMEM)
     return pl.pallas_call(
@@ -379,7 +385,7 @@
         name=name,
         out_shape=shapes,
         in_specs=[pl.BlockSpec(memory_space=pltpu.HBM)] * len(args) if granted else [vmem] * len(args),
-        out_specs=[vmem] * len(outs),
+        out_specs=[pl.BlockSpec(memory_space=pltpu.HBM) if result else vmem] * len(outs),
         scratch_shapes=scratch,
         cost_estimate=pl.CostEstimate(flops=cost, bytes_accessed=cost, transcendentals=0),
         compiler_params=pltpu.CompilerParams(vmem_limit_bytes=(granted or 24576) * 1024),
@@ -430,7 +436,8 @@
     sums = [sums] + [crossed(sums, "zg", j) for j in range(1, NZG)]
     (local,) = call(local_z_kernel, "local_z", [block], [second, z_plan, z_ends, t])
     (out,) = call(last_kernel, "last", [block], [local, spikes, last_row] + sums,
-                  scratch=[pltpu.VMEM((NZG, 5, NB, NX), jnp.float32), pltpu.VMEM((NZG + 1, NB, NX), jnp.float32)])
+                  scratch=[pltpu.VMEM((NZG, 5, NB, NX), jnp.float32), pltpu.VMEM((NZG + 1, NB, NX), jnp.float32),
+                           pltpu.VMEM(block, jnp.float32), pltpu.SemaphoreType.DMA((NB,))], result=True)
     return out
 
 

time: 52.6 us -> 52.7 us (level)
  no operation moved by 1% of the time
where the time goes in v14:
time: 52.7 us; the launch traced here: 52.5 us
  blocking collectives  36.3 us (69%)
  starting transfers between devices  8.88 us (17%)
  waiting for transfers between devices  4.43 us (8%)
  Pallas kernels  2.87 us (5%)
    all_to_all x1, blocking collectives, shards(): lax.all_to_all(bundle.reshape(NZB * VALUES, 1, NX), 'gy', split_axis=0, c...  21.3 us
    all_to_all x1, blocking collectives, shards(): ends = lax.all_to_all(ends, 'gy', split_axis=0, concat_axis=0, tiled=True)  14.9 us
    ppermute x4, starting transfers between devices, swapped(): return lax.ppermute(x, ('zg', 'gy'), pairs)  5.45 us
    ppermute x3, starting transfers between devices, crossed(): lax.ppermute(x, axis, [(i, i ^ by) for i in range(lax.axis_size(axis))])  3.42 us
    ppermute x3, waiting for transfers between devices, crossed(): lax.ppermute(x, axis, [(i, i ^ by) for i in range(lax.axis_size(axis))])  3.08 us
    pallas_call x7, Pallas kernels, call(): pl.pallas_call(kernel, name=name, out_shape=shapes, in_specs=[pl.BlockSpe...  2.87 us
    ppermute x4, waiting for transfers between devices, swapped(): return lax.ppermute(x, ('zg', 'gy'), pairs)  1.35 us
  transfers between devices with their start and end apart: 7, of which 4 were waited for; matrix products, arithmetic and copies ran while one was open for 0% of the time, Pallas kernels for 1%

profile of v14, /device:TPU:1, one launch (start us, length us, event | category | flops | bytes accessed | tf_op | source)
XLA Modules:
  0.0 52.5 jit_solution(15000212211605718384)
XLA Ops:
  0.0 1.0 %load.1 = (f32[4,64,128]{2,1,0:T(8,128)S(1)}, f32[4,64,128]{2,1,0:T(8,128)S(1)}, f32[2,64,128]{2,1,0:T(8,128)S(1)}, f32[2,64,128]{2,1,0:T(8,128)S(1)}, f32[2,4,1...) custom-call(f32[4,64,128]{2,1,0:T(8,128)} %t_hbm.1, f32[4,64,128]{2,1,0:T(8,128)} %k_hbm.1), custom_call_target="tpu_custom_call" | custom-call | flops 2000000 | bytes 2000000 | tf_op jit(solution)/shard_map/load/pallas_call | solution.py:383
  1.0 3.3 %collective-permute-start = (f32[2,64,128]{2,1,0:T(8,128)S(1)}, f32[2,64,128]{2,1,0:T(8,128)S(1)}, u32[]{:S(2)}, u32[]{:S(2)}) collective-permute-start(f32[2,64,128]{2,1,0:T(8,128)S(1)} %get-tuple-element.31), channel_id=1, source_target_pairs={{0,1},{1,0},{2,3},{3,2},{4,5},{5,4},{6,7},{7,6},{8,9},{9,8},{10,11... | collective-permute-start | bytes 196616 | tf_op jit(solution)/shard_map/ppermute | solution.py:406
  4.3 0.0 collective-permute-start.1
  4.3 1.1 %collective-permute-start.2 = (f32[2,4,128]{2,1,0:T(4,128)S(1)}, f32[2,4,128]{2,1,0:T(4,128)S(1)}, u32[]{:S(2)}, u32[]{:S(2)}) collective-permute-start(f32[2,4,128]{2,1,0:T(4,128)S(1)} %get-tuple-element.33), channel_id=1, source_target_pairs={{0,64},{1,65},{2,66},{3,67},{4,68},{5,69},{6,70},{7,71},{8,72},{9,... | collective-permute-start | bytes 12296 | tf_op jit(solution)/shard_map/ppermute | solution.py:406
  5.4 1.0 %collective-permute-start.3 = (f32[2,4,128]{2,1,0:T(4,128)S(1)}, f32[2,4,128]{2,1,0:T(4,128)S(1)}, u32[]{:S(2)}, u32[]{:S(2)}) collective-permute-start(f32[2,4,128]{2,1,0:T(4,128)S(1)} %get-tuple-element.34), channel_id=1, source_target_pairs={{0,1},{1,0},{2,3},{3,2},{4,5},{5,4},{6,7},{7,6},{8,9},{9,8},{10,11... | collective-permute-start | bytes 12296 | tf_op jit(solution)/shard_map/ppermute | solution.py:406
  6.5 0.5 inner.1
  7.0 0.0 collective-permute-done.2.z_even_ref
  7.0 0.3 collective-permute-done.3.z_odd_ref
  7.3 0.0 collective-permute-done.inside_ref
  7.3 1.0 %collective-permute-done.1.across_ref = f32[2,64,128]{2,1,0:T(8,128)S(1)} collective-permute-done((f32[2,64,128]{2,1,0:T(8,128)S(1)}, f32[2,64,128]{2,1,0:T(8,128)S(1)}, u32[]{:S(2)}, u32[]{:S(2)}) %collective-permute-start.1) | collective-permute-done | bytes 65568 | tf_op jit(solution)/shard_map/ppermute | solution.py:406
  8.3 0.4 first.1
  8.7 21.3 %all_to_all.16 = f32[320,1,128]{2,1,0:T(1,128)S(1)} all-to-all(f32[320,1,128]{2,1,0:T(1,128)S(1)} %bitcast.9), channel_id=1, replica_groups=mesh['zg'=4,'gy'=64] {'gy'}, dimensions={0} | all-to-all | bytes 327680 | tf_op jit(solution)/shard_map/all_to_all | solution.py:431
  30.0 0.1 column.1
  30.1 14.9 %all_to_all.17 = f32[64,2,128]{2,1,0:T(2,128)S(1)} all-to-all(f32[64,2,128]{2,1,0:T(2,128)S(1)} %bitcast.8), channel_id=1, replica_groups=mesh['zg'=4,'gy'=64] {'gy'}, dimensions={0} | all-to-all | bytes 131072 | tf_op jit(solution)/shard_map/all_to_all | solution.py:433
  45.1 0.1 second.1
  45.1 2.6 %collective-permute-start.6 = (f32[5,4,128]{2,1,0:T(4,128)S(1)}, f32[5,4,128]{2,1,0:T(4,128)S(1)}, u32[]{:S(2)}, u32[]{:S(2)}) collective-permute-start(f32[5,4,128]{2,1,0:T(4,128)S(1)} %get-tuple-element.44.e0_ref), channel_id=1, source_target_pairs={{0,192},{64,128},{128,64},{192,0},{1,193},{65,129},{129,65},{193,1... | collective-permute-start | bytes 30728 | tf_op jit(solution)/shard_map/ppermute | solution.py:410
  47.7 0.9 %collective-permute-start.5 = (f32[5,4,128]{2,1,0:T(4,128)S(1)}, f32[5,4,128]{2,1,0:T(4,128)S(1)}, u32[]{:S(2)}, u32[]{:S(2)}) collective-permute-start(f32[5,4,128]{2,1,0:T(4,128)S(1)} %get-tuple-element.44.e0_ref), channel_id=1, source_target_pairs={{0,128},{64,192},{128,0},{192,64},{1,129},{65,193},{129,1},{193,65... | collective-permute-start | bytes 30728 | tf_op jit(solution)/shard_map/ppermute | solution.py:410
  48.6 0.0 collective-permute-start.4
  48.6 0.1 local_z.1.local_ref
  48.6 0.3 collective-permute-done.6.e3_ref
  49.0 2.8 %collective-permute-done.5.e2_ref = f32[5,4,128]{2,1,0:T(4,128)S(1)} collective-permute-done((f32[5,4,128]{2,1,0:T(4,128)S(1)}, f32[5,4,128]{2,1,0:T(4,128)S(1)}, u32[]{:S(2)}, u32[]{:S(2)}) %collective-permute-start.5) | collective-permute-done | bytes 10272 | tf_op jit(solution)/shard_map/ppermute | solution.py:410
  51.7 0.0 collective-permute-done.4.e1_ref
  51.7 0.8 %last.1 = f32[4,64,128]{2,1,0:T(8,128)} custom-call(f32[4,64,128]{2,1,0:T(8,128)S(1)} %local_z.1.local_ref, f32[2,4,64,128]{3,2,1,0:T(8,128)S(1)} %get-tuple-element.37.spikes_ref, f32[3,4,128]{2,1,0:T(4,128)S(1)} %get-tuple-element.43.last_row_ref, f32[5,4,128]{2,1,0:T(4,128)S(1)} %get-tuple-element.44.e0_ref, ...), custom_call_target="tpu_custom_call" | custom-call | flops 2000000 | bytes 2000000 | tf_op jit(solution)/shard_map/last/pallas_call | solution.py:383
Async XLA Ops:
  1.0 6.3 %collective-permute-start = (f32[2,64,128]{2,1,0:T(8,128)S(1)}, f32[2,64,128]{2,1,0:T(8,128)S(1)}, u32[]{:S(2)}, u32[]{:S(2)}) collective-permute-start(f32[2,64,128]{2,1,0:T(8,128)S(1)} %get-tuple-element.31), channel_id=1, source_target_pairs={{0,1},{1,0},{2,3},{3,2},{4,5},{5,4},{6,7},{7,6},{8,9},{9,8},{10,11... | collective-permute-start | bytes 196616 | tf_op jit(solution)/shard_map/ppermute | solution.py:406
  4.3 4.0 %collective-permute-start.1 = (f32[2,64,128]{2,1,0:T(8,128)S(1)}, f32[2,64,128]{2,1,0:T(8,128)S(1)}, u32[]{:S(2)}, u32[]{:S(2)}) collective-permute-start(f32[2,64,128]{2,1,0:T(8,128)S(1)} %get-tuple-element.32), channel_id=1, source_target_pairs={{0,64},{1,2},{2,1},{3,4},{4,3},{5,6},{6,5},{7,8},{8,7},{9,10},{10,... | collective-permute-start | bytes 196616 | tf_op jit(solution)/shard_map/ppermute | solution.py:406
  4.3 2.6 %collective-permute-start.2 = (f32[2,4,128]{2,1,0:T(4,128)S(1)}, f32[2,4,128]{2,1,0:T(4,128)S(1)}, u32[]{:S(2)}, u32[]{:S(2)}) collective-permute-start(f32[2,4,128]{2,1,0:T(4,128)S(1)} %get-tuple-element.33), channel_id=1, source_target_pairs={{0,64},{1,65},{2,66},{3,67},{4,68},{5,69},{6,70},{7,71},{8,72},{9,... | collective-permute-start | bytes 12296 | tf_op jit(solution)/shard_map/ppermute | solution.py:406
  5.4 1.9 %collective-permute-start.3 = (f32[2,4,128]{2,1,0:T(4,128)S(1)}, f32[2,4,128]{2,1,0:T(4,128)S(1)}, u32[]{:S(2)}, u32[]{:S(2)}) collective-permute-start(f32[2,4,128]{2,1,0:T(4,128)S(1)} %get-tuple-element.34), channel_id=1, source_target_pairs={{0,1},{1,0},{2,3},{3,2},{4,5},{5,4},{6,7},{7,6},{8,9},{9,8},{10,11... | collective-permute-start | bytes 12296 | tf_op jit(solution)/shard_map/ppermute | solution.py:406
  45.1 3.8 %collective-permute-start.6 = (f32[5,4,128]{2,1,0:T(4,128)S(1)}, f32[5,4,128]{2,1,0:T(4,128)S(1)}, u32[]{:S(2)}, u32[]{:S(2)}) collective-permute-start(f32[5,4,128]{2,1,0:T(4,128)S(1)} %get-tuple-element.44.e0_ref), channel_id=1, source_target_pairs={{0,192},{64,128},{128,64},{192,0},{1,193},{65,129},{129,65},{193,1... | collective-permute-start | bytes 30728 | tf_op jit(solution)/shard_map/ppermute | solution.py:410
  47.7 4.0 %collective-permute-start.5 = (f32[5,4,128]{2,1,0:T(4,128)S(1)}, f32[5,4,128]{2,1,0:T(4,128)S(1)}, u32[]{:S(2)}, u32[]{:S(2)}) collective-permute-start(f32[5,4,128]{2,1,0:T(4,128)S(1)} %get-tuple-element.44.e0_ref), channel_id=1, source_target_pairs={{0,128},{64,192},{128,0},{192,64},{1,129},{65,193},{129,1},{193,65... | collective-permute-start | bytes 30728 | tf_op jit(solution)/shard_map/ppermute | solution.py:410
  48.6 3.2 %collective-permute-start.4 = (f32[5,4,128]{2,1,0:T(4,128)S(1)}, f32[5,4,128]{2,1,0:T(4,128)S(1)}, u32[]{:S(2)}, u32[]{:S(2)}) collective-permute-start(f32[5,4,128]{2,1,0:T(4,128)S(1)} %get-tuple-element.44.e0_ref), channel_id=1, source_target_pairs={{0,64},{64,0},{128,192},{192,128},{1,65},{65,1},{129,193},{193,129... | collective-permute-start | bytes 30728 | tf_op jit(solution)/shard_map/ppermute | solution.py:410

commit v15 on v13

--- a/solution.py
+++ b/solution.py
@@ -424,7 +424,8 @@
         [t, k, inner, faces, x_plan, x_ends, inside, across, z_even, z_odd], scratch=[turned])
     columns = lax.all_to_all(bundle.reshape(NZB * VALUES, 1, NX), "gy", split_axis=0, concat_axis=0, tiled=True)
     (ends,) = call(column_kernel, "column", [(2 * NGY, NX)], [columns.reshape(NGY * VALUES, NX)])
-    ends = lax.all_to_all(ends, "gy", split_axis=0, concat_axis=0, tiled=True)
+    ends = lax.all_to_all(ends.reshape(2 * NGY, 1, NX), "gy", split_axis=0, concat_axis=0, tiled=True)
+    ends = ends.reshape(2 * NZB, NX)
     second, sums, last_row = call(
         second_kernel, "second", [block, (5, NB, NX), (3, NB, NX)], [ends, back, spikes, coeffs, top])
     sums = [sums] + [crossed(sums, "zg", j) for j in range(1, NZG)]

time: 52.6 us -> 52.6 us (level)
  no operation moved by 1% of the time
where the time goes in v15:
time: 52.6 us; the launch traced here: 52.5 us
  blocking collectives  36.3 us (69%)
  starting transfers between devices  8.88 us (17%)
  waiting for transfers between devices  4.43 us (8%)
  Pallas kernels  2.86 us (5%)
    all_to_all x1, blocking collectives, shards(): lax.all_to_all(bundle.reshape(NZB * VALUES, 1, NX), 'gy', split_axis=0, c...  21.3 us
    all_to_all x1, blocking collectives, shards(): lax.all_to_all(ends.reshape(2 * NGY, 1, NX), 'gy', split_axis=0, concat_a...  14.9 us
    ppermute x4, starting transfers between devices, swapped(): return lax.ppermute(x, ('zg', 'gy'), pairs)  5.45 us
    ppermute x3, starting transfers between devices, crossed(): lax.ppermute(x, axis, [(i, i ^ by) for i in range(lax.axis_size(axis))])  3.42 us
    ppermute x3, waiting for transfers between devices, crossed(): lax.ppermute(x, axis, [(i, i ^ by) for i in range(lax.axis_size(axis))])  3.08 us
    pallas_call x7, Pallas kernels, call(): pl.pallas_call(kernel, name=name, out_shape=shapes, in_specs=[pl.BlockSpe...  2.86 us
    ppermute x4, waiting for transfers between devices, swapped(): return lax.ppermute(x, ('zg', 'gy'), pairs)  1.35 us
  transfers between devices with their start and end apart: 7, of which 4 were waited for; matrix products, arithmetic and copies ran while one was open for 0% of the time, Pallas kernels for 1%

profile of v15, /device:TPU:1, one launch (start us, length us, event | category | flops | bytes accessed | tf_op | source)
XLA Modules:
  0.0 52.5 jit_solution(5129194548411023381)
XLA Ops:
  0.0 1.0 %load.1 = (f32[4,64,128]{2,1,0:T(8,128)S(1)}, f32[4,64,128]{2,1,0:T(8,128)S(1)}, f32[2,64,128]{2,1,0:T(8,128)S(1)}, f32[2,64,128]{2,1,0:T(8,128)S(1)}, f32[2,4,1...) custom-call(f32[4,64,128]{2,1,0:T(8,128)} %t_hbm.1, f32[4,64,128]{2,1,0:T(8,128)} %k_hbm.1), custom_call_target="tpu_custom_call" | custom-call | flops 2000000 | bytes 2000000 | tf_op jit(solution)/shard_map/load/pallas_call | solution.py:377
  1.0 3.3 %collective-permute-start = (f32[2,64,128]{2,1,0:T(8,128)S(1)}, f32[2,64,128]{2,1,0:T(8,128)S(1)}, u32[]{:S(2)}, u32[]{:S(2)}) collective-permute-start(f32[2,64,128]{2,1,0:T(8,128)S(1)} %get-tuple-element.31), channel_id=1, source_target_pairs={{0,1},{1,0},{2,3},{3,2},{4,5},{5,4},{6,7},{7,6},{8,9},{9,8},{10,11... | collective-permute-start | bytes 196616 | tf_op jit(solution)/shard_map/ppermute | solution.py:400
  4.3 0.0 collective-permute-start.1
  4.3 1.1 %collective-permute-start.2 = (f32[2,4,128]{2,1,0:T(4,128)S(1)}, f32[2,4,128]{2,1,0:T(4,128)S(1)}, u32[]{:S(2)}, u32[]{:S(2)}) collective-permute-start(f32[2,4,128]{2,1,0:T(4,128)S(1)} %get-tuple-element.33), channel_id=1, source_target_pairs={{0,64},{1,65},{2,66},{3,67},{4,68},{5,69},{6,70},{7,71},{8,72},{9,... | collective-permute-start | bytes 12296 | tf_op jit(solution)/shard_map/ppermute | solution.py:400
  5.4 1.0 %collective-permute-start.3 = (f32[2,4,128]{2,1,0:T(4,128)S(1)}, f32[2,4,128]{2,1,0:T(4,128)S(1)}, u32[]{:S(2)}, u32[]{:S(2)}) collective-permute-start(f32[2,4,128]{2,1,0:T(4,128)S(1)} %get-tuple-element.34), channel_id=1, source_target_pairs={{0,1},{1,0},{2,3},{3,2},{4,5},{5,4},{6,7},{7,6},{8,9},{9,8},{10,11... | collective-permute-start | bytes 12296 | tf_op jit(solution)/shard_map/ppermute | solution.py:400
  6.5 0.5 inner.1
  7.0 0.0 collective-permute-done.2.z_even_ref
  7.0 0.3 collective-permute-done.3.z_odd_ref
  7.3 0.0 collective-permute-done.inside_ref
  7.3 1.0 %collective-permute-done.1.across_ref = f32[2,64,128]{2,1,0:T(8,128)S(1)} collective-permute-done((f32[2,64,128]{2,1,0:T(8,128)S(1)}, f32[2,64,128]{2,1,0:T(8,128)S(1)}, u32[]{:S(2)}, u32[]{:S(2)}) %collective-permute-start.1) | collective-permute-done | bytes 65568 | tf_op jit(solution)/shard_map/ppermute | solution.py:400
  8.3 0.4 first.1
  8.7 21.3 %all_to_all.10 = f32[320,1,128]{2,1,0:T(1,128)S(1)} all-to-all(f32[320,1,128]{2,1,0:T(1,128)S(1)} %bitcast.11), channel_id=1, replica_groups=mesh['zg'=4,'gy'=64] {'gy'}, dimensions={0} | all-to-all | bytes 327680 | tf_op jit(solution)/shard_map/all_to_all | solution.py:425
  30.0 0.1 column.1
  30.1 14.9 %all_to_all.11 = f32[128,1,128]{2,1,0:T(1,128)S(1)} all-to-all(f32[128,1,128]{2,1,0:T(1,128)S(1)} %bitcast.10), channel_id=1, replica_groups=mesh['zg'=4,'gy'=64] {'gy'}, dimensions={0} | all-to-all | bytes 131072 | tf_op jit(solution)/shard_map/all_to_all | solution.py:427
  45.1 0.1 second.1
  45.1 2.6 %collective-permute-start.6 = (f32[5,4,128]{2,1,0:T(4,128)S(1)}, f32[5,4,128]{2,1,0:T(4,128)S(1)}, u32[]{:S(2)}, u32[]{:S(2)}) collective-permute-start(f32[5,4,128]{2,1,0:T(4,128)S(1)} %get-tuple-element.44.e0_ref), channel_id=1, source_target_pairs={{0,192},{64,128},{128,64},{192,0},{1,193},{65,129},{129,65},{193,1... | collective-permute-start | bytes 30728 | tf_op jit(solution)/shard_map/ppermute | solution.py:404
  47.7 0.9 %collective-permute-start.5 = (f32[5,4,128]{2,1,0:T(4,128)S(1)}, f32[5,4,128]{2,1,0:T(4,128)S(1)}, u32[]{:S(2)}, u32[]{:S(2)}) collective-permute-start(f32[5,4,128]{2,1,0:T(4,128)S(1)} %get-tuple-element.44.e0_ref), channel_id=1, source_target_pairs={{0,128},{64,192},{128,0},{192,64},{1,129},{65,193},{129,1},{193,65... | collective-permute-start | bytes 30728 | tf_op jit(solution)/shard_map/ppermute | solution.py:404
  48.6 0.0 collective-permute-start.4
  48.6 0.1 local_z.1.local_ref
  48.6 0.3 collective-permute-done.6.e3_ref
  49.0 2.8 %collective-permute-done.5.e2_ref = f32[5,4,128]{2,1,0:T(4,128)S(1)} collective-permute-done((f32[5,4,128]{2,1,0:T(4,128)S(1)}, f32[5,4,128]{2,1,0:T(4,128)S(1)}, u32[]{:S(2)}, u32[]{:S(2)}) %collective-permute-start.5) | collective-permute-done | bytes 10272 | tf_op jit(solution)/shard_map/ppermute | solution.py:404
  51.7 0.0 collective-permute-done.4.e1_ref
  51.7 0.8 %last.1 = f32[4,64,128]{2,1,0:T(8,128)} custom-call(f32[4,64,128]{2,1,0:T(8,128)S(1)} %local_z.1.local_ref, f32[2,4,64,128]{3,2,1,0:T(8,128)S(1)} %get-tuple-element.37.spikes_ref, f32[3,4,128]{2,1,0:T(4,128)S(1)} %get-tuple-element.43.last_row_ref, f32[5,4,128]{2,1,0:T(4,128)S(1)} %get-tuple-element.44.e0_ref, ...), custom_call_target="tpu_custom_call" | custom-call | flops 2000000 | bytes 2000000 | tf_op jit(solution)/shard_map/last/pallas_call | solution.py:377
Async XLA Ops:
  1.0 6.3 %collective-permute-start = (f32[2,64,128]{2,1,0:T(8,128)S(1)}, f32[2,64,128]{2,1,0:T(8,128)S(1)}, u32[]{:S(2)}, u32[]{:S(2)}) collective-permute-start(f32[2,64,128]{2,1,0:T(8,128)S(1)} %get-tuple-element.31), channel_id=1, source_target_pairs={{0,1},{1,0},{2,3},{3,2},{4,5},{5,4},{6,7},{7,6},{8,9},{9,8},{10,11... | collective-permute-start | bytes 196616 | tf_op jit(solution)/shard_map/ppermute | solution.py:400
  4.3 4.0 %collective-permute-start.1 = (f32[2,64,128]{2,1,0:T(8,128)S(1)}, f32[2,64,128]{2,1,0:T(8,128)S(1)}, u32[]{:S(2)}, u32[]{:S(2)}) collective-permute-start(f32[2,64,128]{2,1,0:T(8,128)S(1)} %get-tuple-element.32), channel_id=1, source_target_pairs={{0,64},{1,2},{2,1},{3,4},{4,3},{5,6},{6,5},{7,8},{8,7},{9,10},{10,... | collective-permute-start | bytes 196616 | tf_op jit(solution)/shard_map/ppermute | solution.py:400
  4.3 2.6 %collective-permute-start.2 = (f32[2,4,128]{2,1,0:T(4,128)S(1)}, f32[2,4,128]{2,1,0:T(4,128)S(1)}, u32[]{:S(2)}, u32[]{:S(2)}) collective-permute-start(f32[2,4,128]{2,1,0:T(4,128)S(1)} %get-tuple-element.33), channel_id=1, source_target_pairs={{0,64},{1,65},{2,66},{3,67},{4,68},{5,69},{6,70},{7,71},{8,72},{9,... | collective-permute-start | bytes 12296 | tf_op jit(solution)/shard_map/ppermute | solution.py:400
  5.4 1.9 %collective-permute-start.3 = (f32[2,4,128]{2,1,0:T(4,128)S(1)}, f32[2,4,128]{2,1,0:T(4,128)S(1)}, u32[]{:S(2)}, u32[]{:S(2)}) collective-permute-start(f32[2,4,128]{2,1,0:T(4,128)S(1)} %get-tuple-element.34), channel_id=1, source_target_pairs={{0,1},{1,0},{2,3},{3,2},{4,5},{5,4},{6,7},{7,6},{8,9},{9,8},{10,11... | collective-permute-start | bytes 12296 | tf_op jit(solution)/shard_map/ppermute | solution.py:400
  45.1 3.8 %collective-permute-start.6 = (f32[5,4,128]{2,1,0:T(4,128)S(1)}, f32[5,4,128]{2,1,0:T(4,128)S(1)}, u32[]{:S(2)}, u32[]{:S(2)}) collective-permute-start(f32[5,4,128]{2,1,0:T(4,128)S(1)} %get-tuple-element.44.e0_ref), channel_id=1, source_target_pairs={{0,192},{64,128},{128,64},{192,0},{1,193},{65,129},{129,65},{193,1... | collective-permute-start | bytes 30728 | tf_op jit(solution)/shard_map/ppermute | solution.py:404
  47.7 4.0 %collective-permute-start.5 = (f32[5,4,128]{2,1,0:T(4,128)S(1)}, f32[5,4,128]{2,1,0:T(4,128)S(1)}, u32[]{:S(2)}, u32[]{:S(2)}) collective-permute-start(f32[5,4,128]{2,1,0:T(4,128)S(1)} %get-tuple-element.44.e0_ref), channel_id=1, source_target_pairs={{0,128},{64,192},{128,0},{192,64},{1,129},{65,193},{129,1},{193,65... | collective-permute-start | bytes 30728 | tf_op jit(solution)/shard_map/ppermute | solution.py:404
  48.6 3.2 %collective-permute-start.4 = (f32[5,4,128]{2,1,0:T(4,128)S(1)}, f32[5,4,128]{2,1,0:T(4,128)S(1)}, u32[]{:S(2)}, u32[]{:S(2)}) collective-permute-start(f32[5,4,128]{2,1,0:T(4,128)S(1)} %get-tuple-element.44.e0_ref), channel_id=1, source_target_pairs={{0,64},{64,0},{128,192},{192,128},{1,65},{65,1},{129,193},{193,129... | collective-permute-start | bytes 30728 | tf_op jit(solution)/shard_map/ppermute | solution.py:404

commit v16 on v13

--- a/solution.py
+++ b/solution.py
@@ -211,7 +211,7 @@
     return chunked(lambda rows: ref[h, rows, :], XC)
 
 
-def first_kernel(t_ref, k_ref, inner_ref, faces_ref, x_plan_ref, x_ends_ref, inside_ref, across_ref, z_even_ref, z_odd_ref,
+def first_kernel(t_ref, k_ref, inner_ref, faces_ref, x_plan_ref, x_ends_ref, inside_ref, across_ref, z_odd_ref, z_even_ref,
                  bundle_ref, back_ref, top_ref, turned):
     gy = lax.axis_index("gy")
     zg = lax.axis_index("zg")
@@ -421,7 +421,7 @@
          (NB, ZC - 1, 3, LANES, NX), (NB,) + ends, (2,) + block, (3, NB, NX)], [t, k], scratch=[turned])
     bundle, back, top = call(
         first_kernel, "first", [(NZB * VALUES, NX), (3, NB - 1, NZB, NX), (NB, NX)],
-        [t, k, inner, faces, x_plan, x_ends, inside, across, z_even, z_odd], scratch=[turned])
+        [t, k, inner, faces, x_plan, x_ends, inside, across, z_odd, z_even], scratch=[turned])
     columns = lax.all_to_all(bundle.reshape(NZB * VALUES, 1, NX), "gy", split_axis=0, concat_axis=0, tiled=True)
     (ends,) = call(column_kernel, "column", [(2 * NGY, NX)], [columns.reshape(NGY * VALUES, NX)])
     ends = lax.all_to_all(ends, "gy", split_axis=0, concat_axis=0, tiled=True)

time: 52.6 us -> 52.6 us (level)
  waiting for transfers between devices: 4.43 us -> 3.8 us
where the time goes in v16:
time: 52.6 us; the launch traced here: 52.5 us
  blocking collectives  36.5 us (69%)
  starting transfers between devices  9.26 us (18%)
  waiting for transfers between devices  3.8 us (7%)
  Pallas kernels  2.86 us (5%)
    all_to_all x1, blocking collectives, shards(): lax.all_to_all(bundle.reshape(NZB * VALUES, 1, NX), 'gy', split_axis=0, c...  21.6 us
    all_to_all x1, blocking collectives, shards(): ends = lax.all_to_all(ends, 'gy', split_axis=0, concat_axis=0, tiled=True)  14.9 us
    ppermute x4, starting transfers between devices, swapped(): return lax.ppermute(x, ('zg', 'gy'), pairs)  5.64 us
    ppermute x3, starting transfers between devices, crossed(): lax.ppermute(x, axis, [(i, i ^ by) for i in range(lax.axis_size(axis))])  3.62 us
    pallas_call x7, Pallas kernels, call(): pl.pallas_call(kernel, name=name, out_shape=shapes, in_specs=[pl.BlockSpe...  2.86 us
    ppermute x3, waiting for transfers between devices, crossed(): lax.ppermute(x, axis, [(i, i ^ by) for i in range(lax.axis_size(axis))])  2.63 us
    ppermute x4, waiting for transfers between devices, swapped(): return lax.ppermute(x, ('zg', 'gy'), pairs)  1.17 us
  transfers between devices with their start and end apart: 7, of which 4 were waited for; matrix products, arithmetic and copies ran while one was open for 0% of the time, Pallas kernels for 1%

profile of v16, /device:TPU:1, one launch (start us, length us, event | category | flops | bytes accessed | tf_op | source)
XLA Modules:
  0.0 52.5 jit_solution(15149329692640492336)
XLA Ops:
  0.0 1.0 %load.1 = (f32[4,64,128]{2,1,0:T(8,128)S(1)}, f32[4,64,128]{2,1,0:T(8,128)S(1)}, f32[2,64,128]{2,1,0:T(8,128)S(1)}, f32[2,64,128]{2,1,0:T(8,128)S(1)}, f32[2,4,1...) custom-call(f32[4,64,128]{2,1,0:T(8,128)} %t_hbm.1, f32[4,64,128]{2,1,0:T(8,128)} %k_hbm.1), custom_call_target="tpu_custom_call" | custom-call | flops 2000000 | bytes 2000000 | tf_op jit(solution)/shard_map/load/pallas_call | solution.py:377
  1.0 3.3 %collective-permute-start = (f32[2,64,128]{2,1,0:T(8,128)S(1)}, f32[2,64,128]{2,1,0:T(8,128)S(1)}, u32[]{:S(2)}, u32[]{:S(2)}) collective-permute-start(f32[2,64,128]{2,1,0:T(8,128)S(1)} %get-tuple-element.31), channel_id=1, source_target_pairs={{0,1},{1,0},{2,3},{3,2},{4,5},{5,4},{6,7},{7,6},{8,9},{9,8},{10,11... | collective-permute-start | bytes 196616 | tf_op jit(solution)/shard_map/ppermute | solution.py:400
  4.3 0.0 collective-permute-start.1
  4.3 0.2 collective-permute-start.2
  4.5 2.1 %collective-permute-start.3 = (f32[2,4,128]{2,1,0:T(4,128)S(1)}, f32[2,4,128]{2,1,0:T(4,128)S(1)}, u32[]{:S(2)}, u32[]{:S(2)}) collective-permute-start(f32[2,4,128]{2,1,0:T(4,128)S(1)} %get-tuple-element.34), channel_id=1, source_target_pairs={{0,64},{1,65},{2,66},{3,67},{4,68},{5,69},{6,70},{7,71},{8,72},{9,... | collective-permute-start | bytes 12296 | tf_op jit(solution)/shard_map/ppermute | solution.py:400
  6.6 0.5 inner.1
  7.1 0.0 collective-permute-done.2.z_odd_ref
  7.1 0.8 %collective-permute-done.3.z_even_ref = f32[2,4,128]{2,1,0:T(4,128)S(1)} collective-permute-done((f32[2,4,128]{2,1,0:T(4,128)S(1)}, f32[2,4,128]{2,1,0:T(4,128)S(1)}, u32[]{:S(2)}, u32[]{:S(2)}) %collective-permute-start.3) | collective-permute-done | bytes 4128 | tf_op jit(solution)/shard_map/ppermute | solution.py:400
  8.0 0.0 collective-permute-done.inside_ref
  8.0 0.3 collective-permute-done.1.across_ref
  8.3 0.4 first.1
  8.7 21.6 %all_to_all.16 = f32[320,1,128]{2,1,0:T(1,128)S(1)} all-to-all(f32[320,1,128]{2,1,0:T(1,128)S(1)} %bitcast.9), channel_id=1, replica_groups=mesh['zg'=4,'gy'=64] {'gy'}, dimensions={0} | all-to-all | bytes 327680 | tf_op jit(solution)/shard_map/all_to_all | solution.py:425
  30.2 0.1 column.1
  30.4 14.9 %all_to_all.17 = f32[64,2,128]{2,1,0:T(2,128)S(1)} all-to-all(f32[64,2,128]{2,1,0:T(2,128)S(1)} %bitcast.8), channel_id=1, replica_groups=mesh['zg'=4,'gy'=64] {'gy'}, dimensions={0} | all-to-all | bytes 131072 | tf_op jit(solution)/shard_map/all_to_all | solution.py:427
  45.3 0.1 second.1
  45.4 2.3 %collective-permute-start.6 = (f32[5,4,128]{2,1,0:T(4,128)S(1)}, f32[5,4,128]{2,1,0:T(4,128)S(1)}, u32[]{:S(2)}, u32[]{:S(2)}) collective-permute-start(f32[5,4,128]{2,1,0:T(4,128)S(1)} %get-tuple-element.44.e0_ref), channel_id=1, source_target_pairs={{0,192},{64,128},{128,64},{192,0},{1,193},{65,129},{129,65},{193,1... | collective-permute-start | bytes 30728 | tf_op jit(solution)/shard_map/ppermute | solution.py:404
  47.7 1.3 %collective-permute-start.5 = (f32[5,4,128]{2,1,0:T(4,128)S(1)}, f32[5,4,128]{2,1,0:T(4,128)S(1)}, u32[]{:S(2)}, u32[]{:S(2)}) collective-permute-start(f32[5,4,128]{2,1,0:T(4,128)S(1)} %get-tuple-element.44.e0_ref), channel_id=1, source_target_pairs={{0,128},{64,192},{128,0},{192,64},{1,129},{65,193},{129,1},{193,65... | collective-permute-start | bytes 30728 | tf_op jit(solution)/shard_map/ppermute | solution.py:404
  49.0 0.0 collective-permute-start.4
  49.0 0.1 local_z.1.local_ref
  49.1 0.1 collective-permute-done.6.e3_ref
  49.2 2.5 %collective-permute-done.5.e2_ref = f32[5,4,128]{2,1,0:T(4,128)S(1)} collective-permute-done((f32[5,4,128]{2,1,0:T(4,128)S(1)}, f32[5,4,128]{2,1,0:T(4,128)S(1)}, u32[]{:S(2)}, u32[]{:S(2)}) %collective-permute-start.5) | collective-permute-done | bytes 10272 | tf_op jit(solution)/shard_map/ppermute | solution.py:404
  51.7 0.0 collective-permute-done.4.e1_ref
  51.7 0.8 %last.1 = f32[4,64,128]{2,1,0:T(8,128)} custom-call(f32[4,64,128]{2,1,0:T(8,128)S(1)} %local_z.1.local_ref, f32[2,4,64,128]{3,2,1,0:T(8,128)S(1)} %get-tuple-element.37.spikes_ref, f32[3,4,128]{2,1,0:T(4,128)S(1)} %get-tuple-element.43.last_row_ref, f32[5,4,128]{2,1,0:T(4,128)S(1)} %get-tuple-element.44.e0_ref, ...), custom_call_target="tpu_custom_call" | custom-call | flops 2000000 | bytes 2000000 | tf_op jit(solution)/shard_map/last/pallas_call | solution.py:377
Async XLA Ops:
  1.0 7.0 %collective-permute-start = (f32[2,64,128]{2,1,0:T(8,128)S(1)}, f32[2,64,128]{2,1,0:T(8,128)S(1)}, u32[]{:S(2)}, u32[]{:S(2)}) collective-permute-start(f32[2,64,128]{2,1,0:T(8,128)S(1)} %get-tuple-element.31), channel_id=1, source_target_pairs={{0,1},{1,0},{2,3},{3,2},{4,5},{5,4},{6,7},{7,6},{8,9},{9,8},{10,11... | collective-permute-start | bytes 196616 | tf_op jit(solution)/shard_map/ppermute | solution.py:400
  4.3 4.0 %collective-permute-start.1 = (f32[2,64,128]{2,1,0:T(8,128)S(1)}, f32[2,64,128]{2,1,0:T(8,128)S(1)}, u32[]{:S(2)}, u32[]{:S(2)}) collective-permute-start(f32[2,64,128]{2,1,0:T(8,128)S(1)} %get-tuple-element.32), channel_id=1, source_target_pairs={{0,64},{1,2},{2,1},{3,4},{4,3},{5,6},{6,5},{7,8},{8,7},{9,10},{10,... | collective-permute-start | bytes 196616 | tf_op jit(solution)/shard_map/ppermute | solution.py:400
  4.3 2.8 %collective-permute-start.2 = (f32[2,4,128]{2,1,0:T(4,128)S(1)}, f32[2,4,128]{2,1,0:T(4,128)S(1)}, u32[]{:S(2)}, u32[]{:S(2)}) collective-permute-start(f32[2,4,128]{2,1,0:T(4,128)S(1)} %get-tuple-element.33), channel_id=1, source_target_pairs={{0,1},{1,0},{2,3},{3,2},{4,5},{5,4},{6,7},{7,6},{8,9},{9,8},{10,11... | collective-permute-start | bytes 12296 | tf_op jit(solution)/shard_map/ppermute | solution.py:400
  4.5 3.4 %collective-permute-start.3 = (f32[2,4,128]{2,1,0:T(4,128)S(1)}, f32[2,4,128]{2,1,0:T(4,128)S(1)}, u32[]{:S(2)}, u32[]{:S(2)}) collective-permute-start(f32[2,4,128]{2,1,0:T(4,128)S(1)} %get-tuple-element.34), channel_id=1, source_target_pairs={{0,64},{1,65},{2,66},{3,67},{4,68},{5,69},{6,70},{7,71},{8,72},{9,... | collective-permute-start | bytes 12296 | tf_op jit(solution)/shard_map/ppermute | solution.py:400
  45.4 3.8 %collective-permute-start.6 = (f32[5,4,128]{2,1,0:T(4,128)S(1)}, f32[5,4,128]{2,1,0:T(4,128)S(1)}, u32[]{:S(2)}, u32[]{:S(2)}) collective-permute-start(f32[5,4,128]{2,1,0:T(4,128)S(1)} %get-tuple-element.44.e0_ref), channel_id=1, source_target_pairs={{0,192},{64,128},{128,64},{192,0},{1,193},{65,129},{129,65},{193,1... | collective-permute-start | bytes 30728 | tf_op jit(solution)/shard_map/ppermute | solution.py:404
  47.7 4.0 %collective-permute-start.5 = (f32[5,4,128]{2,1,0:T(4,128)S(1)}, f32[5,4,128]{2,1,0:T(4,128)S(1)}, u32[]{:S(2)}, u32[]{:S(2)}) collective-permute-start(f32[5,4,128]{2,1,0:T(4,128)S(1)} %get-tuple-element.44.e0_ref), channel_id=1, source_target_pairs={{0,128},{64,192},{128,0},{192,64},{1,129},{65,193},{129,1},{193,65... | collective-permute-start | bytes 30728 | tf_op jit(solution)/shard_map/ppermute | solution.py:404
  49.0 2.7 %collective-permute-start.4 = (f32[5,4,128]{2,1,0:T(4,128)S(1)}, f32[5,4,128]{2,1,0:T(4,128)S(1)}, u32[]{:S(2)}, u32[]{:S(2)}) collective-permute-start(f32[5,4,128]{2,1,0:T(4,128)S(1)} %get-tuple-element.44.e0_ref), channel_id=1, source_target_pairs={{0,64},{64,0},{128,192},{192,128},{1,65},{65,1},{129,193},{193,129... | collective-permute-start | bytes 30728 | tf_op jit(solution)/shard_map/ppermute | solution.py:404

commit v17 on v13

--- a/solution.py
+++ b/solution.py
@@ -14,7 +14,7 @@
 STRIDES = (1, 2, 4)
 VALUES = 5
 
-LOAD_GRANT = 54816
+HALO_GRANT, LOAD_GRANT = 55000, 54940
 
 
 def face(k, q):
@@ -126,20 +126,35 @@
     return b * factors[2 * len(STRIDES)]
 
 
-def load_kernel(t_hbm, k_hbm, t_ref, k_ref, across_ref, inside_ref, z_even_ref, z_odd_ref, sems):
+def halo_kernel(t_hbm, k_hbm, across_ref, inside_ref, z_even_ref, z_odd_ref, edges, sems):
     odd = lax.rem(lax.axis_index("gy"), 2)
     upper = lax.rem(lax.axis_index("zg"), 2) == 1
+    copies = []
+    for j, array in enumerate((t_hbm, k_hbm)):
+        moves = (
+            (array.at[(1 - odd) * (NB - 1)], inside_ref.at[j]),
+            (array.at[odd * (NB - 1)], across_ref.at[j]),
+            (array.at[:, pl.ds(0, LANES)], edges.at[j, 0]),
+            (array.at[:, pl.ds(NZB - LANES, LANES)], edges.at[j, 1]),
+        )
+        for n, (source, target) in enumerate(moves):
+            copies.append(pltpu.make_async_copy(source, target, sems.at[j, n]))
+            copies[-1].start()
+    for copy in copies:
+        copy.wait()
+    for j in range(2):
+        for y in range(NB):
+            first, last = edges[j, 0, y, :1], edges[j, 1, y, LANES - 1:]
+            z_even_ref[j, y:y + 1] = jnp.where(upper, first, last)
+            z_odd_ref[j, y:y + 1] = jnp.where(upper, last, first)
+
+
+def load_kernel(t_hbm, k_hbm, t_ref, k_ref, sems):
     copies = [pltpu.make_async_copy(t_hbm, t_ref, sems.at[0]), pltpu.make_async_copy(k_hbm, k_ref, sems.at[1])]
     for copy in copies:
         copy.start()
-    for j, (copy, ref) in enumerate(zip(copies, (t_ref, k_ref))):
+    for copy in copies:
         copy.wait()
-        across_ref[j] = ref[odd * (NB - 1)]
-        inside_ref[j] = ref[(1 - odd) * (NB - 1)]
-        for y in range(NB):
-            first, last = ref[y, :1], ref[y, NZB - 1:]
-            z_even_ref[j, y:y + 1] = jnp.where(upper, first, last)
-            z_odd_ref[j, y:y + 1] = jnp.where(upper, last, first)
 
 
 def block_row(ref, *at):
@@ -406,9 +421,11 @@
 
 def shards(t, k):
     block = (NB, NZB, NX)
-    t, k, across, inside, z_even, z_odd = call(
-        load_kernel, "load", [block, block, (2, NZB, NX), (2, NZB, NX), (2, NB, NX), (2, NB, NX)], [t, k],
-        scratch=[pltpu.SemaphoreType.DMA((2,))], granted=LOAD_GRANT)
+    across, inside, z_even, z_odd = call(
+        halo_kernel, "halo", [(2, NZB, NX), (2, NZB, NX), (2, NB, NX), (2, NB, NX)], [t, k],
+        scratch=[pltpu.VMEM((2, 2, NB, LANES, NX), jnp.float32), pltpu.SemaphoreType.DMA((2, 4))], granted=HALO_GRANT)
+    t, k = call(load_kernel, "load", [block, block], [t, k],
+                scratch=[pltpu.SemaphoreType.DMA((2,))], granted=LOAD_GRANT)
     across = swapped(across, "gy", 1)
     z_odd = swapped(z_odd, "zg", 1)
     z_even = swapped(z_even, "zg", 0)

time: 52.6 us -> 52.6 us (level)
  waiting for transfers between devices: 4.43 us -> 3.42 us
  Pallas kernels: 2.86 us -> 3.78 us
    ppermute x4, waiting for transfers between devices: 1.35 us -> 0.34 us  [swapped(): return lax.ppermute(x, ('zg', 'gy'), pairs)]
    pallas_call x7 -> x8, Pallas kernels: 2.86 us -> 3.78 us  [call(): pl.pallas_call(kernel, name=name, out_shape=shapes, in_specs=[pl.BlockSpe...]
  transfers between devices with their start and end apart: 7 -> 7, of which waited for: 4 -> 3; matrix products, arithmetic and copies ran while one was open for 0% -> 0% of each run, Pallas kernels for 1% -> 3%
where the time goes in v17:
time: 52.6 us; the launch traced here: 52.4 us
  blocking collectives  36.3 us (69%)
  starting transfers between devices  8.88 us (17%)
  Pallas kernels  3.78 us (7%)
  waiting for transfers between devices  3.42 us (7%)
    all_to_all x1, blocking collectives, shards(): lax.all_to_all(bundle.reshape(NZB * VALUES, 1, NX), 'gy', split_axis=0, c...  21.3 us
    all_to_all x1, blocking collectives, shards(): ends = lax.all_to_all(ends, 'gy', split_axis=0, concat_axis=0, tiled=True)  14.9 us
    ppermute x4, starting transfers between devices, swapped(): return lax.ppermute(x, ('zg', 'gy'), pairs)  5.45 us
    pallas_call x8, Pallas kernels, call(): pl.pallas_call(kernel, name=name, out_shape=shapes, in_specs=[pl.BlockSpe...  3.78 us
    ppermute x3, starting transfers between devices, crossed(): lax.ppermute(x, axis, [(i, i ^ by) for i in range(lax.axis_size(axis))])  3.42 us
    ppermute x3, waiting for transfers between devices, crossed(): lax.ppermute(x, axis, [(i, i ^ by) for i in range(lax.axis_size(axis))])  3.08 us
  transfers between devices with their start and end apart: 7, of which 3 were waited for; matrix products, arithmetic and copies ran while one was open for 0% of the time, Pallas kernels for 3%

profile of v17, /device:TPU:1, one launch (start us, length us, event | category | flops | bytes accessed | tf_op | source)
XLA Modules:
  0.0 52.4 jit_solution(12329859101787528647)
XLA Ops:
  0.0 0.9 %halo.1 = (f32[2,64,128]{2,1,0:T(8,128)S(1)}, f32[2,64,128]{2,1,0:T(8,128)S(1)}, f32[2,4,128]{2,1,0:T(4,128)S(1)}, f32[2,4,128]{2,1,0:T(4,128)S(1)}) custom-call(f32[4,64,128]{2,1,0:T(8,128)} %t_hbm.3, f32[4,64,128]{2,1,0:T(8,128)} %k_hbm.3), custom_call_target="tpu_custom_call" | custom-call | flops 2000000 | bytes 2000000 | tf_op jit(solution)/shard_map/halo/pallas_call | solution.py:392
  0.9 3.3 %collective-permute-start = (f32[2,64,128]{2,1,0:T(8,128)S(1)}, f32[2,64,128]{2,1,0:T(8,128)S(1)}, u32[]{:S(2)}, u32[]{:S(2)}) collective-permute-start(f32[2,64,128]{2,1,0:T(8,128)S(1)} %get-tuple-element.31), channel_id=1, source_target_pairs={{0,1},{1,0},{2,3},{3,2},{4,5},{5,4},{6,7},{7,6},{8,9},{9,8},{10,11... | collective-permute-start | bytes 196616 | tf_op jit(solution)/shard_map/ppermute | solution.py:415
  4.3 0.0 collective-permute-start.1
  4.3 1.1 %collective-permute-start.2 = (f32[2,4,128]{2,1,0:T(4,128)S(1)}, f32[2,4,128]{2,1,0:T(4,128)S(1)}, u32[]{:S(2)}, u32[]{:S(2)}) collective-permute-start(f32[2,4,128]{2,1,0:T(4,128)S(1)} %get-tuple-element.33), channel_id=1, source_target_pairs={{0,64},{1,65},{2,66},{3,67},{4,68},{5,69},{6,70},{7,71},{8,72},{9,... | collective-permute-start | bytes 12296 | tf_op jit(solution)/shard_map/ppermute | solution.py:415
  5.4 1.0 %collective-permute-start.3 = (f32[2,4,128]{2,1,0:T(4,128)S(1)}, f32[2,4,128]{2,1,0:T(4,128)S(1)}, u32[]{:S(2)}, u32[]{:S(2)}) collective-permute-start(f32[2,4,128]{2,1,0:T(4,128)S(1)} %get-tuple-element.34), channel_id=1, source_target_pairs={{0,1},{1,0},{2,3},{3,2},{4,5},{5,4},{6,7},{7,6},{8,9},{9,8},{10,11... | collective-permute-start | bytes 12296 | tf_op jit(solution)/shard_map/ppermute | solution.py:415
  6.4 1.0 %load.1 = (f32[4,64,128]{2,1,0:T(8,128)S(1)}, f32[4,64,128]{2,1,0:T(8,128)S(1)}) custom-call(f32[4,64,128]{2,1,0:T(8,128)} %t_hbm.3, f32[4,64,128]{2,1,0:T(8,128)} %k_hbm.3), custom_call_target="tpu_custom_call" | custom-call | flops 2000000 | bytes 2000000 | tf_op jit(solution)/shard_map/load/pallas_call | solution.py:392
  7.4 0.5 inner.1
  7.9 0.0 collective-permute-done.2.z_even_ref
  7.9 0.0 collective-permute-done.3.z_odd_ref
  7.9 0.0 collective-permute-done.inside_ref
  7.9 0.3 collective-permute-done.1.across_ref
  8.2 0.4 first.1
  8.6 21.3 %all_to_all.16 = f32[320,1,128]{2,1,0:T(1,128)S(1)} all-to-all(f32[320,1,128]{2,1,0:T(1,128)S(1)} %bitcast.9), channel_id=1, replica_groups=mesh['zg'=4,'gy'=64] {'gy'}, dimensions={0} | all-to-all | bytes 327680 | tf_op jit(solution)/shard_map/all_to_all | solution.py:442
  29.9 0.1 column.1
  30.0 14.9 %all_to_all.17 = f32[64,2,128]{2,1,0:T(2,128)S(1)} all-to-all(f32[64,2,128]{2,1,0:T(2,128)S(1)} %bitcast.8), channel_id=1, replica_groups=mesh['zg'=4,'gy'=64] {'gy'}, dimensions={0} | all-to-all | bytes 131072 | tf_op jit(solution)/shard_map/all_to_all | solution.py:444
  45.0 0.1 second.1
  45.1 2.6 %collective-permute-start.6 = (f32[5,4,128]{2,1,0:T(4,128)S(1)}, f32[5,4,128]{2,1,0:T(4,128)S(1)}, u32[]{:S(2)}, u32[]{:S(2)}) collective-permute-start(f32[5,4,128]{2,1,0:T(4,128)S(1)} %get-tuple-element.44.e0_ref), channel_id=1, source_target_pairs={{0,192},{64,128},{128,64},{192,0},{1,193},{65,129},{129,65},{193,1... | collective-permute-start | bytes 30728 | tf_op jit(solution)/shard_map/ppermute | solution.py:419
  47.6 0.9 %collective-permute-start.5 = (f32[5,4,128]{2,1,0:T(4,128)S(1)}, f32[5,4,128]{2,1,0:T(4,128)S(1)}, u32[]{:S(2)}, u32[]{:S(2)}) collective-permute-start(f32[5,4,128]{2,1,0:T(4,128)S(1)} %get-tuple-element.44.e0_ref), channel_id=1, source_target_pairs={{0,128},{64,192},{128,0},{192,64},{1,129},{65,193},{129,1},{193,65... | collective-permute-start | bytes 30728 | tf_op jit(solution)/shard_map/ppermute | solution.py:419
  48.5 0.0 collective-permute-start.4
  48.5 0.1 local_z.1.local_ref
  48.6 0.3 collective-permute-done.6.e3_ref
  48.9 2.8 %collective-permute-done.5.e2_ref = f32[5,4,128]{2,1,0:T(4,128)S(1)} collective-permute-done((f32[5,4,128]{2,1,0:T(4,128)S(1)}, f32[5,4,128]{2,1,0:T(4,128)S(1)}, u32[]{:S(2)}, u32[]{:S(2)}) %collective-permute-start.5) | collective-permute-done | bytes 10272 | tf_op jit(solution)/shard_map/ppermute | solution.py:419
  51.7 0.0 collective-permute-done.4.e1_ref
  51.7 0.8 %last.1 = f32[4,64,128]{2,1,0:T(8,128)} custom-call(f32[4,64,128]{2,1,0:T(8,128)S(1)} %local_z.1.local_ref, f32[2,4,64,128]{3,2,1,0:T(8,128)S(1)} %get-tuple-element.37.spikes_ref, f32[3,4,128]{2,1,0:T(4,128)S(1)} %get-tuple-element.43.last_row_ref, f32[5,4,128]{2,1,0:T(4,128)S(1)} %get-tuple-element.44.e0_ref, ...), custom_call_target="tpu_custom_call" | custom-call | flops 2000000 | bytes 2000000 | tf_op jit(solution)/shard_map/last/pallas_call | solution.py:392
Async XLA Ops:
  0.9 7.0 %collective-permute-start = (f32[2,64,128]{2,1,0:T(8,128)S(1)}, f32[2,64,128]{2,1,0:T(8,128)S(1)}, u32[]{:S(2)}, u32[]{:S(2)}) collective-permute-start(f32[2,64,128]{2,1,0:T(8,128)S(1)} %get-tuple-element.31), channel_id=1, source_target_pairs={{0,1},{1,0},{2,3},{3,2},{4,5},{5,4},{6,7},{7,6},{8,9},{9,8},{10,11... | collective-permute-start | bytes 196616 | tf_op jit(solution)/shard_map/ppermute | solution.py:415
  4.3 4.0 %collective-permute-start.1 = (f32[2,64,128]{2,1,0:T(8,128)S(1)}, f32[2,64,128]{2,1,0:T(8,128)S(1)}, u32[]{:S(2)}, u32[]{:S(2)}) collective-permute-start(f32[2,64,128]{2,1,0:T(8,128)S(1)} %get-tuple-element.32), channel_id=1, source_target_pairs={{0,64},{1,2},{2,1},{3,4},{4,3},{5,6},{6,5},{7,8},{8,7},{9,10},{10,... | collective-permute-start | bytes 196616 | tf_op jit(solution)/shard_map/ppermute | solution.py:415
  4.3 3.6 %collective-permute-start.2 = (f32[2,4,128]{2,1,0:T(4,128)S(1)}, f32[2,4,128]{2,1,0:T(4,128)S(1)}, u32[]{:S(2)}, u32[]{:S(2)}) collective-permute-start(f32[2,4,128]{2,1,0:T(4,128)S(1)} %get-tuple-element.33), channel_id=1, source_target_pairs={{0,64},{1,65},{2,66},{3,67},{4,68},{5,69},{6,70},{7,71},{8,72},{9,... | collective-permute-start | bytes 12296 | tf_op jit(solution)/shard_map/ppermute | solution.py:415
  5.4 2.5 %collective-permute-start.3 = (f32[2,4,128]{2,1,0:T(4,128)S(1)}, f32[2,4,128]{2,1,0:T(4,128)S(1)}, u32[]{:S(2)}, u32[]{:S(2)}) collective-permute-start(f32[2,4,128]{2,1,0:T(4,128)S(1)} %get-tuple-element.34), channel_id=1, source_target_pairs={{0,1},{1,0},{2,3},{3,2},{4,5},{5,4},{6,7},{7,6},{8,9},{9,8},{10,11... | collective-permute-start | bytes 12296 | tf_op jit(solution)/shard_map/ppermute | solution.py:415
  45.1 3.8 %collective-permute-start.6 = (f32[5,4,128]{2,1,0:T(4,128)S(1)}, f32[5,4,128]{2,1,0:T(4,128)S(1)}, u32[]{:S(2)}, u32[]{:S(2)}) collective-permute-start(f32[5,4,128]{2,1,0:T(4,128)S(1)} %get-tuple-element.44.e0_ref), channel_id=1, source_target_pairs={{0,192},{64,128},{128,64},{192,0},{1,193},{65,129},{129,65},{193,1... | collective-permute-start | bytes 30728 | tf_op jit(solution)/shard_map/ppermute | solution.py:419
  47.6 4.0 %collective-permute-start.5 = (f32[5,4,128]{2,1,0:T(4,128)S(1)}, f32[5,4,128]{2,1,0:T(4,128)S(1)}, u32[]{:S(2)}, u32[]{:S(2)}) collective-permute-start(f32[5,4,128]{2,1,0:T(4,128)S(1)} %get-tuple-element.44.e0_ref), channel_id=1, source_target_pairs={{0,128},{64,192},{128,0},{192,64},{1,129},{65,193},{129,1},{193,65... | collective-permute-start | bytes 30728 | tf_op jit(solution)/shard_map/ppermute | solution.py:419
  48.5 3.2 %collective-permute-start.4 = (f32[5,4,128]{2,1,0:T(4,128)S(1)}, f32[5,4,128]{2,1,0:T(4,128)S(1)}, u32[]{:S(2)}, u32[]{:S(2)}) collective-permute-start(f32[5,4,128]{2,1,0:T(4,128)S(1)} %get-tuple-element.44.e0_ref), channel_id=1, source_target_pairs={{0,64},{64,0},{128,192},{192,128},{1,65},{65,1},{129,193},{193,129... | collective-permute-start | bytes 30728 | tf_op jit(solution)/shard_map/ppermute | solution.py:419

commit v18 on v17

--- a/solution.py
+++ b/solution.py
@@ -161,13 +161,14 @@
     return chunked(lambda rows: ref[at + (rows, slice(None))], ZC)
 
 
-def inner_kernel(t_ref, k_ref, inner_ref, faces_ref, x_plan_ref, x_ends_ref, z_plan_ref, z_ends_ref, spikes_ref,
+def inner_kernel(t_ref, k_ref, inner_ref, y_plan_ref, x_plan_ref, x_ends_ref, z_plan_ref, z_ends_ref, spikes_ref,
                  coeffs_ref, turned):
     lane = rows_of((NZB, NX), 1)
     row = rows_of((NZB, NX), 0)
     chunk = rows_of((LANES, NX), 0)
     ts = [block_row(t_ref, y) for y in range(NB)]
     ks = [block_row(k_ref, y) for y in range(NB)]
+    faces = []
     flux_y = None
     for y in range(NB):
         k, t = ks[y], ts[y]
@@ -181,7 +182,7 @@
             total = total - flux_y
         if y < NB - 1:
             next_face = face(ks[y + 1], k)
-            faces_ref[y] = next_face
+            faces.append(next_face)
             flux_y = next_face * (ts[y + 1] - t)
             total = total + flux_y
         inner_ref[y] = total
@@ -209,6 +210,17 @@
         following = jnp.where(chunk == LANES - 1, 1.0, shift(rho, -1, 0))
         spikes_ref[1, y] = jnp.concatenate(unfold(plan, None, rho, following), axis=0)
 
+    g1, g2, g3 = faces
+    i1 = 1.0 / (1.0 + g1 + g2)
+    left1, right1 = g1 * i1, g2 * i1
+    m2 = 1.0 + right1
+    a2 = g1 * right1
+    i2 = 1.0 / (m2 + a2 + g3)
+    left2, right2 = a2 * i2, g3 * i2
+    y_plan = (i1, left1, right1, i2, left2, right2, 1.0 + left1 + left2 * m2, 1.0 + right2 * m2, a2 * right2)
+    for j, entry in enumerate(y_plan):
+        y_plan_ref[j] = entry
+
     for h in range(NB // 2):
         turned[h] = jnp.concatenate(ks[2 * h:2 * h + 2], axis=0).T
         k = block_line(turned, h)
@@ -226,7 +238,7 @@
     return chunked(lambda rows: ref[h, rows, :], XC)
 
 
-def first_kernel(t_ref, k_ref, inner_ref, faces_ref, x_plan_ref, x_ends_ref, inside_ref, across_ref, z_even_ref, z_odd_ref,
+def first_kernel(t_ref, k_ref, inner_ref, y_plan_ref, x_plan_ref, x_ends_ref, inside_ref, across_ref, z_even_ref, z_odd_ref,
                  bundle_ref, back_ref, top_ref, turned):
     gy = lax.axis_index("gy")
     zg = lax.axis_index("zg")
@@ -270,21 +282,11 @@
         b = turned[h].T
         solved += [b[:NZB], b[NZB:]]
     b0, b1, b2, b3 = solved
-    g1, g2, g3 = faces_ref[0], faces_ref[1], faces_ref[2]
-    i1 = 1.0 / (1.0 + g1 + g2)
-    left, right = g1 * i1, g2 * i1
-    source = b0 + left * b1
-    b2 = b2 + right * b1
-    leak = 1.0 + left
-    m2 = 1.0 + right
-    a2 = g1 * right
-    i2 = 1.0 / (m2 + a2 + g3)
-    left, right = a2 * i2, g3 * i2
-    source = source + left * b2
-    b3 = b3 + right * b2
-    leak = leak + left * m2
-    m3 = 1.0 + right * m2
-    a3 = a2 * right
+    i1, left1, right1, i2, left2, right2, leak, m3, a3 = [y_plan_ref[j] for j in range(9)]
+    source = b0 + left1 * b1
+    b2 = b2 + right1 * b1
+    source = source + left2 * b2
+    b3 = b3 + right2 * b2
     i3 = 1.0 / (m3 + a3 + g4)
     left, right = a3 * i3, g4 * i3
 
@@ -299,9 +301,9 @@
     put(4, right * b3)
     beta, lam, rho = b3 * i3, left, right
     back_ref[0, 2], back_ref[1, 2], back_ref[2, 2] = beta, lam, rho
-    beta, lam, rho = (b2 + g3 * beta) * i2, (a2 + g3 * lam) * i2, g3 * rho * i2
+    beta, lam, rho = b2 * i2 + right2 * beta, left2 + right2 * lam, right2 * rho
     back_ref[0, 1], back_ref[1, 1], back_ref[2, 1] = beta, lam, rho
-    beta, lam, rho = (b1 + g2 * beta) * i1, (g1 + g2 * lam) * i1, g2 * rho * i1
+    beta, lam, rho = b1 * i1 + right1 * beta, left1 + right1 * lam, right1 * rho
     back_ref[0, 0], back_ref[1, 0], back_ref[2, 0] = beta, lam, rho
 
 
@@ -432,13 +434,13 @@
     inside = swapped(inside, "gy", 0)
     turned = pltpu.VMEM((NB // 2, NX, 2 * NZB), jnp.float32)
     ends = (2 * len(STRIDES) + 1, LANES, NX)
-    inner, faces, x_plan, x_ends, z_plan, z_ends, spikes, coeffs = call(
+    inner, y_plan, x_plan, x_ends, z_plan, z_ends, spikes, coeffs = call(
         inner_kernel, "inner",
-        [block, (NB - 1, NZB, NX), (NB // 2, XC - 1, 3, LANES, 2 * NZB), (NB // 2,) + ends,
+        [block, (9, NZB, NX), (NB // 2, XC - 1, 3, LANES, 2 * NZB), (NB // 2,) + ends,
          (NB, ZC - 1, 3, LANES, NX), (NB,) + ends, (2,) + block, (3, NB, NX)], [t, k], scratch=[turned])
     bundle, back, top = call(
         first_kernel, "first", [(NZB * VALUES, NX), (3, NB - 1, NZB, NX), (NB, NX)],
-        [t, k, inner, faces, x_plan, x_ends, inside, across, z_even, z_odd], scratch=[turned])
+        [t, k, inner, y_plan, x_plan, x_ends, inside, across, z_even, z_odd], scratch=[turned])
     columns = lax.all_to_all(bundle.reshape(NZB * VALUES, 1, NX), "gy", split_axis=0, concat_axis=0, tiled=True)
     (ends,) = call(column_kernel, "column", [(2 * NGY, NX)], [columns.reshape(NGY * VALUES, NX)])
     ends = lax.all_to_all(ends, "gy", split_axis=0, concat_axis=0, tiled=True)

time: 52.6 us -> 52.6 us (level)
  no operation moved by 1% of the time
where the time goes in v18:
time: 52.6 us; the launch traced here: 52.4 us
  blocking collectives  36.3 us (69%)
  starting transfers between devices  8.88 us (17%)
  Pallas kernels  3.81 us (7%)
  waiting for transfers between devices  3.39 us (6%)
    all_to_all x1, blocking collectives, shards(): lax.all_to_all(bundle.reshape(NZB * VALUES, 1, NX), 'gy', split_axis=0, c...  21.3 us
    all_to_all x1, blocking collectives, shards(): ends = lax.all_to_all(ends, 'gy', split_axis=0, concat_axis=0, tiled=True)  14.9 us
    ppermute x4, starting transfers between devices, swapped(): return lax.ppermute(x, ('zg', 'gy'), pairs)  5.45 us
    pallas_call x8, Pallas kernels, call(): pl.pallas_call(kernel, name=name, out_shape=shapes, in_specs=[pl.BlockSpe...  3.81 us
    ppermute x3, starting transfers between devices, crossed(): lax.ppermute(x, axis, [(i, i ^ by) for i in range(lax.axis_size(axis))])  3.42 us
    ppermute x3, waiting for transfers between devices, crossed(): lax.ppermute(x, axis, [(i, i ^ by) for i in range(lax.axis_size(axis))])  3.08 us
  transfers between devices with their start and end apart: 7, of which 3 were waited for; matrix products, arithmetic and copies ran while one was open for 0% of the time, Pallas kernels for 3%

profile of v18, /device:TPU:1, one launch (start us, length us, event | category | flops | bytes accessed | tf_op | source)
XLA Modules:
  0.0 52.4 jit_solution(17290570085371142630)
XLA Ops:
  0.0 0.9 %halo.1 = (f32[2,64,128]{2,1,0:T(8,128)S(1)}, f32[2,64,128]{2,1,0:T(8,128)S(1)}, f32[2,4,128]{2,1,0:T(4,128)S(1)}, f32[2,4,128]{2,1,0:T(4,128)S(1)}) custom-call(f32[4,64,128]{2,1,0:T(8,128)} %t_hbm.3, f32[4,64,128]{2,1,0:T(8,128)} %k_hbm.3), custom_call_target="tpu_custom_call" | custom-call | flops 2000000 | bytes 2000000 | tf_op jit(solution)/shard_map/halo/pallas_call | solution.py:394
  0.9 3.3 %collective-permute-start = (f32[2,64,128]{2,1,0:T(8,128)S(1)}, f32[2,64,128]{2,1,0:T(8,128)S(1)}, u32[]{:S(2)}, u32[]{:S(2)}) collective-permute-start(f32[2,64,128]{2,1,0:T(8,128)S(1)} %get-tuple-element.31), channel_id=1, source_target_pairs={{0,1},{1,0},{2,3},{3,2},{4,5},{5,4},{6,7},{7,6},{8,9},{9,8},{10,11... | collective-permute-start | bytes 196616 | tf_op jit(solution)/shard_map/ppermute | solution.py:417
  4.3 0.0 collective-permute-start.1
  4.3 1.1 %collective-permute-start.2 = (f32[2,4,128]{2,1,0:T(4,128)S(1)}, f32[2,4,128]{2,1,0:T(4,128)S(1)}, u32[]{:S(2)}, u32[]{:S(2)}) collective-permute-start(f32[2,4,128]{2,1,0:T(4,128)S(1)} %get-tuple-element.33), channel_id=1, source_target_pairs={{0,64},{1,65},{2,66},{3,67},{4,68},{5,69},{6,70},{7,71},{8,72},{9,... | collective-permute-start | bytes 12296 | tf_op jit(solution)/shard_map/ppermute | solution.py:417
  5.4 1.0 %collective-permute-start.3 = (f32[2,4,128]{2,1,0:T(4,128)S(1)}, f32[2,4,128]{2,1,0:T(4,128)S(1)}, u32[]{:S(2)}, u32[]{:S(2)}) collective-permute-start(f32[2,4,128]{2,1,0:T(4,128)S(1)} %get-tuple-element.34), channel_id=1, source_target_pairs={{0,1},{1,0},{2,3},{3,2},{4,5},{5,4},{6,7},{7,6},{8,9},{9,8},{10,11... | collective-permute-start | bytes 12296 | tf_op jit(solution)/shard_map/ppermute | solution.py:417
  6.4 1.0 %load.1 = (f32[4,64,128]{2,1,0:T(8,128)S(1)}, f32[4,64,128]{2,1,0:T(8,128)S(1)}) custom-call(f32[4,64,128]{2,1,0:T(8,128)} %t_hbm.3, f32[4,64,128]{2,1,0:T(8,128)} %k_hbm.3), custom_call_target="tpu_custom_call" | custom-call | flops 2000000 | bytes 2000000 | tf_op jit(solution)/shard_map/load/pallas_call | solution.py:394
  7.4 0.5 %inner.1 = (f32[4,64,128]{2,1,0:T(8,128)S(1)}, f32[9,64,128]{2,1,0:T(8,128)S(1)}, f32[2,15,3,8,128]{4,3,2,1,0:T(8,128)S(1)}, f32[2,7,8,128]{3,2,1,0:T(8,128)S(1)...) custom-call(f32[4,64,128]{2,1,0:T(8,128)S(1)} %get-tuple-element.25., ...), custom_call_target="tpu_custom_call" | custom-call | flops 2000000 | bytes 2000000 | tf_op jit(solution)/shard_map/inner/pallas_call | solution.py:394
  7.9 0.0 collective-permute-done.2.z_even_ref
  7.9 0.0 collective-permute-done.3.z_odd_ref
  7.9 0.0 collective-permute-done.inside_ref
  7.9 0.3 collective-permute-done.1.across_ref
  8.2 0.4 first.1
  8.6 21.3 %all_to_all.16 = f32[320,1,128]{2,1,0:T(1,128)S(1)} all-to-all(f32[320,1,128]{2,1,0:T(1,128)S(1)} %bitcast.9), channel_id=1, replica_groups=mesh['zg'=4,'gy'=64] {'gy'}, dimensions={0} | all-to-all | bytes 327680 | tf_op jit(solution)/shard_map/all_to_all | solution.py:444
  29.9 0.1 column.1
  30.0 14.9 %all_to_all.17 = f32[64,2,128]{2,1,0:T(2,128)S(1)} all-to-all(f32[64,2,128]{2,1,0:T(2,128)S(1)} %bitcast.8), channel_id=1, replica_groups=mesh['zg'=4,'gy'=64] {'gy'}, dimensions={0} | all-to-all | bytes 131072 | tf_op jit(solution)/shard_map/all_to_all | solution.py:446
  45.0 0.1 second.1
  45.1 2.6 %collective-permute-start.6 = (f32[5,4,128]{2,1,0:T(4,128)S(1)}, f32[5,4,128]{2,1,0:T(4,128)S(1)}, u32[]{:S(2)}, u32[]{:S(2)}) collective-permute-start(f32[5,4,128]{2,1,0:T(4,128)S(1)} %get-tuple-element.44.e0_ref), channel_id=1, source_target_pairs={{0,192},{64,128},{128,64},{192,0},{1,193},{65,129},{129,65},{193,1... | collective-permute-start | bytes 30728 | tf_op jit(solution)/shard_map/ppermute | solution.py:421
  47.6 0.9 %collective-permute-start.5 = (f32[5,4,128]{2,1,0:T(4,128)S(1)}, f32[5,4,128]{2,1,0:T(4,128)S(1)}, u32[]{:S(2)}, u32[]{:S(2)}) collective-permute-start(f32[5,4,128]{2,1,0:T(4,128)S(1)} %get-tuple-element.44.e0_ref), channel_id=1, source_target_pairs={{0,128},{64,192},{128,0},{192,64},{1,129},{65,193},{129,1},{193,65... | collective-permute-start | bytes 30728 | tf_op jit(solution)/shard_map/ppermute | solution.py:421
  48.5 0.0 collective-permute-start.4
  48.5 0.1 local_z.1.local_ref
  48.6 0.3 collective-permute-done.6.e3_ref
  48.9 2.8 %collective-permute-done.5.e2_ref = f32[5,4,128]{2,1,0:T(4,128)S(1)} collective-permute-done((f32[5,4,128]{2,1,0:T(4,128)S(1)}, f32[5,4,128]{2,1,0:T(4,128)S(1)}, u32[]{:S(2)}, u32[]{:S(2)}) %collective-permute-start.5) | collective-permute-done | bytes 10272 | tf_op jit(solution)/shard_map/ppermute | solution.py:421
  51.6 0.0 collective-permute-done.4.e1_ref
  51.6 0.8 %last.1 = f32[4,64,128]{2,1,0:T(8,128)} custom-call(f32[4,64,128]{2,1,0:T(8,128)S(1)} %local_z.1.local_ref, f32[2,4,64,128]{3,2,1,0:T(8,128)S(1)} %get-tuple-element.37.spikes_ref, f32[3,4,128]{2,1,0:T(4,128)S(1)} %get-tuple-element.43.last_row_ref, f32[5,4,128]{2,1,0:T(4,128)S(1)} %get-tuple-element.44.e0_ref, ...), custom_call_target="tpu_custom_call" | custom-call | flops 2000000 | bytes 2000000 | tf_op jit(solution)/shard_map/last/pallas_call | solution.py:394
Async XLA Ops:
  0.9 7.0 %collective-permute-start = (f32[2,64,128]{2,1,0:T(8,128)S(1)}, f32[2,64,128]{2,1,0:T(8,128)S(1)}, u32[]{:S(2)}, u32[]{:S(2)}) collective-permute-start(f32[2,64,128]{2,1,0:T(8,128)S(1)} %get-tuple-element.31), channel_id=1, source_target_pairs={{0,1},{1,0},{2,3},{3,2},{4,5},{5,4},{6,7},{7,6},{8,9},{9,8},{10,11... | collective-permute-start | bytes 196616 | tf_op jit(solution)/shard_map/ppermute | solution.py:417
  4.3 4.0 %collective-permute-start.1 = (f32[2,64,128]{2,1,0:T(8,128)S(1)}, f32[2,64,128]{2,1,0:T(8,128)S(1)}, u32[]{:S(2)}, u32[]{:S(2)}) collective-permute-start(f32[2,64,128]{2,1,0:T(8,128)S(1)} %get-tuple-element.32), channel_id=1, source_target_pairs={{0,64},{1,2},{2,1},{3,4},{4,3},{5,6},{6,5},{7,8},{8,7},{9,10},{10,... | collective-permute-start | bytes 196616 | tf_op jit(solution)/shard_map/ppermute | solution.py:417
  4.3 3.7 %collective-permute-start.2 = (f32[2,4,128]{2,1,0:T(4,128)S(1)}, f32[2,4,128]{2,1,0:T(4,128)S(1)}, u32[]{:S(2)}, u32[]{:S(2)}) collective-permute-start(f32[2,4,128]{2,1,0:T(4,128)S(1)} %get-tuple-element.33), channel_id=1, source_target_pairs={{0,64},{1,65},{2,66},{3,67},{4,68},{5,69},{6,70},{7,71},{8,72},{9,... | collective-permute-start | bytes 12296 | tf_op jit(solution)/shard_map/ppermute | solution.py:417
  5.4 2.6 %collective-permute-start.3 = (f32[2,4,128]{2,1,0:T(4,128)S(1)}, f32[2,4,128]{2,1,0:T(4,128)S(1)}, u32[]{:S(2)}, u32[]{:S(2)}) collective-permute-start(f32[2,4,128]{2,1,0:T(4,128)S(1)} %get-tuple-element.34), channel_id=1, source_target_pairs={{0,1},{1,0},{2,3},{3,2},{4,5},{5,4},{6,7},{7,6},{8,9},{9,8},{10,11... | collective-permute-start | bytes 12296 | tf_op jit(solution)/shard_map/ppermute | solution.py:417
  45.1 3.8 %collective-permute-start.6 = (f32[5,4,128]{2,1,0:T(4,128)S(1)}, f32[5,4,128]{2,1,0:T(4,128)S(1)}, u32[]{:S(2)}, u32[]{:S(2)}) collective-permute-start(f32[5,4,128]{2,1,0:T(4,128)S(1)} %get-tuple-element.44.e0_ref), channel_id=1, source_target_pairs={{0,192},{64,128},{128,64},{192,0},{1,193},{65,129},{129,65},{193,1... | collective-permute-start | bytes 30728 | tf_op jit(solution)/shard_map/ppermute | solution.py:421
  47.6 4.0 %collective-permute-start.5 = (f32[5,4,128]{2,1,0:T(4,128)S(1)}, f32[5,4,128]{2,1,0:T(4,128)S(1)}, u32[]{:S(2)}, u32[]{:S(2)}) collective-permute-start(f32[5,4,128]{2,1,0:T(4,128)S(1)} %get-tuple-element.44.e0_ref), channel_id=1, source_target_pairs={{0,128},{64,192},{128,0},{192,64},{1,129},{65,193},{129,1},{193,65... | collective-permute-start | bytes 30728 | tf_op jit(solution)/shard_map/ppermute | solution.py:421
  48.5 3.2 %collective-permute-start.4 = (f32[5,4,128]{2,1,0:T(4,128)S(1)}, f32[5,4,128]{2,1,0:T(4,128)S(1)}, u32[]{:S(2)}, u32[]{:S(2)}) collective-permute-start(f32[5,4,128]{2,1,0:T(4,128)S(1)} %get-tuple-element.44.e0_ref), channel_id=1, source_target_pairs={{0,64},{64,0},{128,192},{192,128},{1,65},{65,1},{129,193},{193,129... | collective-permute-start | bytes 30728 | tf_op jit(solution)/shard_map/ppermute | solution.py:421
